TPU v7x, 32 devices: a whole 2x2x4 slice. The times are simulated.
32 devices in a mesh: dom: 16 (over z, y, x), slab: 2 (over core).
Axes of the slice: x: 2, y: 2, z: 4, core: 2. Of those that a mesh axis runs over, the one named last changes fastest.
Arguments:
- positions: float32 [32768, 3], P(('dom', 'slab')), may hold values from 0 to 20
- species: int32 [32768], P(('dom', 'slab')), may hold values from 0 to 9
- send_pick: int32 [512, 64], P(('dom', 'slab')), may hold values from -1 to 1023, as said below
- ghost_pick: int32 [128, 384], P(('dom', 'slab')), may hold values from 0 to 1023
- near_tiles: int32 [512, 4], P(('dom', 'slab')), may hold values from 0 to 39
- embedding: bfloat16 [10, 128], replicated, may hold values from -6 to 6
- radial_weight: bfloat16 [2, 8, 128], replicated, may hold values from -6 to 6
- update_weight: bfloat16 [2, 512, 128], replicated, may hold values from -0.25 to 0.25
- force_weight: bfloat16 [128, 128], replicated, may hold values from -0.5 to 0.5
Outputs:
- features: bfloat16 [32768, 128], P(('dom', 'slab'))
- forces: float32 [3, 32768], P(None, ('dom', 'slab'))
Inputs may be any that keep to these rules, and one draw needn't show every extreme that they name: `send_pick`: for each domain, a block of 16 x 64; each old row appears at most once in its domain's block; live slots of a destination come first; in every domain some destination is full, and for each slab index one destination along dom receives full slots from every source. `ghost_pick`: ghost rows may repeat. `near_tiles`: tiles index the pool of 64-row tiles and may repeat.
All inputs are finite; a program needn't handle non-finite values.
Results may differ from a plain program's by a relative error of at most 0.0062.
Values may be sent and summed in bfloat16 or wider, within the bound.
No kernel may reach another device: no remote copies, remote signals or barrier semaphores. Data moves between devices by JAX's collectives and lax.ppermute only.
A program may use at most 64 MiB of HBM per device.

v0:
```python
import jax
import jax.numpy as jnp
from jax import lax
from jax.sharding import PartitionSpec as P

LAYERS = 2
TILE = 64


cutoff = 6.0
softening = 0.25


def passed_along(array, axis, by):
    count = lax.axis_size(axis)
    return lax.ppermute(array, axis, [(i, (i + by) % count) for i in range(count)])


def tile_geometry(pos_tiles, live_tiles, index, near_row):
    span = jnp.arange(TILE)
    count = near_row.shape[0]
    pos_i = pos_tiles[index]
    pos_j = pos_tiles[near_row].transpose(1, 0, 2).reshape(3, count * TILE)
    live_i = live_tiles[index]
    live_j = live_tiles[near_row].reshape(count * TILE)
    rows_i = index * TILE + span
    rows_j = (near_row[:, None] * TILE + span[None]).reshape(-1)
    offset = pos_j[:, None, :] - pos_i[:, :, None]
    distance = jnp.sqrt(jnp.sum(offset * offset, axis=0) + softening)
    ratio = distance / cutoff
    envelope = jnp.where(ratio < 1.0, (1.0 - ratio * ratio) ** 2, 0.0)
    keep = (
        live_i[:, None] * live_j[None, :] * (rows_i[:, None] != rows_j[None, :]).astype(jnp.float32)
    )
    return (offset, distance, envelope * keep)


def edge_terms(offset, distance, weight, nbasis):
    unit = offset / distance[None]
    along_x, along_y, along_z = (unit[0], unit[1], unit[2])
    harmonic = jnp.stack(
        [
            jnp.ones_like(along_x),
            along_x,
            along_y,
            along_z,
            along_x * along_y,
            along_y * along_z,
            along_z * along_x,
            along_x * along_x - along_y * along_y,
            3.0 * along_z * along_z - 1.0,
        ]
    )
    orders = jnp.arange(1, nbasis + 1).astype(distance.dtype)
    radial = (
        jnp.sin(orders[:, None, None] * (jnp.pi / cutoff) * distance[None])
        / distance[None]
        * weight[None]
    )
    return (harmonic[:, None] * radial[None]).astype(jnp.bfloat16)


def share_atoms(moved, ghost_pick):
    outgoing = moved[ghost_pick]
    first = passed_along(outgoing[0], "dom", 1)
    second = passed_along(outgoing[1], "dom", -1)
    third = passed_along(outgoing[2], "slab", 1)
    fourth = passed_along(outgoing[3], "slab", -1)
    return jnp.concatenate([moved, first, second, third, fourth], axis=0)


def share_rows(hidden, ghost_pick):
    outgoing = hidden[ghost_pick]
    first = passed_along(outgoing[0], "dom", 1)
    second = passed_along(outgoing[1], "dom", -1)
    third = passed_along(outgoing[2], "slab", 1)
    fourth = passed_along(outgoing[3], "slab", -1)
    return jnp.concatenate([hidden, first, second, third, fourth], axis=0)


def lookup(kinds, embedding):
    onehot = jax.nn.one_hot(kinds, embedding.shape[0], dtype=jnp.bfloat16)
    return jnp.dot(onehot, embedding, preferred_element_type=jnp.float32).astype(jnp.bfloat16)


def layer_step(pos_tiles, live_tiles, h_pool, near, radial_w, update_w, atom_rows):
    nbasis = radial_w.shape[0]
    width = h_pool.shape[1]
    h_tiles = h_pool.reshape(-1, TILE, width)
    radial_f = radial_w.astype(jnp.float32)
    scale = 1.0 / TILE**0.5

    def one(index):
        near_row = near[index]
        offset, distance, weight = tile_geometry(pos_tiles, live_tiles, index, near_row)
        edges = edge_terms(offset, distance, weight, nbasis)
        gathered = h_tiles[near_row].reshape(-1, width)
        weighted = (gathered.astype(jnp.float32)[None] * radial_f[:, None, :]).astype(jnp.bfloat16)
        agg = (
            jnp.einsum("lnij,njc->ilc", edges, weighted, preferred_element_type=jnp.float32) * scale
        )
        square = agg * agg
        query = jnp.concatenate(
            [
                agg[:, 0],
                square[:, 0],
                jnp.sum(square[:, 1:4], axis=1),
                jnp.sum(square[:, 4:9], axis=1),
            ],
            axis=1,
        ).astype(jnp.bfloat16)
        update = jnp.dot(query, update_w, preferred_element_type=jnp.float32)
        before = h_tiles[index].astype(jnp.float32)
        return ((before + jax.nn.silu(update)) * live_tiles[index][:, None]).astype(jnp.bfloat16)

    result = lax.map(one, jnp.arange(atom_rows // TILE))
    return result.reshape(atom_rows, width)


def pair_forces(pos_tiles, live_tiles, g_pool, near, atom_rows):
    width = g_pool.shape[1]
    g_tiles = g_pool.reshape(-1, TILE, width)
    scale = 1.0 / width**0.5
    count = near.shape[1]

    def step(total, index):
        near_row = near[index]
        offset, distance, weight = tile_geometry(pos_tiles, live_tiles, index, near_row)
        others = g_tiles[near_row].reshape(-1, width)
        inner = lax.dot_general(
            g_tiles[index], others, (((1,), (1,)), ((), ())), preferred_element_type=jnp.float32
        )
        strength = weight / distance * inner * scale
        pair = strength[None] * offset
        against = -jnp.sum(pair, axis=1).reshape(3, count, TILE).transpose(1, 0, 2)
        total = total.at[near_row].add(against)
        return (total, jnp.sum(pair, axis=2))

    start = jnp.zeros((g_tiles.shape[0], 3, TILE), jnp.float32)
    total, own = lax.scan(step, start, jnp.arange(atom_rows // TILE))
    total = total.transpose(1, 0, 2).reshape(3, -1)
    local = own.transpose(1, 0, 2).reshape(3, atom_rows) + total[:, :atom_rows]
    return (local, total[:, atom_rows:])


def body(
    positions,
    species,
    send_pick,
    ghost_pick,
    near_tiles,
    embedding,
    radial_weight,
    update_weight,
    force_weight,
):
    atom_rows = positions.shape[0]
    ghost_rows = ghost_pick.shape[1]
    state = jnp.concatenate(
        [positions, jnp.ones((atom_rows, 1), jnp.float32), species.astype(jnp.float32)[:, None]],
        axis=1,
    )
    outgoing = state[jnp.maximum(send_pick, 0)] * (send_pick >= 0).astype(jnp.float32)[..., None]
    moved = lax.all_to_all(outgoing, "dom", split_axis=0, concat_axis=0, tiled=True).reshape(
        atom_rows, 5
    )
    pool = share_atoms(moved, ghost_pick)
    pos_tiles = pool[:, :3].reshape(-1, TILE, 3).transpose(0, 2, 1)
    live_tiles = pool[:, 3].reshape(-1, TILE)
    kinds = pool[:, 4].astype(jnp.int32)
    hidden = lookup(kinds[:atom_rows], embedding)
    h_pool = lookup(kinds, embedding)
    for level in range(LAYERS):
        if level > 0:
            h_pool = share_rows(hidden, ghost_pick)
        hidden = layer_step(
            pos_tiles,
            live_tiles,
            h_pool,
            near_tiles,
            radial_weight[level],
            update_weight[level],
            atom_rows,
        )
    projected = jnp.dot(hidden, force_weight, preferred_element_type=jnp.float32).astype(
        jnp.bfloat16
    )
    g_pool = share_rows(projected, ghost_pick)
    local, outer = pair_forces(pos_tiles, live_tiles, g_pool, near_tiles, atom_rows)
    outer = outer.reshape(3, 4, ghost_rows)
    back_first = passed_along(outer[:, 0], "dom", -1)
    back_second = passed_along(outer[:, 1], "dom", 1)
    back_third = passed_along(outer[:, 2], "slab", -1)
    back_fourth = passed_along(outer[:, 3], "slab", 1)
    local = local.at[:, ghost_pick[0]].add(back_first)
    local = local.at[:, ghost_pick[1]].add(back_second)
    local = local.at[:, ghost_pick[2]].add(back_third)
    local = local.at[:, ghost_pick[3]].add(back_fourth)
    return (hidden, local)


def solution(mesh):
    return jax.shard_map(
        body,
        mesh=mesh,
        in_specs=(
            P(("dom", "slab"), None),
            P(("dom", "slab")),
            P(("dom", "slab"), None),
            P(("dom", "slab"), None),
            P(("dom", "slab"), None),
            P(),
            P(),
            P(),
            P(),
        ),
        out_specs=(P(("dom", "slab"), None), P(None, ("dom", "slab"))),
        check_vma=False,
    )
```

profile of v0, /device:TPU:0, one launch (start us, length us, event | category | flops | bytes accessed | tf_op | source)
XLA Modules:
  0.0 529.6 jit_solution(4173685768440876748)
XLA Ops:
  3.9 2.8 gather_fusion.9
  7.7 8.3 %all-to-all-start = ((f32[16,1,320]{2,1,0:T(1,128)}), f32[16,1,320]{2,1,0:T(1,128)S(1)}, u32[]{:S(2)}, u32[]{:S(2)}) async-start(f32[16,1,320]{2,1,0:T(1,128)} %reshape.804), calls=%async_computation | async-start | bytes 49152 | tf_op jit(solution)/shard_map/all_to_all | solution.py:164
  16.2 7.2 %all-to-all-done = f32[16,1,320]{2,1,0:T(1,128)S(1)} async-done(((f32[16,1,320]{2,1,0:T(1,128)}), f32[16,1,320]{2,1,0:T(1,128)S(1)}, u32[]{:S(2)}, u32[]{:S(2)}) %all-to-all-start) | async-done | bytes 20512 | tf_op jit(solution)/shard_map/all_to_all | solution.py:164
  25.1 2.6 gather_fusion.10
  28.5 5.0 collective-permute-start.1
  34.0 3.2 collective-permute-done
  38.6 158.2 %while.36 = (s32[]{:T(128)}, bf16[16,64,128]{2,1,0:T(8,128)(2,1)S(1)}, s32[16]{0:T(128)S(1)}, bf16[40,64,128]{2,1,0:T(8,128)(2,1)S(1)}, s32[16,4]{1,0:T(8,128)S(...) while((s32[]{:T(128)}, ...), condition=%wide.region_4.5_spmd, body=%wide.region_0.4_spmd.sunk | while | flops 314844512 | bytes 5013956 | solution.py:116
  84.6 1.8 divide_multiply_fusion.4
  196.7 3.2 gather_fusion.11
  201.3 4.4 collective-permute-start.5
  206.2 2.1 collective-permute-done.4
  208.4 158.0 %while.37 = (s32[]{:T(128)}, bf16[16,64,128]{2,1,0:T(8,128)(2,1)S(1)}, s32[16]{0:T(128)S(1)}, bf16[40,64,128]{2,1,0:T(8,128)(2,1)S(1)}, s32[16,4]{1,0:T(8,128)S(...) while((s32[]{:T(128)}, ...), condition=%wide.region_9.10_spmd, body=%wide.region_5.9_spmd.sunk | while | flops 314844512 | bytes 5013956 | solution.py:116
  244.5 1.8 divide_multiply_fusion.5
  366.7 3.2 gather_fusion.12
  370.8 5.0 collective-permute-start.9
  376.3 2.0 collective-permute-done.8
  378.4 125.0 %while.38 = (s32[]{:T(128)}, f32[40,3,64]{2,1,0:T(4,128)S(1)}, f32[16,3,64]{2,1,0:T(4,128)S(1)}, s32[16]{0:T(128)S(1)}, s32[16,4]{1,0:T(8,128)S(1)}, /*index=5*/...) while((s32[]{:T(128)}, f32[40,3,64]{2,1,0:T(4,128)S(1)}, ...), condition=%wide.region_15.16_spmd, body=%wide.region_10.15_spmd.sunk | while | flops 4753304 | bytes 553868 | solution.py:140
  504.0 5.9 %collective-permute-start.12 = (f32[3,384]{0,1:T(8,128)S(1)}, f32[3,384]{0,1:T(8,128)}, u32[]{:S(2)}, u32[]{:S(2)}) collective-permute-start(f32[3,384]{0,1:T(8,128)S(1)} %get-tuple-element.464), channel_id=1, source_target_pairs={{0,30},{2,0},{4,2},{6,4},{8,6},{10,8},{12,10},{14,12},{16,14},{18,... | collective-permute-start | bytes 13832 | tf_op jit(solution)/shard_map/ppermute | solution.py:16
  510.8 2.2 collective-permute-done.12
  513.1 3.2 scatter_custom_fusion.1
  516.3 3.3 collective-permute-done.13
  519.5 3.2 scatter_custom_fusion.2
  522.8 3.2 scatter_custom_fusion.3
  526.0 2.8 scatter_custom_fusion.4
  (1492 shorter events, 258.7 us)
Async XLA Ops:
  0.6 365.9 %copy-start = (bf16[128,128]{1,0:T(8,128)(2,1)S(1)}, bf16[128,128]{1,0:T(8,128)(2,1)}, u32[]{:S(2)}) copy-start(bf16[128,128]{1,0:T(8,128)(2,1)} %param.23) | copy-start | bytes 98308
  3.9 12.1 %copy-start.3 = (s32[4,384]{1,0:T(4,128)S(1)}, s32[4,384]{1,0:T(4,128)}, u32[]{:S(2)}) copy-start(s32[4,384]{1,0:T(4,128)} %param.18) | copy-start | bytes 18436
  3.9 12.1 %copy-start.2 = (bf16[2,512,128]{2,1,0:T(8,128)(2,1)S(1)}, bf16[2,512,128]{2,1,0:T(8,128)(2,1)}, u32[]{:S(2)}) copy-start(bf16[2,512,128]{2,1,0:T(8,128)(2,1)} %param.22) | copy-start | bytes 786436
  6.7 9.4 %copy-start.5 = (bf16[2,8,128]{2,1,0:T(8,128)(2,1)S(1)}, bf16[2,8,128]{2,1,0:T(8,128)(2,1)}, u32[]{:S(2)}) copy-start(bf16[2,8,128]{2,1,0:T(8,128)(2,1)} %param.21) | copy-start | bytes 12292
  6.7 9.4 %copy-start.6 = (s32[16,4]{0,1:T(4,128)S(1)}, s32[16,4]{0,1:T(4,128)}, u32[]{:S(2)}) copy-start(s32[16,4]{0,1:T(4,128)} %param.19) | copy-start | bytes 772
  7.7 15.7 %all-to-all-start = ((f32[16,1,320]{2,1,0:T(1,128)}), f32[16,1,320]{2,1,0:T(1,128)S(1)}, u32[]{:S(2)}, u32[]{:S(2)}) async-start(f32[16,1,320]{2,1,0:T(1,128)} %reshape.804), calls=%async_computation | async-start | bytes 49152 | tf_op jit(solution)/shard_map/all_to_all | solution.py:164
  27.7 10.2 %copy-start.4 = (bf16[10,128]{1,0:T(8,128)(2,1)S(1)}, bf16[10,128]{1,0:T(8,128)(2,1)}, u32[]{:S(2)}) copy-start(bf16[10,128]{1,0:T(8,128)(2,1)} %param.20) | copy-start | bytes 7684
  27.8 9.4 %collective-permute-start = (f32[384,5]{1,0:T(8,128)S(1)}, f32[384,5]{1,0:T(8,128)S(1)}, u32[]{:S(2)}, u32[]{:S(2)}) collective-permute-start(f32[384,5]{1,0:T(8,128)S(1)} %get-tuple-element.468), channel_id=1, source_target_pairs={{0,2},{2,4},{4,6},{6,8},{8,10},{10,12},{12,14},{14,16},{16,18},{18... | collective-permute-start | bytes 23048 | tf_op jit(solution)/shard_map/ppermute | solution.py:16
  28.5 8.8 %collective-permute-start.1 = (f32[384,5]{1,0:T(8,128)S(1)}, f32[384,5]{1,0:T(8,128)S(1)}, u32[]{:S(2)}, u32[]{:S(2)}) collective-permute-start(f32[384,5]{1,0:T(8,128)S(1)} %get-tuple-element.467), channel_id=1, source_target_pairs={{0,30},{2,0},{4,2},{6,4},{8,6},{10,8},{12,10},{14,12},{16,14},{18,... | collective-permute-start | bytes 23048 | tf_op jit(solution)/shard_map/ppermute | solution.py:16
  33.5 3.9 collective-permute-start.2
  33.5 4.1 collective-permute-start.3
  200.0 8.3 %collective-permute-start.4 = (bf16[384,128]{1,0:T(8,128)(2,1)S(1)}, bf16[384,128]{1,0:T(8,128)(2,1)S(1)}, u32[]{:S(2)}, u32[]{:S(2)}) collective-permute-start(bf16[384,128]{1,0:T(8,128)(2,1)S(1)} %get-tuple-element.476), channel_id=1, source_target_pairs={{0,2},{2,4},{4,6},{6,8},{8,10},{10,12},{12,14},{14,16},{16,18},{18... | collective-permute-start | bytes 294920 | tf_op jit(solution)/shard_map/ppermute | solution.py:16
  201.3 7.0 %collective-permute-start.5 = (bf16[384,128]{1,0:T(8,128)(2,1)S(1)}, bf16[384,128]{1,0:T(8,128)(2,1)S(1)}, u32[]{:S(2)}, u32[]{:S(2)}) collective-permute-start(bf16[384,128]{1,0:T(8,128)(2,1)S(1)} %get-tuple-element.475), channel_id=1, source_target_pairs={{0,30},{2,0},{4,2},{6,4},{8,6},{10,8},{12,10},{14,12},{16,14},{18,... | collective-permute-start | bytes 294920 | tf_op jit(solution)/shard_map/ppermute | solution.py:16
  205.7 2.6 collective-permute-start.6
  205.7 2.7 collective-permute-start.7
  366.5 3.5 copy-start.1
  370.0 8.3 %collective-permute-start.8 = (bf16[384,128]{1,0:T(8,128)(2,1)S(1)}, bf16[384,128]{1,0:T(8,128)(2,1)S(1)}, u32[]{:S(2)}, u32[]{:S(2)}) collective-permute-start(bf16[384,128]{1,0:T(8,128)(2,1)S(1)} %get-tuple-element.472), channel_id=1, source_target_pairs={{0,2},{2,4},{4,6},{6,8},{8,10},{10,12},{12,14},{14,16},{16,18},{18... | collective-permute-start | bytes 294920 | tf_op jit(solution)/shard_map/ppermute | solution.py:16
  370.8 7.5 %collective-permute-start.9 = (bf16[384,128]{1,0:T(8,128)(2,1)S(1)}, bf16[384,128]{1,0:T(8,128)(2,1)S(1)}, u32[]{:S(2)}, u32[]{:S(2)}) collective-permute-start(bf16[384,128]{1,0:T(8,128)(2,1)S(1)} %get-tuple-element.471), channel_id=1, source_target_pairs={{0,30},{2,0},{4,2},{6,4},{8,6},{10,8},{12,10},{14,12},{16,14},{18,... | collective-permute-start | bytes 294920 | tf_op jit(solution)/shard_map/ppermute | solution.py:16
  375.7 2.6 collective-permute-start.10
  375.7 2.6 collective-permute-start.11
  504.0 9.1 %collective-permute-start.12 = (f32[3,384]{0,1:T(8,128)S(1)}, f32[3,384]{0,1:T(8,128)}, u32[]{:S(2)}, u32[]{:S(2)}) collective-permute-start(f32[3,384]{0,1:T(8,128)S(1)} %get-tuple-element.464), channel_id=1, source_target_pairs={{0,30},{2,0},{4,2},{6,4},{8,6},{10,8},{12,10},{14,12},{16,14},{18,... | collective-permute-start | bytes 13832 | tf_op jit(solution)/shard_map/ppermute | solution.py:16
  510.1 9.4 %collective-permute-start.13 = (f32[3,384]{0,1:T(8,128)S(1)}, f32[3,384]{0,1:T(8,128)}, u32[]{:S(2)}, u32[]{:S(2)}) collective-permute-start(f32[3,384]{0,1:T(8,128)S(1)} %get-tuple-element.463), channel_id=1, source_target_pairs={{0,2},{2,4},{4,6},{6,8},{8,10},{10,12},{12,14},{14,16},{16,18},{18... | collective-permute-start | bytes 13832 | tf_op jit(solution)/shard_map/ppermute | solution.py:16
  510.2 12.6 %collective-permute-start.14 = (f32[3,384]{0,1:T(8,128)S(1)}, f32[3,384]{0,1:T(8,128)}, u32[]{:S(2)}, u32[]{:S(2)}) collective-permute-start(f32[3,384]{0,1:T(8,128)S(1)} %get-tuple-element.462), channel_id=1, source_target_pairs={{0,1},{1,0},{2,3},{3,2},{4,5},{5,4},{6,7},{7,6},{8,9},{9,8},{10,11... | collective-permute-start | bytes 13832 | tf_op jit(solution)/shard_map/ppermute | solution.py:16
  510.3 15.7 %collective-permute-start.15 = (f32[3,384]{0,1:T(8,128)S(1)}, f32[3,384]{0,1:T(8,128)S(1)}, u32[]{:S(2)}, u32[]{:S(2)}) collective-permute-start(f32[3,384]{0,1:T(8,128)S(1)} %get-tuple-element.461), channel_id=1, source_target_pairs={{0,1},{1,0},{2,3},{3,2},{4,5},{5,4},{6,7},{7,6},{8,9},{9,8},{10,11... | collective-permute-start | bytes 13832 | tf_op jit(solution)/shard_map/ppermute | solution.py:16
where the time goes:
time: 533 us; the launch traced here: 530 us
  loops' own time  193 us (36%)
  local copies, waits for them, and re-layouts  142 us (27%)
  other arithmetic  105 us (20%)
  matrix products  34.9 us (7%)
  starting transfers between devices  33.4 us (6%)
  waiting for transfers between devices  20 us (4%)
    another operation x2, loops' own time, layer_step(): result = lax.map(one, jnp.arange(atom_rows // TILE))  130 us
    another operation x1, loops' own time, pair_forces(): total, own = lax.scan(step, start, jnp.arange(atom_rows // TILE))  63.6 us
    mul x32, other arithmetic, edge_terms(): jnp.sin(orders[:, None, None] * (jnp.pi / cutoff) * distance[None])  57.2 us
    dynamic_slice x48, local copies, waits for them, and re-layouts, layer_step(): result = lax.map(one, jnp.arange(atom_rows // TILE))  28.2 us
    gather x48, local copies, waits for them, and re-layouts, tile_geometry(): pos_j = pos_tiles[near_row].transpose(1, 0, 2).reshape(3, count * TILE)  27.4 us
    gather x48, local copies, waits for them, and re-layouts, tile_geometry(): live_j = live_tiles[near_row].reshape(count * TILE)  26.9 us
    dot_general x32, matrix products, one(): jnp.einsum('lnij,njc->ilc', edges, weighted, preferred_element_type=jnp.f...  25.4 us
    ppermute x16, starting transfers between devices, passed_along(): lax.ppermute(array, axis, [(i, (i + by) % count) for i in range(count)])  25.1 us
  transfers between devices with their start and end apart: 17, of which 6 were waited for; matrix products, arithmetic and copies ran while one was open for 2% of the time, Pallas kernels for 0%

commit v1 on v0

v1 whole, which is shorter than its diff:
```python
import functools

import jax
import jax.numpy as jnp
from jax import lax
from jax.experimental import pallas as pl
from jax.experimental.pallas import tpu as pltpu
from jax.sharding import PartitionSpec as P

LAYERS = 2
TILE = 64
LANES = 128
FACES = 4
NHARM = 9
AWAY = 1000.0
CUTOFF = 6.0
SOFTENING = 0.25
F32 = jnp.float32
BF16 = jnp.bfloat16

COS_TERMS = (1.0, -4.934802200544679, 4.058712126416768, -1.3352627688545893, 0.2353306303588935, -0.02580689139001406)
SIN_TERMS = (3.141592653589793, -5.16771278004997, 2.550164039877345, -0.5992645293207921, 0.08214588661112823, -0.00737043094571435)

VMEM = pl.BlockSpec(memory_space=pltpu.VMEM)
SMEM = pl.BlockSpec(memory_space=pltpu.SMEM)


def params():
    return pltpu.CompilerParams(vmem_limit_bytes=40 * 1024 * 1024)


def pieces(value):
    top = value.astype(BF16)
    rest = value - top.astype(F32)
    middle = rest.astype(BF16)
    low = (rest - middle.astype(F32)).astype(BF16)
    return top, middle, low


def series(terms, square):
    total = jnp.full_like(square, terms[-1])
    for term in reversed(terms[:-1]):
        total = total * square + term
    return total


def iota(shape, dim):
    return lax.broadcasted_iota(jnp.int32, shape, dim)


def send_kernel(n_dom, n_slab, pos_ref, kind_ref, pick_ref, ghost_ref, out_ref, picked_ref):
    rows = pos_ref.shape[1]
    cap = pick_ref.shape[1]
    ghost_rows = ghost_ref.shape[1]
    blocks = rows // LANES
    state = jnp.concatenate([pos_ref[...], kind_ref[...].astype(F32) + 1.0], axis=0)
    top, middle, low = (part.astype(F32) for part in pieces(state))
    table = jnp.concatenate([top, middle, low, jnp.zeros_like(low)], axis=0).astype(BF16)
    table = jnp.concatenate([table[:, m * LANES : (m + 1) * LANES] for m in range(blocks)], axis=0)
    shift = LANES.bit_length() - 1
    for dest in range(n_dom):
        pick = pick_ref[dest : dest + 1, :]
        onehot = (iota((LANES, cap), 0) == (pick & (LANES - 1))).astype(F32).astype(BF16)
        found = jnp.dot(table, onehot, preferred_element_type=F32)
        high = pick >> shift
        total = jnp.zeros((16, cap), F32)
        for m in range(blocks):
            total = total + jnp.where(high == m, found[m * 16 : (m + 1) * 16], 0.0)
        total = total[:8] + total[8:]
        picked_ref[dest] = total + pltpu.roll(total, 4, 0)
    upper = iota((8, cap), 0) < 4
    for dest in range(n_dom):
        left = jnp.where(upper, picked_ref[dest], picked_ref[(dest + 1) % n_dom])
        right = picked_ref[(dest - 1) % n_dom]
        if cap < TILE:
            gap = jnp.zeros((8, TILE - cap), F32)
            block = jnp.concatenate([left, gap, right, gap], axis=1)
        else:
            block = jnp.concatenate([left, right], axis=1)
        for slab in range(n_slab):
            out_ref[dest * n_slab + slab, 0:8, :] = block
    me_dom, me_slab = lax.axis_index("dom"), lax.axis_index("slab")
    ghosts = ghost_ref[...].astype(F32)
    targets = (
        lax.rem(me_dom + 1, n_dom) * n_slab + me_slab,
        lax.rem(me_dom + n_dom - 1, n_dom) * n_slab + me_slab,
        me_dom * n_slab + lax.rem(me_slab + 1, n_slab),
        me_dom * n_slab + lax.rem(me_slab + n_slab - 1, n_slab),
    )
    per = ghost_rows // LANES
    for face, target in enumerate(targets):
        start = 8 + (face % 2) * per
        for m in range(per):
            out_ref[target, start + m : start + m + 1, :] = ghosts[face : face + 1, m * LANES : (m + 1) * LANES]


def payload_rows(ghost_rows):
    return -(-(8 + 2 * (ghost_rows // LANES)) // 8) * 8


def send_states(n_dom, n_slab, positions, species, send_pick, ghost_pick):
    cap = send_pick.shape[1]
    depth = payload_rows(ghost_pick.shape[1])
    return pl.pallas_call(
        functools.partial(send_kernel, n_dom, n_slab),
        out_shape=jax.ShapeDtypeStruct((n_dom * n_slab, depth, LANES), F32),
        in_specs=[VMEM] * 4,
        out_specs=VMEM,
        scratch_shapes=[pltpu.VMEM((n_dom, 8, cap), F32)],
        compiler_params=params(),
        name="send_states",
    )(positions.T, species.reshape(1, -1), send_pick, ghost_pick)


def store_tile(doubled, tile, pool_ref):
    live = doubled[3:4] > 0.5
    for word in range(3):
        pool_ref[tile, word] = jnp.broadcast_to(jnp.where(live, doubled[word : word + 1], AWAY), (8, LANES))


def build_pool(n_dom, n_slab, cap, ghost_rows, recv_ref, emb_ref, pool_ref, column_ref, h_ref, kind_ref):
    me_dom, me_slab = lax.axis_index("dom"), lax.axis_index("slab")
    atom_rows = column_ref.shape[0]
    local_tiles = atom_rows // TILE
    before, after = lax.rem(me_slab + n_slab - 1, n_slab), lax.rem(me_slab + 1, n_slab)
    per = TILE // cap
    half = iota((1, LANES), 1) < TILE
    for pair in range(local_tiles // 2):
        kinds = []
        for tile in (2 * pair, 2 * pair + 1):
            parts = [recv_ref[(tile * per + p) * n_slab + me_slab, 0:8, :][:, :cap] for p in range(per)]
            doubled = jnp.concatenate(parts * 2, axis=1)
            store_tile(doubled, tile, pool_ref)
            column = doubled.T[:TILE]
            live = column[:, 3:4] > 0.5
            spot = iota((TILE, 8), 1)
            column_ref[tile * TILE : (tile + 1) * TILE, :] = jnp.where((spot >= 3) | live, column, -AWAY)
            kinds.append(doubled[3:4])
        kind_ref[0:1, pair * LANES : (pair + 1) * LANES] = jnp.where(half, kinds[0], kinds[1])

    def rows_of(slab):
        return jnp.concatenate([recv_ref[e * n_slab + slab, 0:8, :] for e in range(n_dom)], axis=0)

    own = pieces(rows_of(me_slab))
    below = pieces(rows_of(before))
    above = below if n_slab == 2 else pieces(rows_of(after))
    own_at = me_dom * n_slab
    width = ghost_rows // LANES
    sources = (
        (lax.rem(me_dom + n_dom - 1, n_dom) * n_slab + me_slab, 0, own, TILE, 0),
        (lax.rem(me_dom + 1, n_dom) * n_slab + me_slab, 1, own, 0, 4),
        (own_at + before, 0, below, 0, 0),
        (own_at + after, 1, above, 0, 0),
    )
    shift = cap.bit_length() - 1
    for face, (origin, place, tables, lane_start, row_start) in enumerate(sources):
        for m in range(width):
            at = 8 + place * width + m
            pick = recv_ref[origin, at : at + 1, :].astype(jnp.int32)
            onehot = (iota((LANES, LANES), 0) == (pick & (cap - 1)) + lane_start).astype(F32).astype(BF16)
            found = sum(jnp.dot(table, onehot, preferred_element_type=F32) for table in (tables[0], tables[2], tables[1]))
            high = pick >> shift
            total = jnp.zeros((8, LANES), F32)
            for e in range(n_dom):
                total = total + jnp.where(high == e, found[e * 8 : (e + 1) * 8], 0.0)
            if row_start:
                total = pltpu.roll(total, 4, 0)
            swapped = pltpu.roll(total, TILE, 1)
            tile = local_tiles + (face * ghost_rows) // TILE + 2 * m
            store_tile(jnp.where(half, total, swapped), tile, pool_ref)
            store_tile(jnp.where(half, swapped, total), tile + 1, pool_ref)
            spot = tile * TILE
            kind_ref[0:1, spot : spot + LANES] = total[3:4]
    nspecies, width = emb_ref.shape
    table = jnp.concatenate([emb_ref[...].astype(F32), jnp.zeros((16 - nspecies, width), F32)], axis=0).astype(BF16)
    step = 512
    for start in range(0, h_ref.shape[0], step):
        kinds = kind_ref[0:1, start : start + step].astype(jnp.int32)
        onehot = (iota((16, step), 0) == kinds - 1).astype(F32).astype(BF16)
        h_ref[start : start + step, :] = lax.dot_general(onehot, table, (((0,), (0,)), ((), ())), preferred_element_type=F32).astype(BF16)


def half_rows(near_ref, pool_ref, tile, side):
    first, second = near_ref[2 * side, tile], near_ref[2 * side + 1, tile]
    lane = iota((8, LANES), 1)
    left = lane < TILE
    xyz = [jnp.where(left, pool_ref[first, w], pool_ref[second, w]) for w in range(3)]
    rows = jnp.where(left, first * TILE, second * TILE) + (lane & (TILE - 1))
    return first, second, xyz, rows


def tall(value, count):
    return jnp.concatenate([value] * count, axis=0) if count > 1 else value


def geometry(column_ref, start, count, xyz, rows):
    column = column_ref[pl.ds(start, count), :]
    offset = [tall(xyz[w], count // 8) - column[:, w : w + 1] for w in range(3)]
    square = offset[0] * offset[0] + offset[1] * offset[1] + offset[2] * offset[2] + SOFTENING
    inverse = lax.rsqrt(square)
    ratio = jnp.minimum(square * inverse * (1.0 / CUTOFF), 1.0)
    same = tall(rows, count // 8) == iota((count, LANES), 0) + start
    ratio = jnp.where(same, 1.0, ratio)
    fade = 1.0 - ratio * ratio
    return offset, inverse, ratio, fade * fade


def edges_of(column_ref, start, count, xyz, rows):
    offset, inverse, ratio, envelope = geometry(column_ref, start, count, xyz, rows)
    x, y, z = (part * inverse for part in offset)
    harmonic = [x, y, z, x * y, y * z, z * x, (x - y) * (x + y), 3.0 * (z * z) - 1.0]
    shifted = ratio - 0.5
    square = shifted * shifted
    sine = series(COS_TERMS, square)
    cosine = -shifted * series(SIN_TERMS, square)
    twice = cosine + cosine
    radial = [sine * (envelope * inverse)]
    radial.append(twice * radial[0])
    while len(radial) < 8:
        radial.append(twice * radial[-1] - radial[-2])
    return [part.astype(BF16) for part in harmonic], [part.astype(BF16) for part in radial]


def make_edges(near_ref, pool_ref, column_ref, h_ref, radial_ref, tile, edge_ref, weight_ref):
    nbasis = radial_ref.shape[0]
    near = pool_ref.shape[0] * 0 + 4
    span = near * TILE
    chunk = 16
    for side in range(2):
        first, second, xyz, rows = half_rows(near_ref, pool_ref, tile, side)
        for place, other in enumerate((first, second)):
            h = h_ref[pl.ds(pl.multiple_of(other * TILE, TILE), TILE), :]
            for n in range(nbasis):
                spot = n * span + side * LANES + place * TILE
                weight_ref[spot : spot + TILE, :] = h * radial_ref[n : n + 1, :]
        for part in range(TILE // chunk):
            start = pl.multiple_of(tile * TILE + part * chunk, chunk)
            harmonic, radial = edges_of(column_ref, start, chunk, xyz, rows)
            for n in range(nbasis):
                spot = n * span + side * LANES
                edge_ref[part * chunk : (part + 1) * chunk, spot : spot + LANES] = radial[n]
                for k in range(1, NHARM):
                    row = k * TILE + part * chunk
                    edge_ref[row : row + chunk, spot : spot + LANES] = harmonic[k - 1] * radial[n]


def contract(edge_ref, weight_ref, tile, query_ref):
    channels = weight_ref.shape[1]
    agg = jnp.dot(edge_ref[...], weight_ref[...], preferred_element_type=F32) * (1.0 / TILE**0.5)
    part = [agg[k * TILE : (k + 1) * TILE] for k in range(NHARM)]
    square = [one * one for one in part]
    query = [part[0], square[0], square[1] + square[2] + square[3], square[4] + square[5] + square[6] + square[7] + square[8]]
    start = pl.multiple_of(tile * TILE, TILE)
    for spot, one in enumerate(query):
        query_ref[pl.ds(start, TILE), spot * channels : (spot + 1) * channels] = one.astype(BF16)


def run_layer(near_ref, pool_ref, column_ref, h_ref, radial_ref, update_ref, out_ref, edges, weights, query_ref):
    tiles = near_ref.shape[1]

    def make(tile, slot):
        make_edges(near_ref, pool_ref, column_ref, h_ref, radial_ref, tile, edges[slot], weights[slot])

    make(0, 0)

    def step(index, carry):
        tile = 2 * index
        make(tile + 1, 1)
        contract(edges[0], weights[0], tile, query_ref)
        make(jnp.minimum(tile + 2, tiles - 1), 0)
        contract(edges[1], weights[1], tile + 1, query_ref)
        return carry

    lax.fori_loop(0, tiles // 2, step, 0)
    block = 256
    for start in range(0, out_ref.shape[0], block):
        update = jnp.dot(query_ref[start : start + block, :], update_ref[...], preferred_element_type=F32)
        live = (column_ref[start : start + block, 3:4] > 0.5).astype(F32)
        fresh = h_ref[start : start + block, :].astype(F32) + update * (1.0 / (1.0 + jnp.exp(-update)))
        out_ref[start : start + block, :] = (fresh * live).astype(BF16)


def gather_rows(pick_ref, values, outs):
    rows = values.shape[0]
    ghost_rows = pick_ref.shape[1]
    picks = pick_ref[...].astype(F32)
    picks = jnp.concatenate([picks, jnp.zeros_like(picks)], axis=0)
    spots = [(ref, start) for ref in outs for start in range(0, ref.shape[0], ghost_rows)]
    for m in range(ghost_rows // LANES):
        columns = picks[:, m * LANES : (m + 1) * LANES].T.astype(jnp.int32)
        for face, (ref, start) in enumerate(spots):
            onehot = (columns[:, face : face + 1] == iota((LANES, rows), 1)).astype(F32).astype(BF16)
            found = jnp.dot(onehot, values, preferred_element_type=F32)
            ref[start + m * LANES : start + (m + 1) * LANES, :] = found.astype(BF16)


def first_kernel(n_dom, n_slab, cap, n_out, near_ref, recv_ref, emb_ref, radial_ref, update_ref, pick_ref, *rest):
    pool_ref, column_ref, out_ref = rest[:3]
    outs = rest[3 : 3 + n_out]
    edge_a, edge_b, weight_a, weight_b, query_ref, h_ref, kind_ref = rest[3 + n_out :]
    build_pool(n_dom, n_slab, cap, pick_ref.shape[1], recv_ref, emb_ref, pool_ref, column_ref, h_ref, kind_ref)
    run_layer(near_ref, pool_ref, column_ref, h_ref, radial_ref.at[0], update_ref.at[0], out_ref, (edge_a, edge_b), (weight_a, weight_b), query_ref)
    gather_rows(pick_ref, out_ref[...], outs)


def second_kernel(n_in, level, near_ref, pool_ref, column_ref, h_in_ref, *rest):
    ghosts = rest[:n_in]
    radial_ref, update_ref, force_ref, pick_ref, out_ref, g_ref = rest[n_in : n_in + 6]
    outs = rest[n_in + 6 : 2 * n_in + 6]
    edge_a, edge_b, weight_a, weight_b, query_ref, h_ref = rest[2 * n_in + 6 :]
    start = 0
    for ref in (h_in_ref,) + tuple(ghosts):
        h_ref[start : start + ref.shape[0], :] = ref[...]
        start += ref.shape[0]
    run_layer(near_ref, pool_ref, column_ref, h_ref, radial_ref.at[level], update_ref.at[level], out_ref, (edge_a, edge_b), (weight_a, weight_b), query_ref)
    projected = jnp.dot(out_ref[...], force_ref[...], preferred_element_type=F32).astype(BF16)
    g_ref[...] = projected
    gather_rows(pick_ref, projected, outs)


def layer_scratch(nbasis, near, channels, atom_rows, pool_rows):
    span = near * TILE
    return [
        pltpu.VMEM((NHARM * TILE, nbasis * span), BF16),
        pltpu.VMEM((NHARM * TILE, nbasis * span), BF16),
        pltpu.VMEM((nbasis * span, channels), BF16),
        pltpu.VMEM((nbasis * span, channels), BF16),
        pltpu.VMEM((atom_rows, 4 * channels), BF16),
        pltpu.VMEM((pool_rows, channels), BF16),
    ]


def force_kernel(n_in, near_ref, pool_ref, column_ref, g_in_ref, *rest):
    ghosts = rest[:n_in]
    local_ref = rest[n_in]
    outs = rest[n_in + 1 : 2 * n_in + 1]
    g_ref, total_ref, own_ref = rest[2 * n_in + 1 :]
    tiles = near_ref.shape[1]
    atom_rows, channels = g_in_ref.shape
    start = 0
    for ref in (g_in_ref,) + tuple(ghosts):
        g_ref[start : start + ref.shape[0], :] = ref[...]
        start += ref.shape[0]
    total_ref[...] = jnp.zeros_like(total_ref)
    scale = 1.0 / channels**0.5
    left = iota((8, LANES), 1) < TILE

    def step(tile, carry):
        start = pl.multiple_of(tile * TILE, TILE)
        mine = g_ref[pl.ds(start, TILE), :]
        own = [None] * 3
        for side in range(2):
            first, second, xyz, rows = half_rows(near_ref, pool_ref, tile, side)
            others = jnp.concatenate([g_ref[pl.ds(pl.multiple_of(one * TILE, TILE), TILE), :] for one in (first, second)], axis=0)
            inner = lax.dot_general(mine, others, (((1,), (1,)), ((), ())), preferred_element_type=F32)
            offset, inverse, _, envelope = geometry(column_ref, start, TILE, xyz, rows)
            strength = envelope * inverse * (inner * scale)
            for w in range(3):
                pair = strength * offset[w]
                own[w] = pair if own[w] is None else own[w] + pair
                against = sum(pair[8 * v : 8 * v + 8] for v in range(TILE // 8))
                total_ref[first, w] -= jnp.where(left, against, 0.0)
                total_ref[second, w] -= jnp.where(left, 0.0, against)
        for w in range(3):
            own_ref[w, pl.ds(start, TILE), :] = own[w]
        return carry

    lax.fori_loop(0, tiles, step, 0)
    local = jnp.zeros((8, atom_rows), F32)
    for w in range(3):
        ones = (iota((8, LANES), 0) == w).astype(F32).astype(BF16)
        for part in pieces(own_ref[w]):
            local = local + lax.dot_general(ones, part, (((1,), (1,)), ((), ())), preferred_element_type=F32)
    half = iota((1, LANES), 1) < TILE
    sums = []
    for w in range(3):
        folded = jnp.sum(total_ref[:, w], axis=1)
        sums.append(folded + pltpu.roll(folded, TILE, 1))
    local_ref[...] = local
    spots = [(ref, at) for ref in outs for at in range(0, ref.shape[1], LANES)]
    for pair in range(total_ref.shape[0] // 2):
        for w in range(3):
            row = jnp.where(half, sums[w][2 * pair : 2 * pair + 1], sums[w][2 * pair + 1 : 2 * pair + 2])
            if pair < atom_rows // LANES:
                local_ref[w : w + 1, pair * LANES : (pair + 1) * LANES] += row
            else:
                ref, at = spots[pair - atom_rows // LANES]
                ref[w : w + 1, at : at + LANES] = row


def add_kernel(local_ref, pick_ref, *rest):
    backs, out_ref = rest[:-1], rest[-1]
    atom_rows = local_ref.shape[1]
    ghost_rows = pick_ref.shape[1]
    blocks = atom_rows // LANES
    spots = [(ref, at) for ref in backs for at in range(0, ref.shape[1], ghost_rows)]
    shift = LANES.bit_length() - 1
    total = jnp.zeros((blocks * 8, LANES), F32)
    for face, (ref, at) in enumerate(spots):
        pick = pick_ref[face : face + 1, :]
        back = jnp.where(iota((8, ghost_rows), 0) < 3, ref[:, at : at + ghost_rows], 0.0)
        high = pick >> shift
        spread = jnp.concatenate([jnp.where(high == m, back, 0.0) for m in range(blocks)], axis=0)
        onehot = (iota((LANES, ghost_rows), 0) == (pick & (LANES - 1))).astype(F32).astype(BF16)
        for part in pieces(spread):
            total = total + lax.dot_general(part, onehot, (((1,), (1,)), ((), ())), preferred_element_type=F32)
    for m in range(blocks):
        spot = slice(m * LANES, (m + 1) * LANES)
        out_ref[:, spot] = local_ref[0:3, spot] + total[m * 8 : m * 8 + 3]


def passed_along(array, axis, by):
    count = lax.axis_size(axis)
    return lax.ppermute(array, axis, [(i, (i + by) % count) for i in range(count)])


def exchange(arrays, by):
    moved = [passed_along(arrays[0], "dom", by), passed_along(arrays[1], "dom", -by)]
    for one, way in zip(arrays[2:], (by, -by)):
        moved.append(passed_along(one, "slab", way))
    return moved


def body(n_dom, n_slab, positions, species, send_pick, ghost_pick, near_tiles, embedding, radial_weight, update_weight, force_weight):
    atom_rows = positions.shape[0]
    cap = send_pick.shape[1]
    ghost_rows = ghost_pick.shape[1]
    tiles, near = near_tiles.shape
    channels = embedding.shape[1]
    nbasis = radial_weight.shape[1]
    pool_rows = atom_rows + FACES * ghost_rows
    near_t = near_tiles.T
    face_rows = [ghost_rows, ghost_rows] + ([2 * ghost_rows] if n_slab == 2 else [ghost_rows, ghost_rows])
    n_out = len(face_rows)
    face_out = [jax.ShapeDtypeStruct((rows, channels), BF16) for rows in face_rows]
    scratch = layer_scratch(nbasis, near, channels, atom_rows, pool_rows)

    sent = send_states(n_dom, n_slab, positions, species, send_pick, ghost_pick)
    got = lax.all_to_all(sent, ("dom", "slab"), split_axis=0, concat_axis=0, tiled=True)

    pool, column, hidden, *faces = pl.pallas_call(
        functools.partial(first_kernel, n_dom, n_slab, cap, n_out),
        out_shape=[
            jax.ShapeDtypeStruct((pool_rows // TILE, 3, 8, LANES), F32),
            jax.ShapeDtypeStruct((atom_rows, 8), F32),
            jax.ShapeDtypeStruct((atom_rows, channels), BF16),
        ]
        + face_out,
        in_specs=[SMEM] + [VMEM] * 5,
        out_specs=[VMEM] * (3 + n_out),
        scratch_shapes=scratch + [pltpu.VMEM((8, pool_rows), F32)],
        compiler_params=params(),
        name="first_layer",
    )(near_t, got, embedding, radial_weight, update_weight, ghost_pick)

    faces = exchange(faces, 1)
    features, mine, *faces = pl.pallas_call(
        functools.partial(second_kernel, n_out, 1),
        out_shape=[jax.ShapeDtypeStruct((atom_rows, channels), BF16)] * 2 + face_out,
        in_specs=[SMEM] + [VMEM] * (7 + n_out),
        out_specs=[VMEM] * (2 + n_out),
        scratch_shapes=scratch,
        compiler_params=params(),
        name="second_layer",
    )(near_t, pool, column, hidden, *faces, radial_weight, update_weight, force_weight, ghost_pick)

    faces = exchange(faces, 1)
    local, *backs = pl.pallas_call(
        functools.partial(force_kernel, n_out),
        out_shape=[jax.ShapeDtypeStruct((8, atom_rows), F32)] + [jax.ShapeDtypeStruct((8, rows), F32) for rows in face_rows],
        in_specs=[SMEM] + [VMEM] * (3 + n_out),
        out_specs=[VMEM] * (1 + n_out),
        scratch_shapes=[
            pltpu.VMEM((pool_rows, channels), BF16),
            pltpu.VMEM((pool_rows // TILE, 3, 8, LANES), F32),
            pltpu.VMEM((3, atom_rows, LANES), F32),
        ],
        compiler_params=params(),
        name="pair_forces",
    )(near_t, pool, column, mine, *faces)

    backs = exchange(backs, -1)
    forces = pl.pallas_call(
        add_kernel,
        out_shape=jax.ShapeDtypeStruct((3, atom_rows), F32),
        in_specs=[VMEM] * (2 + n_out),
        out_specs=VMEM,
        compiler_params=params(),
        name="add_ghost_forces",
    )(local, ghost_pick, *backs)
    return features, forces


def solution(mesh):
    both = ("dom", "slab")
    return jax.shard_map(
        functools.partial(body, mesh.shape["dom"], mesh.shape["slab"]),
        mesh=mesh,
        in_specs=(P(both, None), P(both), P(both, None), P(both, None), P(both, None), P(), P(), P(), P()),
        out_specs=(P(both, None), P(None, both)),
        check_vma=False,
    )
```

time: 533 us -> 100 us (0.19)
  loops' own time: 193 us -> 0 us
  local copies, waits for them, and re-layouts: 142 us -> 2.82 us
  other arithmetic: 105 us -> 0 us
  Pallas kernels: 0 us -> 48 us
  matrix products: 34.9 us -> 0 us
  blocking collectives: 0 us -> 17.7 us
  starting transfers between devices: 33.4 us -> 17 us
  waiting for transfers between devices: 20 us -> 13.5 us
    another operation x3 -> x0, loops' own time: 193 us -> none  [the longest x2 130 us: layer_step(): result = lax.map(one, jnp.arange(atom_rows // TILE))]
    gather x149 -> x0, local copies, waits for them, and re-layouts: 93.4 us -> none  [the longest x48 27.4 us: tile_geometry(): pos_j = pos_tiles[near_row].transpose(1, 0, 2).reshape(3, count * TILE)]
    mul x112 -> x0, other arithmetic: 57.7 us -> none  [the longest x32 57.2 us: edge_terms(): jnp.sin(orders[:, None, None] * (jnp.pi / cutoff) * distance[None])]
    pallas_call x0 -> x5, Pallas kernels: none -> 48 us  [the longest x1 21.2 us: body(): pl.pallas_call(functools.partial(first_kernel, n_dom, n_slab, cap, n_out)...]
    dot_general x82 -> x0, matrix products: 34.9 us -> none  [the longest x32 25.4 us: one(): jnp.einsum('lnij,njc->ilc', edges, weighted, preferred_element_type=jnp.f...]
    dynamic_slice x48 -> x0, local copies, waits for them, and re-layouts: 28.2 us -> none  [layer_step(): result = lax.map(one, jnp.arange(atom_rows // TILE))]
    scatter-add x20 -> x0, other arithmetic: 22.8 us -> none  [the longest x16 10.3 us: step(): total = total.at[near_row].add(against)]
    all_to_all x0 -> x1, blocking collectives: none -> 17.7 us  [body(): lax.all_to_all(sent, ('dom', 'slab'), split_axis=0, concat_axis=0, tiled=...]
  transfers between devices with their start and end apart: 17 -> 9, of which waited for: 6 -> 4; matrix products, arithmetic and copies ran while one was open for 2% -> 0% of each run, Pallas kernels for 0% -> 0%
where the time goes in v1:
time: 100 us; the launch traced here: 99.8 us
  Pallas kernels  48 us (48%)
  blocking collectives  17.7 us (18%)
  starting transfers between devices  17 us (17%)
  waiting for transfers between devices  13.5 us (14%)
  local copies, waits for them, and re-layouts  2.82 us (3%)
    pallas_call x1, Pallas kernels, body(): pl.pallas_call(functools.partial(first_kernel, n_dom, n_slab, cap, n_out)...  21.2 us
    pallas_call x1, Pallas kernels, body(): pl.pallas_call(functools.partial(second_kernel, n_out, 1), out_shape=[jax...  20.3 us
    all_to_all x1, blocking collectives, body(): lax.all_to_all(sent, ('dom', 'slab'), split_axis=0, concat_axis=0, tiled=...  17.7 us
    ppermute x9, starting transfers between devices, passed_along(): lax.ppermute(array, axis, [(i, (i + by) % count) for i in range(count)])  17 us
    ppermute x9, waiting for transfers between devices, passed_along(): lax.ppermute(array, axis, [(i, (i + by) % count) for i in range(count)])  13.5 us
    pallas_call x1, Pallas kernels, body(): pl.pallas_call(functools.partial(force_kernel, n_out), out_shape=[jax.Sha...  4.78 us
    unnamed x20, local copies, waits for them, and re-layouts  2.82 us
  transfers between devices with their start and end apart: 9, of which 4 were waited for; matrix products, arithmetic and copies ran while one was open for 0% of the time, Pallas kernels for 0%

profile of v1, /device:TPU:0, one launch (start us, length us, event | category | flops | bytes accessed | tf_op | source)
XLA Modules:
  0.0 99.8 jit_solution(613834970108749062)
XLA Ops:
  0.6 0.7 copy-done.1
  1.3 0.7 copy-done.6
  2.0 0.7 copy-done.7
  2.7 0.7 copy-done.8
  3.4 0.4 send_states.1
  3.8 0.0 copy-start.4
  3.8 0.0 copy-start.5
  3.9 17.7 %all_to_all.5.recv_ref = f32[32,16,128]{2,1,0:T(8,128)S(1)} all-to-all(f32[32,16,128]{2,1,0:T(8,128)S(1)} %send_states.1), channel_id=1, replica_groups=mesh['dom'=16,'slab'=2] {'dom','slab'}, dimensions={0} | all-to-all | bytes 524288 | tf_op jit(solution)/shard_map/all_to_all | solution.py:439
  21.6 21.2 %first_layer.1 = (f32[40,3,8,128]{3,2,1,0:T(8,128)S(1)}, f32[1024,8]{1,0:T(8,128)S(1)}, bf16[1024,128]{1,0:T(8,128)(2,1)S(1)}, bf16[384,128]{1,0:T(8,128)(2,1)S(...) custom-call(s32[4,16]{1,0:T(4,128)S(1)} %bitcast.3, f32[32,16,128]{2,1,0:T(8,128)S(1)} %all_to_all.5.recv_ref, ...), custom_call_target="tpu_custom_call" | custom-call | tf_op jit(solution)/shard_map/first_layer/pallas_call | solution.py:441
  42.9 0.1 collective-permute-start.2
  42.9 0.8 collective-permute-start
  43.8 4.9 %collective-permute-start.1 = (bf16[384,128]{1,0:T(8,128)(2,1)S(1)}, bf16[384,128]{1,0:T(8,128)(2,1)S(1)}, u32[]{:S(2)}, u32[]{:S(2)}) collective-permute-start(bf16[384,128]{1,0:T(8,128)(2,1)S(1)} %get-tuple-element.21), channel_id=1, source_target_pairs={{0,30},{2,0},{4,2},{6,4},{8,6},{10,8},{12,10},{14,12},{16,14},{18,... | collective-permute-start | bytes 294920 | tf_op jit(solution)/shard_map/ppermute | solution.py:414
  48.6 3.1 %collective-permute-done.rest_0_ = bf16[384,128]{1,0:T(8,128)(2,1)S(1)} collective-permute-done((bf16[384,128]{1,0:T(8,128)(2,1)S(1)}, bf16[384,128]{1,0:T(8,128)(2,1)S(1)}, u32[]{:S(2)}, u32[]{:S(2)}) %collective-permute-start) | collective-permute-done | bytes 98336 | tf_op jit(solution)/shard_map/ppermute | solution.py:414
  51.7 20.3 %second_layer.1 = (bf16[1024,128]{1,0:T(8,128)(2,1)}, bf16[1024,128]{1,0:T(8,128)(2,1)S(1)}, bf16[384,128]{1,0:T(8,128)(2,1)S(1)}, bf16[384,128]{1,0:T(8,128)(2,1)S(1)}, bf16[768,128]{1,0:T(8,128)(2,1)S(1)}) custom-call(s32[4,16]{1,0:T(4,128)S(1)} %bitcast.4, f32[40,3,8,128]{3,2,1,0:T(8,128)S(1)} %get-tuple-element.17.pool_ref, ...), custom_call_target="tpu_custom_call" | custom-call | tf_op jit(solution)/shard_map/second_layer/pallas_call | solution.py:457
  72.1 0.1 collective-permute-start.5
  72.2 0.1 collective-permute-start.3
  72.2 5.6 %collective-permute-start.4 = (bf16[384,128]{1,0:T(8,128)(2,1)S(1)}, bf16[384,128]{1,0:T(8,128)(2,1)S(1)}, u32[]{:S(2)}, u32[]{:S(2)}) collective-permute-start(bf16[384,128]{1,0:T(8,128)(2,1)S(1)} %get-tuple-element.26), channel_id=1, source_target_pairs={{0,30},{2,0},{4,2},{6,4},{8,6},{10,8},{12,10},{14,12},{16,14},{18,... | collective-permute-start | bytes 294920 | tf_op jit(solution)/shard_map/ppermute | solution.py:414
  77.8 3.1 %collective-permute-done.3.rest_0_ = bf16[384,128]{1,0:T(8,128)(2,1)S(1)} collective-permute-done((bf16[384,128]{1,0:T(8,128)(2,1)S(1)}, bf16[384,128]{1,0:T(8,128)(2,1)S(1)}, u32[]{:S(2)}, u32[]{:S(2)}) %collective-permute-start.3) | collective-permute-done | bytes 98336 | tf_op jit(solution)/shard_map/ppermute | solution.py:414
  81.0 4.8 %pair_forces.1 = (f32[8,1024]{1,0:T(8,128)S(1)}, f32[8,384]{1,0:T(8,128)S(1)}, f32[8,384]{1,0:T(8,128)S(1)}, f32[8,768]{1,0:T(8,128)S(1)}) custom-call(s32[4,16]{1,0:T(4,128)S(1)} %bitcast.5, f32[40,3,8,128]{3,2,1,0:T(8,128)S(1)} %get-tuple-element.17.pool_ref, f32[1024,8]{1,0:T(8,128)S(1)} %get-tuple-element.18.column_ref, ...), custom_call_target="tpu_custom_call" | custom-call | tf_op jit(solution)/shard_map/pair_forces/pallas_call | solution.py:468
  85.8 0.1 collective-permute-start.8
  85.8 5.4 %collective-permute-start.6 = (f32[8,384]{1,0:T(8,128)S(1)}, f32[8,384]{1,0:T(8,128)S(1)}, u32[]{:S(2)}, u32[]{:S(2)}) collective-permute-start(f32[8,384]{1,0:T(8,128)S(1)} %get-tuple-element.29), channel_id=1, source_target_pairs={{0,30},{2,0},{4,2},{6,4},{8,6},{10,8},{12,10},{14,12},{16,14},{18,... | collective-permute-start | bytes 36872 | tf_op jit(solution)/shard_map/ppermute | solution.py:414
  91.2 1.4 %collective-permute-done.6.rest_0_ = f32[8,384]{1,0:T(8,128)S(1)} collective-permute-done((f32[8,384]{1,0:T(8,128)S(1)}, f32[8,384]{1,0:T(8,128)S(1)}, u32[]{:S(2)}, u32[]{:S(2)}) %collective-permute-start.6) | collective-permute-done | bytes 12320 | tf_op jit(solution)/shard_map/ppermute | solution.py:414
  92.6 5.9 %collective-permute-done.7.rest_1_ = f32[8,384]{1,0:T(8,128)S(1)} collective-permute-done((f32[8,384]{1,0:T(8,128)S(1)}, f32[8,384]{1,0:T(8,128)S(1)}, u32[]{:S(2)}, u32[]{:S(2)}) %collective-permute-start.7) | collective-permute-done | bytes 12320 | tf_op jit(solution)/shard_map/ppermute | solution.py:414
  98.5 1.3 %add_ghost_forces.1 = f32[3,1024]{1,0:T(4,128)} custom-call(f32[8,1024]{1,0:T(8,128)S(1)} %get-tuple-element.28.local_ref, s32[4,384]{1,0:T(4,128)S(1)} %copy-done.2, f32[8,384]{1,0:T(8,128)S(1)} %collective-permute-done.6.rest_0_, f32[8,384]{1,0:T(8,128)S(1)} %collective-permute-done.7.rest_1_, f32[8,768]{1,0:T(8,128)S(1)} %collective-permute-done.8.rest_2_), custom_call_target="tpu_custom_call" | custom-call | tf_op jit(solution)/shard_map/add_ghost_forces/pallas_call | solution.py:483
  (20 shorter events, 0.1 us)
Async XLA Ops:
  0.6 0.7 copy-start.1
  1.3 0.7 copy-start.6
  2.0 0.7 copy-start.7
  2.7 0.7 copy-start.8
  3.8 17.8 %copy-start = (bf16[2,512,128]{2,1,0:T(8,128)(2,1)S(1)}, bf16[2,512,128]{2,1,0:T(8,128)(2,1)}, u32[]{:S(2)}) copy-start(bf16[2,512,128]{2,1,0:T(8,128)(2,1)} %rest_4_.1) | copy-start | bytes 786436
  3.8 17.8 %copy-start.2 = (s32[4,384]{1,0:T(4,128)S(1)}, s32[4,384]{1,0:T(4,128)}, u32[]{:S(2)}) copy-start(s32[4,384]{1,0:T(4,128)} %pick_ref.5) | copy-start | bytes 18436
  3.8 17.7 %copy-start.4 = (s32[16,4]{0,1:T(4,128)S(1)}, s32[16,4]{0,1:T(4,128)}, u32[]{:S(2)}) copy-start(s32[16,4]{0,1:T(4,128)} %param.13) | copy-start | bytes 772
  3.8 17.7 %copy-start.5 = (bf16[2,8,128]{2,1,0:T(8,128)(2,1)S(1)}, bf16[2,8,128]{2,1,0:T(8,128)(2,1)}, u32[]{:S(2)}) copy-start(bf16[2,8,128]{2,1,0:T(8,128)(2,1)} %rest_3_.1) | copy-start | bytes 12292
  3.9 17.7 %copy-start.9 = (bf16[10,128]{1,0:T(8,128)(2,1)S(1)}, bf16[10,128]{1,0:T(8,128)(2,1)}, u32[]{:S(2)}) copy-start(bf16[10,128]{1,0:T(8,128)(2,1)} %emb_ref.1) | copy-start | bytes 7684
  21.6 30.1 %copy-start.3 = (bf16[128,128]{1,0:T(8,128)(2,1)S(1)}, bf16[128,128]{1,0:T(8,128)(2,1)}, u32[]{:S(2)}) copy-start(bf16[128,128]{1,0:T(8,128)(2,1)} %rest_5_.1) | copy-start | bytes 98308
  42.9 8.9 %collective-permute-start.2 = (bf16[768,128]{1,0:T(8,128)(2,1)S(1)}, bf16[768,128]{1,0:T(8,128)(2,1)S(1)}, u32[]{:S(2)}, u32[]{:S(2)}) collective-permute-start(bf16[768,128]{1,0:T(8,128)(2,1)S(1)} %get-tuple-element.22), channel_id=1, source_target_pairs={{0,1},{1,0},{2,3},{3,2},{4,5},{5,4},{6,7},{7,6},{8,9},{9,8},{10,11... | collective-permute-start | bytes 589832 | tf_op jit(solution)/shard_map/ppermute | solution.py:414
  42.9 8.8 %collective-permute-start = (bf16[384,128]{1,0:T(8,128)(2,1)S(1)}, bf16[384,128]{1,0:T(8,128)(2,1)S(1)}, u32[]{:S(2)}, u32[]{:S(2)}) collective-permute-start(bf16[384,128]{1,0:T(8,128)(2,1)S(1)} %get-tuple-element.20), channel_id=1, source_target_pairs={{0,2},{2,4},{4,6},{6,8},{8,10},{10,12},{12,14},{14,16},{16,18},{18... | collective-permute-start | bytes 294920 | tf_op jit(solution)/shard_map/ppermute | solution.py:414
  43.8 8.0 %collective-permute-start.1 = (bf16[384,128]{1,0:T(8,128)(2,1)S(1)}, bf16[384,128]{1,0:T(8,128)(2,1)S(1)}, u32[]{:S(2)}, u32[]{:S(2)}) collective-permute-start(bf16[384,128]{1,0:T(8,128)(2,1)S(1)} %get-tuple-element.21), channel_id=1, source_target_pairs={{0,30},{2,0},{4,2},{6,4},{8,6},{10,8},{12,10},{14,12},{16,14},{18,... | collective-permute-start | bytes 294920 | tf_op jit(solution)/shard_map/ppermute | solution.py:414
  72.1 8.9 %collective-permute-start.5 = (bf16[768,128]{1,0:T(8,128)(2,1)S(1)}, bf16[768,128]{1,0:T(8,128)(2,1)S(1)}, u32[]{:S(2)}, u32[]{:S(2)}) collective-permute-start(bf16[768,128]{1,0:T(8,128)(2,1)S(1)} %get-tuple-element.27), channel_id=1, source_target_pairs={{0,1},{1,0},{2,3},{3,2},{4,5},{5,4},{6,7},{7,6},{8,9},{9,8},{10,11... | collective-permute-start | bytes 589832 | tf_op jit(solution)/shard_map/ppermute | solution.py:414
  72.2 8.8 %collective-permute-start.3 = (bf16[384,128]{1,0:T(8,128)(2,1)S(1)}, bf16[384,128]{1,0:T(8,128)(2,1)S(1)}, u32[]{:S(2)}, u32[]{:S(2)}) collective-permute-start(bf16[384,128]{1,0:T(8,128)(2,1)S(1)} %get-tuple-element.25), channel_id=1, source_target_pairs={{0,2},{2,4},{4,6},{6,8},{8,10},{10,12},{12,14},{14,16},{16,18},{18... | collective-permute-start | bytes 294920 | tf_op jit(solution)/shard_map/ppermute | solution.py:414
  72.2 8.7 %collective-permute-start.4 = (bf16[384,128]{1,0:T(8,128)(2,1)S(1)}, bf16[384,128]{1,0:T(8,128)(2,1)S(1)}, u32[]{:S(2)}, u32[]{:S(2)}) collective-permute-start(bf16[384,128]{1,0:T(8,128)(2,1)S(1)} %get-tuple-element.26), channel_id=1, source_target_pairs={{0,30},{2,0},{4,2},{6,4},{8,6},{10,8},{12,10},{14,12},{16,14},{18,... | collective-permute-start | bytes 294920 | tf_op jit(solution)/shard_map/ppermute | solution.py:414
  85.8 12.8 %collective-permute-start.8 = (f32[8,768]{1,0:T(8,128)S(1)}, f32[8,768]{1,0:T(8,128)S(1)}, u32[]{:S(2)}, u32[]{:S(2)}) collective-permute-start(f32[8,768]{1,0:T(8,128)S(1)} %get-tuple-element.31), channel_id=1, source_target_pairs={{0,1},{1,0},{2,3},{3,2},{4,5},{5,4},{6,7},{7,6},{8,9},{9,8},{10,11... | collective-permute-start | bytes 73736 | tf_op jit(solution)/shard_map/ppermute | solution.py:414
  85.8 6.8 %collective-permute-start.6 = (f32[8,384]{1,0:T(8,128)S(1)}, f32[8,384]{1,0:T(8,128)S(1)}, u32[]{:S(2)}, u32[]{:S(2)}) collective-permute-start(f32[8,384]{1,0:T(8,128)S(1)} %get-tuple-element.29), channel_id=1, source_target_pairs={{0,30},{2,0},{4,2},{6,4},{8,6},{10,8},{12,10},{14,12},{16,14},{18,... | collective-permute-start | bytes 36872 | tf_op jit(solution)/shard_map/ppermute | solution.py:414
  91.2 7.3 %collective-permute-start.7 = (f32[8,384]{1,0:T(8,128)S(1)}, f32[8,384]{1,0:T(8,128)S(1)}, u32[]{:S(2)}, u32[]{:S(2)}) collective-permute-start(f32[8,384]{1,0:T(8,128)S(1)} %get-tuple-element.30), channel_id=1, source_target_pairs={{0,2},{2,4},{4,6},{6,8},{8,10},{10,12},{12,14},{14,16},{16,18},{18... | collective-permute-start | bytes 36872 | tf_op jit(solution)/shard_map/ppermute | solution.py:414

commit v2 on v1

v2 whole, which is shorter than its diff:
```python
import functools

import jax
import jax.numpy as jnp
from jax import lax
from jax.experimental import pallas as pl
from jax.experimental.pallas import tpu as pltpu
from jax.sharding import PartitionSpec as P

LAYERS = 2
TILE = 64
LANES = 128
FACES = 4
NHARM = 9
AWAY = 1000.0
CUTOFF = 6.0
SOFTENING = 0.25
F32 = jnp.float32
BF16 = jnp.bfloat16

COS_TERMS = (1.0, -4.934802200544679, 4.058712126416768, -1.3352627688545893, 0.2353306303588935, -0.02580689139001406)
SIN_TERMS = (3.141592653589793, -5.16771278004997, 2.550164039877345, -0.5992645293207921, 0.08214588661112823, -0.00737043094571435)

VMEM = pl.BlockSpec(memory_space=pltpu.VMEM)
SMEM = pl.BlockSpec(memory_space=pltpu.SMEM)


def params(mib=40):
    return pltpu.CompilerParams(vmem_limit_bytes=mib * 1024 * 1024)


def pieces(value):
    top = value.astype(BF16)
    rest = value - top.astype(F32)
    middle = rest.astype(BF16)
    low = (rest - middle.astype(F32)).astype(BF16)
    return top, middle, low


def series(terms, square):
    total = jnp.full_like(square, terms[-1])
    for term in reversed(terms[:-1]):
        total = total * square + term
    return total


def iota(shape, dim):
    return lax.broadcasted_iota(jnp.int32, shape, dim)


def send_kernel(n_dom, n_slab, pos_in, kind_in, pick_in, ghost_in, near_in, embedding_in, radial_in, update_in, force_in, out_ref, weights_ref, numbers_ref,
                pos_ref, kind_ref, pick_ref, ghost_ref, near_ref, embedding_ref, radial_ref, picked_ref, sems):
    update_spot, force_spot = weight_spots(radial_in.shape, update_in.shape)
    pairs = [(pos_in, pos_ref), (kind_in, kind_ref), (pick_in, pick_ref), (ghost_in, ghost_ref), (near_in, near_ref), (embedding_in, embedding_ref), (radial_in, radial_ref)]
    pairs += [(update_in.at[m], weights_ref.at[spot : spot + update_in.shape[1]]) for m, spot in enumerate(update_spot)]
    pairs += [(force_in, weights_ref.at[force_spot : force_spot + force_in.shape[0]])]
    copies = []
    for spot, (source, target) in enumerate(pairs):
        copies.append(pltpu.make_async_copy(source, target, sems.at[spot]))
        copies[-1].start()
    for copy in copies:
        copy.wait()
    numbers_ref[...] = jnp.zeros_like(numbers_ref)
    numbers_ref[0:FACES, :] = ghost_ref[...]
    numbers_ref[FACES : FACES + near_ref.shape[0], 0 : near_ref.shape[1]] = near_ref[...]
    blank = jnp.zeros((16, embedding_ref.shape[1]), F32)
    for level in range(radial_ref.shape[0]):
        weights_ref[16 * level : 16 * level + 16, :] = jnp.concatenate([radial_ref[level].astype(F32), blank[radial_ref.shape[1] :]], axis=0).astype(BF16)
    spot = 16 * radial_ref.shape[0]
    weights_ref[spot : spot + 16, :] = jnp.concatenate([embedding_ref[...].astype(F32), blank[embedding_ref.shape[0] :]], axis=0).astype(BF16)
    rows = pos_ref.shape[1]
    cap = pick_ref.shape[1]
    blocks = rows // LANES
    state = jnp.concatenate([pos_ref[...], kind_ref[...].astype(F32) + 1.0], axis=0)
    top, middle, low = (part.astype(F32) for part in pieces(state))
    table = jnp.concatenate([top, middle, low, jnp.zeros_like(low)], axis=0).astype(BF16)
    table = jnp.concatenate([table[:, m * LANES : (m + 1) * LANES] for m in range(blocks)], axis=0)
    shift = LANES.bit_length() - 1
    for dest in range(n_dom):
        pick = pick_ref[dest : dest + 1, :]
        onehot = (iota((LANES, cap), 0) == (pick & (LANES - 1))).astype(F32).astype(BF16)
        found = jnp.dot(table, onehot, preferred_element_type=F32)
        high = pick >> shift
        total = jnp.zeros((16, cap), F32)
        for m in range(blocks):
            total = total + jnp.where(high == m, found[m * 16 : (m + 1) * 16], 0.0)
        total = total[:8] + total[8:]
        picked_ref[dest] = total + pltpu.roll(total, 4, 0)
    packs = []
    bits = rows.bit_length() - 1
    for face in range(FACES):
        picks = ghost_ref[face : face + 1, :]
        third = [picks[:, m * TILE : (m + 1) * TILE] for m in range(picks.shape[1] // TILE)]
        count = len(third) // 2
        lines = [(third[r] + (third[r + count] << bits)).astype(F32) for r in range(count)]
        near = near_ref[...].astype(F32)
        lines.append(jnp.concatenate([near[k : k + 1] for k in range(near.shape[0])], axis=1))
        packs.append(jnp.concatenate(lines, axis=0))
    upper = iota((8, cap), 0) < 4
    for dest in range(n_dom):
        left = jnp.where(upper, picked_ref[dest], picked_ref[(dest + 1) % n_dom])
        right = picked_ref[(dest - 1) % n_dom]
        if cap < TILE:
            gap = jnp.zeros((8, TILE - cap), F32)
            block = jnp.concatenate([left, gap, right, gap], axis=1)
        else:
            block = jnp.concatenate([left, right], axis=1)
        for slab in range(n_slab):
            out_ref[dest * n_slab + slab] = block
    me_dom, me_slab = lax.axis_index("dom"), lax.axis_index("slab")
    targets = (
        lax.rem(me_dom + 1, n_dom) * n_slab + me_slab,
        lax.rem(me_dom + n_dom - 1, n_dom) * n_slab + me_slab,
        me_dom * n_slab + lax.rem(me_slab + 1, n_slab),
        me_dom * n_slab + lax.rem(me_slab + n_slab - 1, n_slab),
    )
    for face, target in enumerate(targets):
        start = 0 if face == 3 else 4
        out_ref[target, start : start + 4, TILE:] = packs[face]


def weight_spots(radial_shape, update_shape):
    first = 16 * radial_shape[0] + 16
    spots = [first + m * update_shape[1] for m in range(update_shape[0])]
    return spots, first + update_shape[0] * update_shape[1]


def send_states(n_dom, n_slab, positions, species, send_pick, ghost_pick, near_tiles, embedding, radial, update, force):
    cap = send_pick.shape[1]
    inputs = (positions.T, species.reshape(1, -1), send_pick, ghost_pick, near_tiles.T, embedding, radial, update, force)
    count = weight_spots(radial.shape, update.shape)[1] + force.shape[0]
    return pl.pallas_call(
        functools.partial(send_kernel, n_dom, n_slab),
        out_shape=[
            jax.ShapeDtypeStruct((n_dom * n_slab, 8, LANES), F32),
            jax.ShapeDtypeStruct((count, force.shape[1]), BF16),
            jax.ShapeDtypeStruct((8, ghost_pick.shape[1]), jnp.int32),
        ],
        in_specs=[pl.BlockSpec(memory_space=pl.ANY)] * len(inputs),
        out_specs=[VMEM] * 3,
        scratch_shapes=[pltpu.VMEM(one.shape, one.dtype) for one in inputs[:7]]
        + [pltpu.VMEM((n_dom, 8, cap), F32), pltpu.SemaphoreType.DMA((8 + update.shape[0],))],
        compiler_params=params(63),
        name="send_states",
    )(*inputs)


def store_tile(doubled, tile, pool_ref):
    live = doubled[3:4] > 0.5
    for word in range(3):
        pool_ref[tile, word] = jnp.broadcast_to(jnp.where(live, doubled[word : word + 1], AWAY), (8, LANES))


def find_rows(tables, lane, group, groups):
    onehot = (iota((LANES, LANES), 0) == lane).astype(F32).astype(BF16)
    found = sum(jnp.dot(table, onehot, preferred_element_type=F32) for table in (tables[0], tables[2], tables[1]))
    total = jnp.zeros((8, LANES), F32)
    for one in range(groups):
        total = total + jnp.where(group == one, found[one * 8 : (one + 1) * 8], 0.0)
    return total


def build_pool(n_dom, n_slab, cap, ghost_rows, recv_ref, emb_ref, pool_ref, column_ref, around_ref, taken_ref, h_ref, kind_ref):
    me_dom, me_slab = lax.axis_index("dom"), lax.axis_index("slab")
    atom_rows = column_ref.shape[0]
    local_tiles = atom_rows // TILE
    before, after = lax.rem(me_slab + n_slab - 1, n_slab), lax.rem(me_slab + 1, n_slab)
    per = TILE // cap
    half = iota((1, LANES), 1) < TILE
    for pair in range(local_tiles // 2):
        kinds = []
        for tile in (2 * pair, 2 * pair + 1):
            parts = [recv_ref[(tile * per + p) * n_slab + me_slab, 0:8, :][:, :cap] for p in range(per)]
            doubled = jnp.concatenate(parts * 2, axis=1)
            store_tile(doubled, tile, pool_ref)
            column = doubled.T[:TILE]
            live = column[:, 3:4] > 0.5
            spot = iota((TILE, 8), 1)
            column_ref[tile * TILE : (tile + 1) * TILE, :] = jnp.where((spot >= 3) | live, column, -AWAY)
            kinds.append(doubled[3:4])
        kind_ref[0:1, pair * LANES : (pair + 1) * LANES] = jnp.where(half, kinds[0], kinds[1])

    def rows_of(slab):
        return jnp.concatenate([recv_ref[e * n_slab + slab, 0:8, :] for e in range(n_dom)], axis=0)

    own = pieces(rows_of(me_slab))
    below = pieces(rows_of(before))
    above = below if n_slab == 2 else pieces(rows_of(after))
    own_at = me_dom * n_slab
    width = ghost_rows // LANES
    sources = (
        (lax.rem(me_dom + n_dom - 1, n_dom) * n_slab + me_slab, 4, own, TILE, 0),
        (lax.rem(me_dom + 1, n_dom) * n_slab + me_slab, 4, own, 0, 4),
        (own_at + before, 4, below, 0, 0),
        (own_at + after, 0, above, 0, 0),
    )
    shift = cap.bit_length() - 1
    bits = atom_rows.bit_length() - 1
    for face, (origin, place, tables, lane_start, row_start) in enumerate(sources):
        packed = recv_ref[origin, place : place + 4, :][:, TILE:].astype(jnp.int32)
        around_ref[face : face + 1, :] = jnp.concatenate([packed[width : width + 1]] * 2, axis=1)
        lines = [packed[r : r + 1] for r in range(width)]
        thirds = [line & (atom_rows - 1) for line in lines] + [line >> bits for line in lines]
        for m in range(width):
            pick = jnp.concatenate(thirds[2 * m : 2 * m + 2], axis=1)
            taken_ref[face : face + 1, m * LANES : (m + 1) * LANES] = pick
            total = find_rows(tables, (pick & (cap - 1)) + lane_start, pick >> shift, n_dom)
            if row_start:
                total = pltpu.roll(total, 4, 0)
            swapped = pltpu.roll(total, TILE, 1)
            tile = local_tiles + (face * ghost_rows) // TILE + 2 * m
            store_tile(jnp.where(half, total, swapped), tile, pool_ref)
            store_tile(jnp.where(half, swapped, total), tile + 1, pool_ref)
            spot = tile * TILE
            kind_ref[0:1, spot : spot + LANES] = total[3:4]
    table = emb_ref[...]
    step = 512
    for start in range(0, h_ref.shape[0], step):
        kinds = kind_ref[0:1, start : start + step].astype(jnp.int32)
        onehot = (iota((16, step), 0) == kinds - 1).astype(F32).astype(BF16)
        h_ref[start : start + step, :] = lax.dot_general(onehot, table, (((0,), (0,)), ((), ())), preferred_element_type=F32).astype(BF16)


class Near:
    def __init__(self, table_ref, shape):
        self.table_ref, self.shape = table_ref, shape

    def __getitem__(self, at):
        return self.table_ref[FACES + at[0], at[1]]


def half_rows(near_ref, pool_ref, tile, side):
    first, second = near_ref[2 * side, tile], near_ref[2 * side + 1, tile]
    lane = iota((8, LANES), 1)
    left = lane < TILE
    xyz = [jnp.where(left, pool_ref[first, w], pool_ref[second, w]) for w in range(3)]
    rows = jnp.where(left, first * TILE, second * TILE) + (lane & (TILE - 1))
    return first, second, xyz, rows


def tall(value, count):
    return jnp.concatenate([value] * count, axis=0) if count > 1 else value


def geometry(column_ref, start, count, xyz, rows):
    column = column_ref[pl.ds(start, count), :]
    offset = [tall(xyz[w], count // 8) - column[:, w : w + 1] for w in range(3)]
    square = offset[0] * offset[0] + offset[1] * offset[1] + offset[2] * offset[2] + SOFTENING
    inverse = lax.rsqrt(square)
    ratio = jnp.minimum(square * inverse * (1.0 / CUTOFF), 1.0)
    same = tall(rows, count // 8) == iota((count, LANES), 0) + start
    ratio = jnp.where(same, 1.0, ratio)
    fade = 1.0 - ratio * ratio
    return offset, inverse, ratio, fade * fade


def edges_of(column_ref, start, count, xyz, rows):
    offset, inverse, ratio, envelope = geometry(column_ref, start, count, xyz, rows)
    x, y, z = (part * inverse for part in offset)
    harmonic = [x, y, z, x * y, y * z, z * x, (x - y) * (x + y), 3.0 * (z * z) - 1.0]
    shifted = ratio - 0.5
    square = shifted * shifted
    sine = series(COS_TERMS, square)
    cosine = -shifted * series(SIN_TERMS, square)
    twice = cosine + cosine
    radial = [sine * (envelope * inverse)]
    radial.append(twice * radial[0])
    while len(radial) < 8:
        radial.append(twice * radial[-1] - radial[-2])
    return harmonic, radial


def store_part(near_ref, pool_ref, column_ref, tile, side, part, harmonic_ref, radial_ref):
    chunk = 16
    _, _, xyz, rows = half_rows(near_ref, pool_ref, tile, side)
    spot = slice(part * chunk, (part + 1) * chunk)
    harmonic, radial = edges_of(column_ref, pl.multiple_of(tile * TILE + part * chunk, chunk), chunk, xyz, rows)
    for k, one in enumerate(harmonic):
        harmonic_ref[k, spot, :] = one.astype(BF16)
    for n, one in enumerate(radial):
        radial_ref[n, spot, :] = one.astype(BF16)
    return jnp.maximum(radial[-1][:8], radial[-1][8:])[:1]


def side_sum(near_ref, h_ref, weight_ref, tile, side, harmonic_ref, radial_ref, gates):
    nears = [near_ref[2 * side + place, tile] for place in range(2)]
    features = jnp.concatenate([h_ref[pl.ds(pl.multiple_of(other * TILE, TILE), TILE), :] for other in nears], axis=0)
    nbasis = weight_ref.shape[0]
    radial = [radial_ref[n] for n in range(nbasis)]
    rows = [jnp.concatenate(radial, axis=1)]
    for k in range(NHARM - 1):
        harmonic = harmonic_ref[k]
        rows.append(jnp.concatenate([harmonic * one for one in radial], axis=1))
    weight = weight_ref[...].astype(F32)
    steps = []
    for m in range(nbasis // 2):
        part = weight[2 * m : 2 * m + 2]
        for one in gates[m]:
            part = jnp.where(one < 1e30, part, 0.0)
        part = part.astype(BF16)
        steps += [features * part[n : n + 1] for n in range(2)]
    return jnp.dot(jnp.concatenate(rows, axis=0), jnp.concatenate(steps, axis=0), preferred_element_type=F32)


def store_query(agg_ref, tile, query_ref):
    channels = agg_ref.shape[1]
    part = [agg_ref[k * TILE : (k + 1) * TILE, :] * (1.0 / TILE**0.5) for k in range(NHARM)]
    square = [one * one for one in part]
    query = [part[0], square[0], square[1] + square[2] + square[3], square[4] + square[5] + square[6] + square[7] + square[8]]
    start = pl.multiple_of(tile * TILE, TILE)
    for spot, one in enumerate(query):
        query_ref[pl.ds(start, TILE), spot * channels : (spot + 1) * channels] = one.astype(BF16)
    return query[-1][:1]


def run_layer(near_ref, pool_ref, column_ref, h_ref, weight_ref, update_ref, out_ref, query_ref, agg_ref, harm_now, harm_next, radial_now, radial_next):
    tiles = near_ref.shape[1]

    harmonics, radials = (harm_now, harm_next), (radial_now, radial_next)

    def make(tile, unit, slot):
        side, part = divmod(unit, 4)
        return store_part(near_ref, pool_ref, column_ref, tile, side, part, harmonics[slot].at[side], radials[slot].at[side])

    for unit in range(8):
        make(0, unit, 0)
    agg_ref[...] = jnp.zeros_like(agg_ref)

    def step(index, carry):
        for turn in range(4):
            slot = turn % 2
            tile = 4 * index + turn
            later = jnp.minimum(tile + 1, tiles - 1)
            query = store_query(agg_ref, jnp.maximum(tile - 1, 0), query_ref)
            units = [make(later, unit, 1 - slot) for unit in range(8)]
            gates = ((), (), (), ())
            sides = [side_sum(near_ref, h_ref, weight_ref, tile, side, harmonics[slot].at[side], radials[slot].at[side], gates) for side in range(2)]
            agg_ref[...] = sides[0] + sides[1]
        return carry

    lax.fori_loop(0, tiles // 4, step, 0)
    store_query(agg_ref, tiles - 1, query_ref)
    block = 256
    for start in range(0, out_ref.shape[0], block):
        update = jnp.dot(query_ref[start : start + block, :], update_ref[...], preferred_element_type=F32)
        live = (column_ref[start : start + block, 3:4] > 0.5).astype(F32)
        fresh = h_ref[start : start + block, :].astype(F32) + update * (1.0 / (1.0 + jnp.exp(-update)))
        out_ref[start : start + block, :] = (fresh * live).astype(BF16)


def spread(refs, size):
    return [(ref, start) for ref in refs for start in range(0, ref.shape[0], size)]


def gather_rows(pick_ref, tasks):
    ghost_rows = pick_ref.shape[1]
    picks = pick_ref[...].astype(F32)
    if picks.shape[0] < 8:
        picks = jnp.concatenate([picks, jnp.zeros((8 - picks.shape[0], ghost_rows), F32)], axis=0)
    for m in range(ghost_rows // LANES):
        columns = picks[:, m * LANES : (m + 1) * LANES].T.astype(jnp.int32)
        for face, source, target, start in tasks:
            onehot = (columns[:, face : face + 1] == iota((LANES, source.shape[0]), 1)).astype(F32).astype(BF16)
            found = jnp.dot(onehot, source[...], preferred_element_type=F32)
            target[start + m * LANES : start + (m + 1) * LANES, :] = found.astype(BF16)


def views(weights_ref, spot):
    radial, nbasis, update, depth = spot
    return weights_ref.at[radial : radial + nbasis], weights_ref.at[update : update + depth]


def first_kernel(n_dom, n_slab, cap, n_out, spot, emb_spot, tiles, table_ref, recv_ref, weights_ref, numbers_ref, *rest):
    near_ref = Near(table_ref, tiles)
    pick_ref = numbers_ref
    emb_ref = weights_ref.at[emb_spot : emb_spot + 16]
    pool_ref, column_ref, around_ref, taken_ref, out_ref = rest[:5]
    outs = rest[5 : 5 + n_out]
    *scratch, h_ref, kind_ref = rest[5 + n_out :]
    build_pool(n_dom, n_slab, cap, pick_ref.shape[1], recv_ref, emb_ref, pool_ref, column_ref, around_ref, taken_ref, h_ref, kind_ref)
    run_layer(near_ref, pool_ref, column_ref, h_ref, *views(weights_ref, spot), out_ref, *scratch)
    gather_rows(pick_ref, [(face, out_ref, ref, start) for face, (ref, start) in enumerate(spread(outs, pick_ref.shape[1]))])


def second_kernel(n_in, spot, force_spot, tiles, table_ref, pool_ref, column_ref, h_in_ref, *rest):
    near_ref = Near(table_ref, tiles)
    ghosts = rest[:n_in]
    weights_ref, out_ref, g_ref = rest[n_in : n_in + 3]
    *scratch, h_ref = rest[n_in + 3 :]
    start = 0
    for ref in (h_in_ref,) + tuple(ghosts):
        h_ref[start : start + ref.shape[0], :] = ref[...]
        start += ref.shape[0]
    run_layer(near_ref, pool_ref, column_ref, h_ref, *views(weights_ref, spot), out_ref, *scratch)
    g_ref[...] = jnp.dot(out_ref[...], weights_ref[force_spot:, :], preferred_element_type=F32).astype(BF16)


def layer_scratch(nbasis, near, channels, atom_rows, pool_rows):
    half = near * TILE // 2
    return [
        pltpu.VMEM((atom_rows, 4 * channels), BF16),
        pltpu.VMEM((NHARM * TILE, channels), F32),
        *[pltpu.VMEM((2, NHARM - 1, TILE, half), BF16)] * 2,
        *[pltpu.VMEM((2, nbasis, TILE, half), BF16)] * 2,
        pltpu.VMEM((pool_rows, channels), BF16),
    ]


def list_blocks(near_ref, around_ref, atom_tiles, face_tiles, early_ref, late_ref):
    near = near_ref.shape[0]
    pool_tiles = atom_tiles + FACES * face_tiles
    spare = (5 * atom_tiles) * 128 + pool_tiles + FACES * face_tiles
    first_slab = atom_tiles + 2 * face_tiles

    def own(tile, counts):
        early, late = counts
        for k in range(near):
            other = near_ref[k, tile]
            entry = tile * 128 + other
            with_dom = ((other >= atom_tiles) & (other < first_slab)).astype(jnp.int32)
            early_ref[early] = entry
            late_ref[late] = entry
            early, late = early + 1 - with_dom, late + with_dom
        return early, late

    counts = lax.fori_loop(0, atom_tiles, own, (jnp.int32(0), jnp.int32(0)))

    def of_others(ref, pairs):
        def others(tile, count):
            for domain, face in pairs:
                start = atom_tiles + face * face_tiles
                for k in range(near):
                    other = around_ref[domain, k * atom_tiles + tile] - start
                    ref[count] = (atom_tiles * (domain + 1) + tile) * 128 + pool_tiles + face * face_tiles + other
                    count = count + ((other >= 0) & (other < face_tiles)).astype(jnp.int32)
            return count

        return others

    early = lax.fori_loop(0, atom_tiles, of_others(early_ref, ((2, 3), (3, 2))), counts[0])
    late = lax.fori_loop(0, atom_tiles, of_others(late_ref, ((0, 1), (1, 0))), counts[1])
    for extra in range(3):
        early_ref[early + extra] = spare
        late_ref[late + extra] = spare
    return early, late


def block_pair(first, second, atom_tiles, pool_ref, column_ref, gi_ref, gj_ref):
    scale = 1.0 / gi_ref.shape[1] ** 0.5
    lane = iota((8, LANES), 1)
    left = lane < TILE
    half = iota((TILE, LANES), 1) < TILE
    i_tiles = [pl.multiple_of((one >> 7) * TILE, TILE) for one in (first, second)]
    j_tiles = [one & 127 for one in (first, second)]
    same = [jnp.where((one >> 7 == one & 127) & (one >> 7 < atom_tiles), 0, 4096) for one in (first, second)]
    rows = jnp.where(left, same[0], same[1]) + (lane & (TILE - 1))
    columns = [column_ref[pl.ds(one, TILE), :] for one in i_tiles]
    mine = jnp.concatenate([gi_ref[pl.ds(one, TILE), :] for one in i_tiles], axis=0)
    others = jnp.concatenate([gj_ref[pl.ds(pl.multiple_of(one * TILE, TILE), TILE), :] for one in j_tiles], axis=0)
    inner = lax.dot_general(mine, others, (((1,), (1,)), ((), ())), preferred_element_type=F32)
    inner = jnp.where(half, inner[:TILE], inner[TILE:])
    offset = []
    for w in range(3):
        away = tall(jnp.where(left, pool_ref[j_tiles[0], w], pool_ref[j_tiles[1], w]), TILE // 8)
        offset.append(away - jnp.where(half, columns[0][:, w : w + 1], columns[1][:, w : w + 1]))
    square = offset[0] * offset[0] + offset[1] * offset[1] + offset[2] * offset[2] + SOFTENING
    inverse = lax.rsqrt(square)
    ratio = jnp.minimum(square * inverse * (1.0 / CUTOFF), 1.0)
    ratio = jnp.where(tall(rows, TILE // 8) == iota((TILE, LANES), 0), 1.0, ratio)
    fade = 1.0 - ratio * ratio
    strength = fade * fade * inverse * (inner * scale)
    return [strength * one for one in offset]


def sum_blocks(list_ref, count, atom_tiles, pool_ref, column_ref, gi_ref, gj_ref, own_ref, total_ref):
    own_ref[...] = jnp.zeros_like(own_ref)
    total_ref[...] = jnp.zeros_like(total_ref)
    left = iota((8, LANES), 1) < TILE
    half = iota((TILE, LANES), 1) < TILE

    def step(index, carry):
        entries = [list_ref[4 * index + spot] for spot in range(4)]
        found = [block_pair(entries[2 * p], entries[2 * p + 1], atom_tiles, pool_ref, column_ref, gi_ref, gj_ref) for p in range(2)]
        for p in range(2):
            for spot in range(2):
                entry = entries[2 * p + spot]
                i_tile, j_tile = jnp.minimum(entry >> 7, atom_tiles), entry & 127
                for w in range(3):
                    pair = found[p][w]
                    against = sum(pair[8 * v : 8 * v + 8] for v in range(TILE // 8))
                    total_ref[j_tile, w] -= jnp.where(left, against, 0.0) if spot == 0 else jnp.where(left, 0.0, against)
                    own_ref[i_tile, w] += jnp.where(half, pair, 0.0) if spot == 0 else jnp.where(half, 0.0, pair)
        return carry

    lax.fori_loop(0, (count + 3) // 4, step, 0)


def gather_forces(pick_ref, faces, atom_tiles, face_tiles, own_ref, total_ref):
    atom_rows = atom_tiles * TILE
    pool_tiles = atom_tiles + FACES * face_tiles
    half = iota((1, LANES), 1) < TILE
    sums = []
    for w in range(3):
        folded = jnp.sum(total_ref[:, w], axis=1)
        sums.append(folded + pltpu.roll(folded, TILE, 1))

    def row(tile):
        lines = [jnp.where(half, sums[w][tile : tile + 1], sums[w][tile + 1 : tile + 2]) for w in range(3)]
        return jnp.concatenate(lines + [jnp.zeros((5, LANES), F32)], axis=0)

    blocks = atom_rows // LANES
    shift = LANES.bit_length() - 1
    total = jnp.concatenate([row(2 * m) for m in range(blocks)], axis=0)
    for face in faces:
        for m in range(face_tiles // 2):
            pick = pick_ref[face : face + 1, m * LANES : (m + 1) * LANES]
            back = row(pool_tiles + face * face_tiles + 2 * m)
            high = pick >> shift
            wide = jnp.concatenate([jnp.where(high == one, back, 0.0) for one in range(blocks)], axis=0)
            onehot = (iota((LANES, LANES), 0) == (pick & (LANES - 1))).astype(F32).astype(BF16)
            for part in pieces(wide)[:2]:
                total = total + lax.dot_general(part, onehot, (((1,), (1,)), ((), ())), preferred_element_type=F32)
    total = jnp.concatenate([total[m * 8 : (m + 1) * 8] for m in range(blocks)], axis=1)
    for w in range(3):
        ones = (iota((8, LANES), 0) == w).astype(F32).astype(BF16)
        mine = jnp.concatenate([own_ref[tile, w] for tile in range(atom_tiles)], axis=0)
        for part in pieces(mine)[:2]:
            total = total + lax.dot_general(ones, part, (((1,), (1,)), ((), ())), preferred_element_type=F32)
    return total


def near_forces_kernel(n_dom, n_slab, cap, tiles, table_ref, around_ref, recv_ref, numbers_ref, taken_ref, pool_in, column_in, g_ref, *rest):
    near_ref = Near(table_ref, tiles)
    pick_ref = numbers_ref
    slabs = rest[: 1 if n_slab == 2 else 2]
    part_ref, pool_ref, column_ref, out_g_ref, late_ref, gi_ref, gj_ref, own_ref, total_ref, early_ref = rest[len(slabs) :]
    atom_rows, channels = g_ref.shape
    ghost_rows = pick_ref.shape[1]
    atom_tiles, face_tiles = atom_rows // TILE, ghost_rows // TILE
    pool_tiles = atom_tiles + FACES * face_tiles
    me_slab = lax.axis_index("slab")
    before, after = lax.rem(me_slab + n_slab - 1, n_slab), lax.rem(me_slab + 1, n_slab)
    early, late = list_blocks(near_ref, around_ref, atom_tiles, face_tiles, early_ref, late_ref.at[0])
    late_ref[1, 0] = late
    column_ref[0:atom_rows, :] = column_in[...]
    column_ref[5 * atom_rows :, :] = jnp.full((TILE, 8), -AWAY, F32)
    per = TILE // cap
    spot = iota((TILE, 8), 1)

    def put(domain, tile, column):
        live = column[:, 3:4] > 0.5
        start = atom_rows * (domain + 1) + tile * TILE
        column_ref[start : start + TILE, :] = jnp.where((spot >= 3) | live, column, -AWAY)

    def tile_of(slab, tile):
        parts = [recv_ref[(tile * per + p) * n_slab + slab] for p in range(per)]
        return jnp.concatenate([one[:, start : start + cap] for start in (0, TILE) for one in parts], axis=1)

    for tile in range(atom_tiles):
        block = tile_of(me_slab, tile)
        put(0, tile, block.T[TILE:])
        put(1, tile, pltpu.roll(block, 4, 0).T[:TILE])
        below = tile_of(before, tile).T[:TILE]
        put(2, tile, below)
        put(3, tile, below if n_slab == 2 else tile_of(after, tile).T[:TILE])
    pool_ref[0:pool_tiles] = pool_in[...]
    pool_ref[pool_tiles + FACES * face_tiles] = jnp.full((3, 8, LANES), AWAY, F32)
    own = pieces(jnp.concatenate([recv_ref[e * n_slab + me_slab] for e in range(n_dom)], axis=0))
    shift = cap.bit_length() - 1
    half = iota((1, LANES), 1) < TILE
    for face in range(FACES):
        for m in range(ghost_rows // LANES):
            pick = pick_ref[face : face + 1, m * LANES : (m + 1) * LANES]
            total = find_rows(own, pick & (cap - 1), pick >> shift, n_dom)
            swapped = pltpu.roll(total, TILE, 1)
            tile = pool_tiles + face * face_tiles + 2 * m
            store_tile(jnp.where(half, total, swapped), tile, pool_ref)
            store_tile(jnp.where(half, swapped, total), tile + 1, pool_ref)
    gi_ref[0:atom_rows, :] = g_ref[...]
    gj_ref[0:atom_rows, :] = g_ref[...]
    spare = jnp.zeros((TILE, channels), BF16)
    gi_ref[5 * atom_rows :, :] = spare
    gj_ref[(pool_tiles + FACES * face_tiles) * TILE :, :] = spare
    gi_ref[3 * atom_rows : 4 * atom_rows, :] = slabs[0][...]
    gi_ref[4 * atom_rows : 5 * atom_rows, :] = slabs[-1][...]
    gather_rows(pick_ref, [(face, g_ref, gj_ref, pool_tiles * TILE + face * ghost_rows) for face in range(FACES)])
    gather_rows(taken_ref, [(face, ref, gj_ref, atom_rows + face * ghost_rows) for face, ref in ((2, slabs[0]), (3, slabs[-1]))])
    out_g_ref[...] = gj_ref[pool_tiles * TILE : pool_tiles * TILE + 2 * ghost_rows, :]
    sum_blocks(early_ref, early, atom_tiles, pool_ref, column_ref, gi_ref, gj_ref, own_ref, total_ref)
    part_ref[...] = gather_forces(pick_ref, (2, 3), atom_tiles, face_tiles, own_ref, total_ref)


def far_forces_kernel(list_ref, numbers_ref, taken_ref, pool_ref, column_ref, g_ref, out_g_ref, below_ref, above_ref, part_ref, out_ref, gi_ref, gj_ref, own_ref, total_ref):
    pick_ref = numbers_ref
    atom_rows, channels = g_ref.shape
    ghost_rows = pick_ref.shape[1]
    atom_tiles, face_tiles = atom_rows // TILE, ghost_rows // TILE
    pool_tiles = atom_tiles + FACES * face_tiles
    spare = jnp.zeros((TILE, channels), BF16)
    gi_ref[0:atom_rows, :] = g_ref[...]
    gi_ref[atom_rows : 2 * atom_rows, :] = below_ref[...]
    gi_ref[2 * atom_rows : 3 * atom_rows, :] = above_ref[...]
    gi_ref[5 * atom_rows :, :] = spare
    gj_ref[pool_tiles * TILE : pool_tiles * TILE + 2 * ghost_rows, :] = out_g_ref[...]
    gj_ref[(pool_tiles + FACES * face_tiles) * TILE :, :] = spare
    gather_rows(taken_ref, [(face, ref, gj_ref, atom_rows + face * ghost_rows) for face, ref in ((0, below_ref), (1, above_ref))])
    sum_blocks(list_ref.at[0], list_ref[1, 0], atom_tiles, pool_ref, column_ref, gi_ref, gj_ref, own_ref, total_ref)
    total = gather_forces(pick_ref, (0, 1), atom_tiles, face_tiles, own_ref, total_ref) + part_ref[...]
    out_ref[...] = total[0:3]


def passed_along(array, axis, by):
    count = lax.axis_size(axis)
    return lax.ppermute(array, axis, [(i, (i + by) % count) for i in range(count)])


def exchange(arrays, by):
    moved = [passed_along(arrays[0], "dom", by), passed_along(arrays[1], "dom", -by)]
    for one, way in zip(arrays[2:], (by, -by)):
        moved.append(passed_along(one, "slab", way))
    return moved


def body(n_dom, n_slab, positions, species, send_pick, ghost_pick, near_tiles, embedding, radial_weight, update_weight, force_weight):
    atom_rows = positions.shape[0]
    cap = send_pick.shape[1]
    ghost_rows = ghost_pick.shape[1]
    tiles, near = near_tiles.shape
    channels = embedding.shape[1]
    nbasis = radial_weight.shape[1]
    pool_rows = atom_rows + FACES * ghost_rows
    face_rows = [ghost_rows, ghost_rows] + ([2 * ghost_rows] if n_slab == 2 else [ghost_rows, ghost_rows])
    n_out = len(face_rows)
    face_out = [jax.ShapeDtypeStruct((rows, channels), BF16) for rows in face_rows]
    scratch = layer_scratch(nbasis, near, channels, atom_rows, pool_rows)

    sent, weights, numbers = send_states(n_dom, n_slab, positions, species, send_pick, ghost_pick, near_tiles, embedding, radial_weight, update_weight, force_weight)
    update_spot, force_spot = weight_spots(radial_weight.shape, update_weight.shape)
    spots = [(16 * m, nbasis, at, update_weight.shape[1]) for m, at in enumerate(update_spot)]
    got = lax.all_to_all(sent, ("dom", "slab"), split_axis=0, concat_axis=0, tiled=True)

    pool, column, around, taken, hidden, *faces = pl.pallas_call(
        functools.partial(first_kernel, n_dom, n_slab, cap, n_out, spots[0], 16 * len(spots), (near, tiles)),
        out_shape=[
            jax.ShapeDtypeStruct((pool_rows // TILE, 3, 8, LANES), F32),
            jax.ShapeDtypeStruct((atom_rows, 8), F32),
            jax.ShapeDtypeStruct((8, LANES), jnp.int32),
            jax.ShapeDtypeStruct((8, ghost_rows), jnp.int32),
            jax.ShapeDtypeStruct((atom_rows, channels), BF16),
        ]
        + face_out,
        in_specs=[SMEM] + [VMEM] * 3,
        out_specs=[VMEM] * (5 + n_out),
        scratch_shapes=scratch + [pltpu.VMEM((8, pool_rows), F32)],
        compiler_params=params(),
        name="first_layer",
    )(numbers, got, weights, numbers)

    faces = exchange(faces, 1)
    features, mine = pl.pallas_call(
        functools.partial(second_kernel, n_out, spots[1], force_spot, (near, tiles)),
        out_shape=[jax.ShapeDtypeStruct((atom_rows, channels), BF16)] * 2,
        in_specs=[SMEM] + [VMEM] * (4 + n_out),
        out_specs=[VMEM] * 2,
        scratch_shapes=scratch,
        compiler_params=params(),
        name="second_layer",
    )(numbers, pool, column, hidden, *faces, weights)

    slabs = [passed_along(mine, "slab", 1)]
    if n_slab != 2:
        slabs.append(passed_along(mine, "slab", -1))
    below, above = passed_along(mine, "dom", 1), passed_along(mine, "dom", -1)
    face_tiles = ghost_rows // TILE
    i_rows = 5 * atom_rows + TILE
    j_tiles = pool_rows // TILE + FACES * face_tiles + 1
    longest = (near * tiles) * 5 + 4
    force_scratch = [
        pltpu.VMEM((i_rows, channels), BF16),
        pltpu.VMEM((j_tiles * TILE, channels), BF16),
        pltpu.VMEM((tiles + 1, 3, TILE, LANES), F32),
        pltpu.VMEM((j_tiles, 3, 8, LANES), F32),
    ]
    part, pool, column, out_g, late = pl.pallas_call(
        functools.partial(near_forces_kernel, n_dom, n_slab, cap, (near, tiles)),
        out_shape=[
            jax.ShapeDtypeStruct((8, atom_rows), F32),
            jax.ShapeDtypeStruct((j_tiles, 3, 8, LANES), F32),
            jax.ShapeDtypeStruct((i_rows, 8), F32),
            jax.ShapeDtypeStruct((2 * ghost_rows, channels), BF16),
            jax.ShapeDtypeStruct((2, longest), jnp.int32),
        ],
        in_specs=[SMEM] * 2 + [VMEM] * (6 + len(slabs)),
        out_specs=[VMEM] * 4 + [SMEM],
        scratch_shapes=force_scratch + [pltpu.SMEM((longest,), jnp.int32)],
        cost_estimate=pl.CostEstimate(flops=4_000_000_000, bytes_accessed=4_000_000, transcendentals=0),
        compiler_params=params(),
        name="near_forces",
    )(numbers, around, got, numbers, taken, pool, column, mine, *slabs)
    forces = pl.pallas_call(
        far_forces_kernel,
        out_shape=jax.ShapeDtypeStruct((3, atom_rows), F32),
        in_specs=[SMEM] + [VMEM] * 9,
        out_specs=VMEM,
        scratch_shapes=force_scratch,
        compiler_params=params(),
        name="far_forces",
    )(late, numbers, taken, pool, column, mine, out_g, below, above, part)
    return features, forces


def solution(mesh):
    both = ("dom", "slab")
    return jax.shard_map(
        functools.partial(body, mesh.shape["dom"], mesh.shape["slab"]),
        mesh=mesh,
        in_specs=(P(both, None), P(both), P(both, None), P(both, None), P(both, None), P(), P(), P(), P()),
        out_specs=(P(both, None), P(None, both)),
        check_vma=False,
    )
```

time: 100 us -> 81.3 us (0.81)
  waiting for transfers between devices: 13.5 us -> 2.99 us
  starting transfers between devices: 17 us -> 11.5 us
  blocking collectives: 17.7 us -> 15.5 us
  local copies, waits for them, and re-layouts: 2.82 us -> 1.68 us
    ppermute x9 -> x6, waiting for transfers between devices: 13.5 us -> 2.99 us  [passed_along(): lax.ppermute(array, axis, [(i, (i + by) % count) for i in range(count)])]
    ppermute x9 -> x6, starting transfers between devices: 17 us -> 11.5 us  [passed_along(): lax.ppermute(array, axis, [(i, (i + by) % count) for i in range(count)])]
    all_to_all x1, blocking collectives: 17.7 us -> 15.5 us  [body(): lax.all_to_all(sent, ('dom', 'slab'), split_axis=0, concat_axis=0, tiled=...]
    unnamed x20 -> x6, local copies, waits for them, and re-layouts: 2.82 us -> 1.68 us
  transfers between devices with their start and end apart: 9 -> 6, of which waited for: 4 -> 1; matrix products, arithmetic and copies ran while one was open for 0% -> 0% of each run, Pallas kernels for 0% -> 13%
where the time goes in v2:
time: 81.3 us; the launch traced here: 80.8 us
  Pallas kernels  48.4 us (60%)
  blocking collectives  15.5 us (19%)
  starting transfers between devices  11.5 us (14%)
  waiting for transfers between devices  2.99 us (4%)
  local copies, waits for them, and re-layouts  1.68 us (2%)
    pallas_call x1, Pallas kernels, body(): pl.pallas_call(functools.partial(first_kernel, n_dom, n_slab, cap, n_out,...  15.9 us
    all_to_all x1, blocking collectives, body(): lax.all_to_all(sent, ('dom', 'slab'), split_axis=0, concat_axis=0, tiled=...  15.5 us
    pallas_call x1, Pallas kernels, body(): pl.pallas_call(functools.partial(second_kernel, n_out, spots[1], force_sp...  14.4 us
    ppermute x6, starting transfers between devices, passed_along(): lax.ppermute(array, axis, [(i, (i + by) % count) for i in range(count)])  11.5 us
    pallas_call x1, Pallas kernels, body(): pl.pallas_call(functools.partial(near_forces_kernel, n_dom, n_slab, cap,...  10.6 us
    pallas_call x1, Pallas kernels, body(): pl.pallas_call(far_forces_kernel, out_shape=jax.ShapeDtypeStruct((3, atom...  5.24 us
    ppermute x6, waiting for transfers between devices, passed_along(): lax.ppermute(array, axis, [(i, (i + by) % count) for i in range(count)])  2.99 us
    pallas_call x1, Pallas kernels, send_states(): pl.pallas_call(functools.partial(send_kernel, n_dom, n_slab), out_shape=[...  2.26 us
  transfers between devices with their start and end apart: 6, of which 1 were waited for; matrix products, arithmetic and copies ran while one was open for 0% of the time, Pallas kernels for 13%

profile of v2, /device:TPU:0, one launch (start us, length us, event | category | flops | bytes accessed | tf_op | source)
XLA Modules:
  0.0 80.8 jit_solution(6558004543994565205)
XLA Ops:
  0.6 2.3 %send_states.1 = (f32[32,8,128]{2,1,0:T(8,128)}, bf16[1200,128]{1,0:T(8,128)(2,1)}, s32[8,384]{1,0:T(8,128)}) custom-call(f32[3,1024]{1,0:T(4,128)} %bitcast.3, s32[1,1024]{1,0:T(1,128)} %bitcast.4, s32[16,64]{1,0:T(8,128)} %pick_in.1, s32[4,384]{1,0:T(4,128)} %ghost_in.1, s32[4,16]{1,0:T(4,128)} %bitcast.5, bf16[10,128]{1,0:T(8,128)(2,1)} %embedding_in.1, ...), custom_call_target="tpu_custom_call" | custom-call | tf_op jit(solution)/shard_map/send_states/pallas_call | solution.py:132
  2.9 0.0 copy-start.2
  2.9 15.5 %all_to_all.5.recv_ref = f32[32,8,128]{2,1,0:T(8,128)S(1)} all-to-all(f32[32,8,128]{2,1,0:T(8,128)} %get-tuple-element.21), channel_id=1, replica_groups=mesh['dom'=16,'slab'=2] {'dom','slab'}, dimensions={0} | all-to-all | bytes 262144 | tf_op jit(solution)/shard_map/all_to_all | solution.py:640
  18.5 0.0 copy-start
  18.5 1.0 %copy-done = bf16[1200,128]{1,0:T(8,128)(2,1)S(1)} copy-done((bf16[1200,128]{1,0:T(8,128)(2,1)S(1)}, bf16[1200,128]{1,0:T(8,128)(2,1)}, u32[]{:S(2)}) %copy-start) | copy-done | bytes 307224
  19.4 0.0 copy-start.1
  19.4 0.7 copy-done.1
  20.1 15.9 %first_layer.1 = (f32[40,3,8,128]{3,2,1,0:T(8,128)S(1)}, f32[1024,8]{1,0:T(8,128)S(1)}, s32[8,128]{1,0:T(8,128)S(1)}, s32[8,384]{1,0:T(8,128)S(1)}, bf16[1024,12...) custom-call(s32[8,384]{1,0:T(8,128)S(1)} %copy-done.1, ...), custom_call_target="tpu_custom_call" | custom-call | tf_op jit(solution)/shard_map/first_layer/pallas_call | solution.py:642
  36.1 0.3 collective-permute-start.2
  36.3 0.4 collective-permute-start
  36.7 5.3 %collective-permute-start.1 = (bf16[384,128]{1,0:T(8,128)(2,1)S(1)}, bf16[384,128]{1,0:T(8,128)(2,1)S(1)}, u32[]{:S(2)}, u32[]{:S(2)}) collective-permute-start(bf16[384,128]{1,0:T(8,128)(2,1)S(1)} %get-tuple-element.27), channel_id=1, source_target_pairs={{0,30},{2,0},{4,2},{6,4},{8,6},{10,8},{12,10},{14,12},{16,14},{18,... | collective-permute-start | bytes 294920 | tf_op jit(solution)/shard_map/ppermute | solution.py:614
  42.0 3.0 %collective-permute-done.rest_0_ = bf16[384,128]{1,0:T(8,128)(2,1)S(1)} collective-permute-done((bf16[384,128]{1,0:T(8,128)(2,1)S(1)}, bf16[384,128]{1,0:T(8,128)(2,1)S(1)}, u32[]{:S(2)}, u32[]{:S(2)}) %collective-permute-start) | collective-permute-done | bytes 98336 | tf_op jit(solution)/shard_map/ppermute | solution.py:614
  44.9 0.0 collective-permute-done.1.rest_1_
  44.9 0.0 collective-permute-done.2.rest_2_
  44.9 14.4 %second_layer.1 = (bf16[1024,128]{1,0:T(8,128)(2,1)}, bf16[1024,128]{1,0:T(8,128)(2,1)S(1)}) custom-call(s32[8,384]{1,0:T(8,128)S(1)} %copy-done.1, f32[40,3,8,128]{3,2,1,0:T(8,128)S(1)} %get-tuple-element.23.pool_ref.pool_in, f32[1024,8]{1,0:T(8,128)S(1)} %get-tuple-element.24.column_ref.column_in, bf16[1024,128]{1,0:T(8,128)(2,1)S(1)} %get-tuple-element.25.h_in_ref, ...), custom_call_target="tpu_custom_call" | custom-call | tf_op jit(solution)/shard_map/second_layer/pallas_call | solution.py:660
  59.3 0.0 collective-permute-start.3
  59.3 0.0 collective-permute-start.4
  59.3 5.6 %collective-permute-start.5 = (bf16[1024,128]{1,0:T(8,128)(2,1)S(1)}, bf16[1024,128]{1,0:T(8,128)(2,1)S(1)}, u32[]{:S(2)}, u32[]{:S(2)}) collective-permute-start(bf16[1024,128]{1,0:T(8,128)(2,1)S(1)} %get-tuple-element.32.g_ref), channel_id=1, source_target_pairs={{0,30},{2,0},{4,2},{6,4},{8,6},{10,8},{12,10},{14,12},{16,14},{18,... | collective-permute-start | bytes 786440 | tf_op jit(solution)/shard_map/ppermute | solution.py:614
  64.9 0.0 collective-permute-done.3.rest_0_
  64.9 0.0 copy-done.2
  64.9 10.6 %near_forces.1 = (f32[8,1024]{1,0:T(8,128)S(1)}, f32[65,3,8,128]{3,2,1,0:T(8,128)S(1)}, f32[5184,8]{1,0:T(8,128)S(1)}, bf16[768,128]{1,0:T(8,128)(2,1)S(1)}, s32[2,324]{1,0:T(2,128)S(1)}) custom-call(s32[8,384]{1,0:T(8,128)S(1)} %copy-done.2, s32[8,128]{1,0:T(8,128)S(1)} %get-tuple-element.30.around_ref, f32[32,8,128]{2,1,0:T(8,128)S(1)} %all_to_all.5.recv_ref, ...), custom_call_target="tpu_custom_call" | custom-call | flops 4000000000 | bytes 4000000 | tf_op jit(solution)/shard_map/near_forces/pallas_call | solution.py:684
  75.6 0.0 collective-permute-done.4.below_ref
  75.6 0.0 collective-permute-done.5.above_ref
  75.6 5.2 %far_forces.1 = f32[3,1024]{1,0:T(4,128)} custom-call(s32[2,324]{1,0:T(2,128)S(1)} %get-tuple-element.33.list_ref, s32[8,384]{1,0:T(8,128)S(1)} %copy-done.2, s32[8,384]{1,0:T(8,128)S(1)} %get-tuple-element.31.taken_ref, f32[65,3,8,128]{3,2,1,0:T(8,128)S(1)} %get-tuple-element.34.pool_ref, f32[5184,8]{1,0:T(8,128)S(1)} %get-tuple-element.35.column_ref, ...), custom_call_target="tpu_custom_call" | custom-call | tf_op jit(solution)/shard_map/far_forces/pallas_call | solution.py:700
Async XLA Ops:
  2.9 62.0 %copy-start.2 = (s32[8,384]{1,0:T(8,128)S(1)}, s32[8,384]{1,0:T(8,128)}, u32[]{:S(2)}) copy-start(s32[8,384]{1,0:T(8,128)} %get-tuple-element.20.table_ref.numbers_ref) | copy-start | bytes 36868
  18.5 1.0 %copy-start = (bf16[1200,128]{1,0:T(8,128)(2,1)S(1)}, bf16[1200,128]{1,0:T(8,128)(2,1)}, u32[]{:S(2)}) copy-start(bf16[1200,128]{1,0:T(8,128)(2,1)} %get-tuple-element.22.weights_ref.rest_3_) | copy-start | bytes 921604
  19.4 0.7 copy-start.1
  36.1 8.9 %collective-permute-start.2 = (bf16[768,128]{1,0:T(8,128)(2,1)S(1)}, bf16[768,128]{1,0:T(8,128)(2,1)S(1)}, u32[]{:S(2)}, u32[]{:S(2)}) collective-permute-start(bf16[768,128]{1,0:T(8,128)(2,1)S(1)} %get-tuple-element.28), channel_id=1, source_target_pairs={{0,1},{1,0},{2,3},{3,2},{4,5},{5,4},{6,7},{7,6},{8,9},{9,8},{10,11... | collective-permute-start | bytes 589832 | tf_op jit(solution)/shard_map/ppermute | solution.py:614
  36.3 8.6 %collective-permute-start = (bf16[384,128]{1,0:T(8,128)(2,1)S(1)}, bf16[384,128]{1,0:T(8,128)(2,1)S(1)}, u32[]{:S(2)}, u32[]{:S(2)}) collective-permute-start(bf16[384,128]{1,0:T(8,128)(2,1)S(1)} %get-tuple-element.26), channel_id=1, source_target_pairs={{0,2},{2,4},{4,6},{6,8},{8,10},{10,12},{12,14},{14,16},{16,18},{18... | collective-permute-start | bytes 294920 | tf_op jit(solution)/shard_map/ppermute | solution.py:614
  36.7 8.2 %collective-permute-start.1 = (bf16[384,128]{1,0:T(8,128)(2,1)S(1)}, bf16[384,128]{1,0:T(8,128)(2,1)S(1)}, u32[]{:S(2)}, u32[]{:S(2)}) collective-permute-start(bf16[384,128]{1,0:T(8,128)(2,1)S(1)} %get-tuple-element.27), channel_id=1, source_target_pairs={{0,30},{2,0},{4,2},{6,4},{8,6},{10,8},{12,10},{14,12},{16,14},{18,... | collective-permute-start | bytes 294920 | tf_op jit(solution)/shard_map/ppermute | solution.py:614
  59.3 5.6 %collective-permute-start.3 = (bf16[1024,128]{1,0:T(8,128)(2,1)S(1)}, bf16[1024,128]{1,0:T(8,128)(2,1)S(1)}, u32[]{:S(2)}, u32[]{:S(2)}) collective-permute-start(bf16[1024,128]{1,0:T(8,128)(2,1)S(1)} %get-tuple-element.32.g_ref), channel_id=1, source_target_pairs={{0,1},{1,0},{2,3},{3,2},{4,5},{5,4},{6,7},{7,6},{8,9},{9,8},{10,11... | collective-permute-start | bytes 786440 | tf_op jit(solution)/shard_map/ppermute | solution.py:614
  59.3 16.3 %collective-permute-start.4 = (bf16[1024,128]{1,0:T(8,128)(2,1)S(1)}, bf16[1024,128]{1,0:T(8,128)(2,1)S(1)}, u32[]{:S(2)}, u32[]{:S(2)}) collective-permute-start(bf16[1024,128]{1,0:T(8,128)(2,1)S(1)} %get-tuple-element.32.g_ref), channel_id=1, source_target_pairs={{0,2},{2,4},{4,6},{6,8},{8,10},{10,12},{12,14},{14,16},{16,18},{18... | collective-permute-start | bytes 786440 | tf_op jit(solution)/shard_map/ppermute | solution.py:614
  59.3 16.3 %collective-permute-start.5 = (bf16[1024,128]{1,0:T(8,128)(2,1)S(1)}, bf16[1024,128]{1,0:T(8,128)(2,1)S(1)}, u32[]{:S(2)}, u32[]{:S(2)}) collective-permute-start(bf16[1024,128]{1,0:T(8,128)(2,1)S(1)} %get-tuple-element.32.g_ref), channel_id=1, source_target_pairs={{0,30},{2,0},{4,2},{6,4},{8,6},{10,8},{12,10},{14,12},{16,14},{18,... | collective-permute-start | bytes 786440 | tf_op jit(solution)/shard_map/ppermute | solution.py:614

commit v3 on v2

--- a/solution.py
+++ b/solution.py
@@ -26,7 +26,7 @@
 
 
 def params(mib=40):
-    return pltpu.CompilerParams(vmem_limit_bytes=mib * 1024 * 1024)
+    return pltpu.CompilerParams(vmem_limit_bytes=int(mib * 1024 * 1024))
 
 
 def pieces(value):
@@ -313,7 +313,7 @@
     return query[-1][:1]
 
 
-def run_layer(near_ref, pool_ref, column_ref, h_ref, weight_ref, update_ref, out_ref, query_ref, agg_ref, harm_now, harm_next, radial_now, radial_next):
+def run_layer(turns, near_ref, pool_ref, column_ref, h_ref, weight_ref, update_ref, out_ref, query_ref, agg_ref, harm_now, harm_next, radial_now, radial_next):
     tiles = near_ref.shape[1]
 
     harmonics, radials = (harm_now, harm_next), (radial_now, radial_next)
@@ -327,9 +327,9 @@
     agg_ref[...] = jnp.zeros_like(agg_ref)
 
     def step(index, carry):
-        for turn in range(4):
+        for turn in range(turns):
             slot = turn % 2
-            tile = 4 * index + turn
+            tile = turns * index + turn
             later = jnp.minimum(tile + 1, tiles - 1)
             query = store_query(agg_ref, jnp.maximum(tile - 1, 0), query_ref)
             units = [make(later, unit, 1 - slot) for unit in range(8)]
@@ -338,11 +338,12 @@
             agg_ref[...] = sides[0] + sides[1]
         return carry
 
-    lax.fori_loop(0, tiles // 4, step, 0)
+    lax.fori_loop(0, tiles // turns, step, 0)
     store_query(agg_ref, tiles - 1, query_ref)
+    changes = jnp.dot(query_ref[...], update_ref[...], preferred_element_type=F32)
     block = 256
     for start in range(0, out_ref.shape[0], block):
-        update = jnp.dot(query_ref[start : start + block, :], update_ref[...], preferred_element_type=F32)
+        update = changes[start : start + block]
         live = (column_ref[start : start + block, 3:4] > 0.5).astype(F32)
         fresh = h_ref[start : start + block, :].astype(F32) + update * (1.0 / (1.0 + jnp.exp(-update)))
         out_ref[start : start + block, :] = (fresh * live).astype(BF16)
@@ -352,17 +353,28 @@
     return [(ref, start) for ref in refs for start in range(0, ref.shape[0], size)]
 
 
-def gather_rows(pick_ref, tasks):
+def is_even():
+    return lax.rem(lax.axis_index("dom"), 2) == 0
+
+
+def gather_rows(pick_ref, tasks, keep=None):
     ghost_rows = pick_ref.shape[1]
     picks = pick_ref[...].astype(F32)
+    if keep is not None:
+        picks = jnp.concatenate([jnp.where(keep, picks[0:1], picks[1:2]), jnp.where(keep, picks[1:2], picks[0:1]), picks[2:]], axis=0)
     if picks.shape[0] < 8:
         picks = jnp.concatenate([picks, jnp.zeros((8 - picks.shape[0], ghost_rows), F32)], axis=0)
-    for m in range(ghost_rows // LANES):
-        columns = picks[:, m * LANES : (m + 1) * LANES].T.astype(jnp.int32)
-        for face, source, target, start in tasks:
-            onehot = (columns[:, face : face + 1] == iota((LANES, source.shape[0]), 1)).astype(F32).astype(BF16)
-            found = jnp.dot(onehot, source[...], preferred_element_type=F32)
-            target[start + m * LANES : start + (m + 1) * LANES, :] = found.astype(BF16)
+    columns = [picks[:, m * LANES : (m + 1) * LANES].T.astype(jnp.int32) for m in range(ghost_rows // LANES)]
+    sources = []
+    for _, source, _, _ in tasks:
+        if not any(source is one for one in sources):
+            sources.append(source)
+    for source in sources:
+        here = [task for task in tasks if task[1] is source]
+        onehot = [(column[:, task[0] : task[0] + 1] == iota((LANES, source.shape[0]), 1)).astype(F32).astype(BF16) for task in here for column in columns]
+        found = jnp.dot(jnp.concatenate(onehot, axis=0), source[...], preferred_element_type=F32).astype(BF16)
+        for spot, (_, _, target, start) in enumerate(here):
+            target[pl.ds(start if isinstance(start, int) else pl.multiple_of(start, LANES), ghost_rows), :] = found[spot * ghost_rows : (spot + 1) * ghost_rows]
 
 
 def views(weights_ref, spot):
@@ -374,24 +386,30 @@
     near_ref = Near(table_ref, tiles)
     pick_ref = numbers_ref
     emb_ref = weights_ref.at[emb_spot : emb_spot + 16]
-    pool_ref, column_ref, around_ref, taken_ref, out_ref = rest[:5]
-    outs = rest[5 : 5 + n_out]
-    *scratch, h_ref, kind_ref = rest[5 + n_out :]
+    pool_ref, column_ref, around_ref, taken_ref, kept_ref, out_ref = rest[:6]
+    outs = rest[6 : 6 + n_out]
+    *scratch, h_ref, kind_ref = rest[6 + n_out :]
+    kept_ref[...] = weights_ref[...]
     build_pool(n_dom, n_slab, cap, pick_ref.shape[1], recv_ref, emb_ref, pool_ref, column_ref, around_ref, taken_ref, h_ref, kind_ref)
-    run_layer(near_ref, pool_ref, column_ref, h_ref, *views(weights_ref, spot), out_ref, *scratch)
-    gather_rows(pick_ref, [(face, out_ref, ref, start) for face, (ref, start) in enumerate(spread(outs, pick_ref.shape[1]))])
-
-
-def second_kernel(n_in, spot, force_spot, tiles, table_ref, pool_ref, column_ref, h_in_ref, *rest):
+    run_layer(4, near_ref, pool_ref, column_ref, h_ref, *views(weights_ref, spot), out_ref, *scratch)
+    gather_rows(pick_ref, [(face, out_ref, ref, start) for face, (ref, start) in enumerate(spread(outs, pick_ref.shape[1]))], is_even())
+
+
+def second_kernel(n_in, spot, force_spot, tiles, table_ref, list_ref, pool_ref, column_ref, h_in_ref, *rest):
     near_ref = Near(table_ref, tiles)
     ghosts = rest[:n_in]
     weights_ref, out_ref, g_ref = rest[n_in : n_in + 3]
     *scratch, h_ref = rest[n_in + 3 :]
-    start = 0
-    for ref in (h_in_ref,) + tuple(ghosts):
+    atom_rows, ghost_rows = h_in_ref.shape[0], ghosts[0].shape[0]
+    even = is_even().astype(jnp.int32)
+    h_ref[0:atom_rows, :] = h_in_ref[...]
+    for block, ref in zip((even, 1 - even), ghosts):
+        h_ref[pl.ds(pl.multiple_of(atom_rows + block * ghost_rows, LANES), ghost_rows), :] = ref[...]
+    start = atom_rows + 2 * ghost_rows
+    for ref in ghosts[2:]:
         h_ref[start : start + ref.shape[0], :] = ref[...]
         start += ref.shape[0]
-    run_layer(near_ref, pool_ref, column_ref, h_ref, *views(weights_ref, spot), out_ref, *scratch)
+    run_layer(16, near_ref, pool_ref, column_ref, h_ref, *views(weights_ref, spot), out_ref, *scratch)
     g_ref[...] = jnp.dot(out_ref[...], weights_ref[force_spot:, :], preferred_element_type=F32).astype(BF16)
 
 
@@ -439,7 +457,7 @@
 
     early = lax.fori_loop(0, atom_tiles, of_others(early_ref, ((2, 3), (3, 2))), counts[0])
     late = lax.fori_loop(0, atom_tiles, of_others(late_ref, ((0, 1), (1, 0))), counts[1])
-    for extra in range(3):
+    for extra in range(7):
         early_ref[early + extra] = spare
         late_ref[late + extra] = spare
     return early, late
@@ -479,9 +497,9 @@
     half = iota((TILE, LANES), 1) < TILE
 
     def step(index, carry):
-        entries = [list_ref[4 * index + spot] for spot in range(4)]
-        found = [block_pair(entries[2 * p], entries[2 * p + 1], atom_tiles, pool_ref, column_ref, gi_ref, gj_ref) for p in range(2)]
-        for p in range(2):
+        entries = [list_ref[8 * index + spot] for spot in range(8)]
+        found = [block_pair(entries[2 * p], entries[2 * p + 1], atom_tiles, pool_ref, column_ref, gi_ref, gj_ref) for p in range(4)]
+        for p in range(4):
             for spot in range(2):
                 entry = entries[2 * p + spot]
                 i_tile, j_tile = jnp.minimum(entry >> 7, atom_tiles), entry & 127
@@ -492,7 +510,7 @@
                     own_ref[i_tile, w] += jnp.where(half, pair, 0.0) if spot == 0 else jnp.where(half, 0.0, pair)
         return carry
 
-    lax.fori_loop(0, (count + 3) // 4, step, 0)
+    lax.fori_loop(0, (count + 7) // 8, step, 0)
 
 
 def gather_forces(pick_ref, faces, atom_tiles, face_tiles, own_ref, total_ref):
@@ -529,18 +547,16 @@
     return total
 
 
-def near_forces_kernel(n_dom, n_slab, cap, tiles, table_ref, around_ref, recv_ref, numbers_ref, taken_ref, pool_in, column_in, g_ref, *rest):
+def neighbour_kernel(n_dom, n_slab, cap, tiles, table_ref, around_ref, recv_ref, numbers_ref, pool_in, column_in, early_ref, late_ref, pool_ref, column_ref):
     near_ref = Near(table_ref, tiles)
     pick_ref = numbers_ref
-    slabs = rest[: 1 if n_slab == 2 else 2]
-    part_ref, pool_ref, column_ref, out_g_ref, late_ref, gi_ref, gj_ref, own_ref, total_ref, early_ref = rest[len(slabs) :]
-    atom_rows, channels = g_ref.shape
-    ghost_rows = pick_ref.shape[1]
+    atom_rows, ghost_rows = column_in.shape[0], pick_ref.shape[1]
     atom_tiles, face_tiles = atom_rows // TILE, ghost_rows // TILE
     pool_tiles = atom_tiles + FACES * face_tiles
     me_slab = lax.axis_index("slab")
     before, after = lax.rem(me_slab + n_slab - 1, n_slab), lax.rem(me_slab + 1, n_slab)
-    early, late = list_blocks(near_ref, around_ref, atom_tiles, face_tiles, early_ref, late_ref.at[0])
+    early, late = list_blocks(near_ref, around_ref, atom_tiles, face_tiles, early_ref.at[0], late_ref.at[0])
+    early_ref[1, 0] = early
     late_ref[1, 0] = late
     column_ref[0:atom_rows, :] = column_in[...]
     column_ref[5 * atom_rows :, :] = jnp.full((TILE, 8), -AWAY, F32)
@@ -576,6 +592,16 @@
             tile = pool_tiles + face * face_tiles + 2 * m
             store_tile(jnp.where(half, total, swapped), tile, pool_ref)
             store_tile(jnp.where(half, swapped, total), tile + 1, pool_ref)
+
+
+def near_forces_kernel(n_slab, list_ref, numbers_ref, taken_ref, pool_ref, column_ref, g_ref, *rest):
+    pick_ref = numbers_ref
+    slabs = rest[: 1 if n_slab == 2 else 2]
+    part_ref, out_g_ref, gi_ref, gj_ref, own_ref, total_ref = rest[len(slabs) :]
+    atom_rows, channels = g_ref.shape
+    ghost_rows = pick_ref.shape[1]
+    atom_tiles, face_tiles = atom_rows // TILE, ghost_rows // TILE
+    pool_tiles = atom_tiles + FACES * face_tiles
     gi_ref[0:atom_rows, :] = g_ref[...]
     gj_ref[0:atom_rows, :] = g_ref[...]
     spare = jnp.zeros((TILE, channels), BF16)
@@ -586,11 +612,11 @@
     gather_rows(pick_ref, [(face, g_ref, gj_ref, pool_tiles * TILE + face * ghost_rows) for face in range(FACES)])
     gather_rows(taken_ref, [(face, ref, gj_ref, atom_rows + face * ghost_rows) for face, ref in ((2, slabs[0]), (3, slabs[-1]))])
     out_g_ref[...] = gj_ref[pool_tiles * TILE : pool_tiles * TILE + 2 * ghost_rows, :]
-    sum_blocks(early_ref, early, atom_tiles, pool_ref, column_ref, gi_ref, gj_ref, own_ref, total_ref)
+    sum_blocks(list_ref.at[0], list_ref[1, 0], atom_tiles, pool_ref, column_ref, gi_ref, gj_ref, own_ref, total_ref)
     part_ref[...] = gather_forces(pick_ref, (2, 3), atom_tiles, face_tiles, own_ref, total_ref)
 
 
-def far_forces_kernel(list_ref, numbers_ref, taken_ref, pool_ref, column_ref, g_ref, out_g_ref, below_ref, above_ref, part_ref, out_ref, gi_ref, gj_ref, own_ref, total_ref):
+def far_forces_kernel(list_ref, numbers_ref, taken_ref, pool_ref, column_ref, g_ref, out_g_ref, first_ref, second_ref, part_ref, out_ref, gi_ref, gj_ref, own_ref, total_ref):
     pick_ref = numbers_ref
     atom_rows, channels = g_ref.shape
     ghost_rows = pick_ref.shape[1]
@@ -598,12 +624,14 @@
     pool_tiles = atom_tiles + FACES * face_tiles
     spare = jnp.zeros((TILE, channels), BF16)
     gi_ref[0:atom_rows, :] = g_ref[...]
-    gi_ref[atom_rows : 2 * atom_rows, :] = below_ref[...]
-    gi_ref[2 * atom_rows : 3 * atom_rows, :] = above_ref[...]
+    even = is_even().astype(jnp.int32)
+    spots = (even, 1 - even)
+    for spot, ref in zip(spots, (first_ref, second_ref)):
+        gi_ref[pl.ds(pl.multiple_of((1 + spot) * atom_rows, LANES), atom_rows), :] = ref[...]
     gi_ref[5 * atom_rows :, :] = spare
     gj_ref[pool_tiles * TILE : pool_tiles * TILE + 2 * ghost_rows, :] = out_g_ref[...]
     gj_ref[(pool_tiles + FACES * face_tiles) * TILE :, :] = spare
-    gather_rows(taken_ref, [(face, ref, gj_ref, atom_rows + face * ghost_rows) for face, ref in ((0, below_ref), (1, above_ref))])
+    gather_rows(taken_ref, [(face, ref, gj_ref, atom_rows + spots[face] * ghost_rows) for face, ref in ((0, first_ref), (1, second_ref))], even == 0)
     sum_blocks(list_ref.at[0], list_ref[1, 0], atom_tiles, pool_ref, column_ref, gi_ref, gj_ref, own_ref, total_ref)
     total = gather_forces(pick_ref, (0, 1), atom_tiles, face_tiles, own_ref, total_ref) + part_ref[...]
     out_ref[...] = total[0:3]
@@ -614,11 +642,10 @@
     return lax.ppermute(array, axis, [(i, (i + by) % count) for i in range(count)])
 
 
-def exchange(arrays, by):
-    moved = [passed_along(arrays[0], "dom", by), passed_along(arrays[1], "dom", -by)]
-    for one, way in zip(arrays[2:], (by, -by)):
-        moved.append(passed_along(one, "slab", way))
-    return moved
+def swapped(first, second):
+    count = lax.axis_size("dom")
+    ends = lax.ppermute(second, "dom", [(i, (i - 1 if i % 2 == 0 else i + 1) % count) for i in range(count)])
+    return lax.ppermute(first, "dom", [(i, i + 1 if i % 2 == 0 else i - 1) for i in range(count)]), ends
 
 
 def body(n_dom, n_slab, positions, species, send_pick, ghost_pick, near_tiles, embedding, radial_weight, update_weight, force_weight):
@@ -632,6 +659,10 @@
     face_rows = [ghost_rows, ghost_rows] + ([2 * ghost_rows] if n_slab == 2 else [ghost_rows, ghost_rows])
     n_out = len(face_rows)
     face_out = [jax.ShapeDtypeStruct((rows, channels), BF16) for rows in face_rows]
+    face_tiles = ghost_rows // TILE
+    i_rows = 5 * atom_rows + TILE
+    j_tiles = pool_rows // TILE + FACES * face_tiles + 1
+    longest = (near * tiles) * 5 + 8
     scratch = layer_scratch(nbasis, near, channels, atom_rows, pool_rows)
 
     sent, weights, numbers = send_states(n_dom, n_slab, positions, species, send_pick, ghost_pick, near_tiles, embedding, radial_weight, update_weight, force_weight)
@@ -639,64 +670,68 @@
     spots = [(16 * m, nbasis, at, update_weight.shape[1]) for m, at in enumerate(update_spot)]
     got = lax.all_to_all(sent, ("dom", "slab"), split_axis=0, concat_axis=0, tiled=True)
 
-    pool, column, around, taken, hidden, *faces = pl.pallas_call(
+    pool, column, around, taken, kept, hidden, *faces = pl.pallas_call(
         functools.partial(first_kernel, n_dom, n_slab, cap, n_out, spots[0], 16 * len(spots), (near, tiles)),
         out_shape=[
             jax.ShapeDtypeStruct((pool_rows // TILE, 3, 8, LANES), F32),
             jax.ShapeDtypeStruct((atom_rows, 8), F32),
             jax.ShapeDtypeStruct((8, LANES), jnp.int32),
             jax.ShapeDtypeStruct((8, ghost_rows), jnp.int32),
+            jax.ShapeDtypeStruct(weights.shape, BF16),
             jax.ShapeDtypeStruct((atom_rows, channels), BF16),
         ]
         + face_out,
         in_specs=[SMEM] + [VMEM] * 3,
-        out_specs=[VMEM] * (5 + n_out),
+        out_specs=[VMEM] * (6 + n_out),
         scratch_shapes=scratch + [pltpu.VMEM((8, pool_rows), F32)],
         compiler_params=params(),
         name="first_layer",
     )(numbers, got, weights, numbers)
 
-    faces = exchange(faces, 1)
+    early, late, wide_pool, wide_column = pl.pallas_call(
+        functools.partial(neighbour_kernel, n_dom, n_slab, cap, (near, tiles)),
+        out_shape=[
+            jax.ShapeDtypeStruct((2, longest), jnp.int32),
+            jax.ShapeDtypeStruct((2, longest), jnp.int32),
+            jax.ShapeDtypeStruct((j_tiles, 3, 8, LANES), F32),
+            jax.ShapeDtypeStruct((i_rows, 8), F32),
+        ],
+        in_specs=[SMEM] * 2 + [VMEM] * 4,
+        out_specs=[SMEM] * 2 + [VMEM] * 2,
+        compiler_params=params(),
+        name="neighbours",
+    )(numbers, around, got, numbers, pool, column)
+    faces = [*swapped(*faces[:2]), *(passed_along(one, "slab", way) for one, way in zip(faces[2:], (1, -1)))]
     features, mine = pl.pallas_call(
         functools.partial(second_kernel, n_out, spots[1], force_spot, (near, tiles)),
         out_shape=[jax.ShapeDtypeStruct((atom_rows, channels), BF16)] * 2,
-        in_specs=[SMEM] + [VMEM] * (4 + n_out),
+        in_specs=[SMEM] * 2 + [VMEM] * (4 + n_out),
         out_specs=[VMEM] * 2,
         scratch_shapes=scratch,
         compiler_params=params(),
         name="second_layer",
-    )(numbers, pool, column, hidden, *faces, weights)
+    )(numbers, early, pool, column, hidden, *faces, kept)
 
     slabs = [passed_along(mine, "slab", 1)]
     if n_slab != 2:
         slabs.append(passed_along(mine, "slab", -1))
-    below, above = passed_along(mine, "dom", 1), passed_along(mine, "dom", -1)
-    face_tiles = ghost_rows // TILE
-    i_rows = 5 * atom_rows + TILE
-    j_tiles = pool_rows // TILE + FACES * face_tiles + 1
-    longest = (near * tiles) * 5 + 4
+    first, second = swapped(mine, mine)
     force_scratch = [
         pltpu.VMEM((i_rows, channels), BF16),
         pltpu.VMEM((j_tiles * TILE, channels), BF16),
         pltpu.VMEM((tiles + 1, 3, TILE, LANES), F32),
         pltpu.VMEM((j_tiles, 3, 8, LANES), F32),
     ]
-    part, pool, column, out_g, late = pl.pallas_call(
-        functools.partial(near_forces_kernel, n_dom, n_slab, cap, (near, tiles)),
-        out_shape=[
-            jax.ShapeDtypeStruct((8, atom_rows), F32),
-            jax.ShapeDtypeStruct((j_tiles, 3, 8, LANES), F32),
-            jax.ShapeDtypeStruct((i_rows, 8), F32),
-            jax.ShapeDtypeStruct((2 * ghost_rows, channels), BF16),
-            jax.ShapeDtypeStruct((2, longest), jnp.int32),
-        ],
-        in_specs=[SMEM] * 2 + [VMEM] * (6 + len(slabs)),
-        out_specs=[VMEM] * 4 + [SMEM],
-        scratch_shapes=force_scratch + [pltpu.SMEM((longest,), jnp.int32)],
+    part, out_g = pl.pallas_call(
+        functools.partial(near_forces_kernel, n_slab),
+        out_shape=[jax.ShapeDtypeStruct((8, atom_rows), F32), jax.ShapeDtypeStruct((2 * ghost_rows, channels), BF16)],
+        in_specs=[SMEM] + [VMEM] * (5 + len(slabs)),
+        out_specs=[VMEM] * 2,
+        scratch_shapes=force_scratch,
         cost_estimate=pl.CostEstimate(flops=4_000_000_000, bytes_accessed=4_000_000, transcendentals=0),
         compiler_params=params(),
         name="near_forces",
-    )(numbers, around, got, numbers, taken, pool, column, mine, *slabs)
+    )(early, numbers, taken, wide_pool, wide_column, mine, *slabs)
     forces = pl.pallas_call(
         far_forces_kernel,
         out_shape=jax.ShapeDtypeStruct((3, atom_rows), F32),
@@ -705,7 +740,7 @@
         scratch_shapes=force_scratch,
         compiler_params=params(),
         name="far_forces",
-    )(late, numbers, taken, pool, column, mine, out_g, below, above, part)
+    )(late, numbers, taken, wide_pool, wide_column, mine, out_g, first, second, part)
     return features, forces
 
 

time: 81.3 us -> 78.3 us (0.963)
  starting transfers between devices: 11.5 us -> 5.49 us
  waiting for transfers between devices: 2.99 us -> 6.74 us
    ppermute x6 -> x2, starting transfers between devices: 11.5 us -> 0.3 us  [passed_along(): lax.ppermute(array, axis, [(i, (i + by) % count) for i in range(count)])]
    ppermute x0 -> x4, waiting for transfers between devices: none -> 6.73 us  [the longest x2 5.58 us: swapped(): lax.ppermute(second, 'dom', [(i, (i - 1 if i % 2 == 0 else i + 1) % count...]
    ppermute x0 -> x4, starting transfers between devices: none -> 5.19 us  [the longest x2 4.87 us: swapped(): lax.ppermute(second, 'dom', [(i, (i - 1 if i % 2 == 0 else i + 1) % count...]
    ppermute x6 -> x2, waiting for transfers between devices: 2.99 us -> 0.01 us  [passed_along(): lax.ppermute(array, axis, [(i, (i + by) % count) for i in range(count)])]
    pallas_call x1 -> x2, Pallas kernels: 10.6 us -> 10.4 us  [the longest x1 6.5 us: body(): pl.pallas_call(functools.partial(near_forces_kernel, n_slab), out_shape=[...]
    unnamed x6 -> x4, local copies, waits for them, and re-layouts: 1.68 us -> 1.67 us
  transfers between devices with their start and end apart: 6 -> 6, of which waited for: 1 -> 3; matrix products, arithmetic and copies ran while one was open for 0% -> 0% of each run, Pallas kernels for 13% -> 13%
where the time goes in v3:
time: 78.3 us; the launch traced here: 78.1 us
  Pallas kernels  48 us (61%)
  blocking collectives  15.5 us (20%)
  waiting for transfers between devices  6.74 us (9%)
  starting transfers between devices  5.49 us (7%)
  local copies, waits for them, and re-layouts  1.67 us (2%)
    pallas_call x1, Pallas kernels, body(): pl.pallas_call(functools.partial(first_kernel, n_dom, n_slab, cap, n_out,...  16.2 us
    all_to_all x1, blocking collectives, body(): lax.all_to_all(sent, ('dom', 'slab'), split_axis=0, concat_axis=0, tiled=...  15.5 us
    pallas_call x1, Pallas kernels, body(): pl.pallas_call(functools.partial(second_kernel, n_out, spots[1], force_sp...  13.8 us
    pallas_call x1, Pallas kernels, body(): pl.pallas_call(functools.partial(near_forces_kernel, n_slab), out_shape=[...  6.5 us
    ppermute x2, waiting for transfers between devices, swapped(): lax.ppermute(second, 'dom', [(i, (i - 1 if i % 2 == 0 else i + 1) % count...  5.58 us
    pallas_call x1, Pallas kernels, body(): pl.pallas_call(far_forces_kernel, out_shape=jax.ShapeDtypeStruct((3, atom...  5.34 us
    ppermute x2, starting transfers between devices, swapped(): lax.ppermute(second, 'dom', [(i, (i - 1 if i % 2 == 0 else i + 1) % count...  4.87 us
    pallas_call x1, Pallas kernels, body(): pl.pallas_call(functools.partial(neighbour_kernel, n_dom, n_slab, cap, (n...  3.89 us
  transfers between devices with their start and end apart: 6, of which 3 were waited for; matrix products, arithmetic and copies ran while one was open for 0% of the time, Pallas kernels for 13%

profile of v3, /device:TPU:0, one launch (start us, length us, event | category | flops | bytes accessed | tf_op | source)
XLA Modules:
  0.0 78.1 jit_solution(16045461810070151372)
XLA Ops:
  0.6 2.3 %send_states.1 = (f32[32,8,128]{2,1,0:T(8,128)}, bf16[1200,128]{1,0:T(8,128)(2,1)}, s32[8,384]{1,0:T(8,128)}) custom-call(f32[3,1024]{1,0:T(4,128)} %bitcast.3, s32[1,1024]{1,0:T(1,128)} %bitcast.4, s32[16,64]{1,0:T(8,128)} %pick_in.1, s32[4,384]{1,0:T(4,128)} %ghost_in.1, s32[4,16]{1,0:T(4,128)} %bitcast.5, bf16[10,128]{1,0:T(8,128)(2,1)} %embedding_in.1, ...), custom_call_target="tpu_custom_call" | custom-call | tf_op jit(solution)/shard_map/send_states/pallas_call | solution.py:132
  2.9 15.5 %all_to_all.5.recv_ref = f32[32,8,128]{2,1,0:T(8,128)S(1)} all-to-all(f32[32,8,128]{2,1,0:T(8,128)} %get-tuple-element.23), channel_id=1, replica_groups=mesh['dom'=16,'slab'=2] {'dom','slab'}, dimensions={0} | all-to-all | bytes 262144 | tf_op jit(solution)/shard_map/all_to_all | solution.py:671
  18.4 0.0 copy-start
  18.4 0.7 copy-done
  19.2 0.0 copy-start.1
  19.2 1.0 %copy-done.1 = bf16[1200,128]{1,0:T(8,128)(2,1)S(1)} copy-done((bf16[1200,128]{1,0:T(8,128)(2,1)S(1)}, bf16[1200,128]{1,0:T(8,128)(2,1)}, u32[]{:S(2)}) %copy-start.1) | copy-done | bytes 307224
  20.1 16.2 %first_layer.1 = (f32[40,3,8,128]{3,2,1,0:T(8,128)S(1)}, f32[1024,8]{1,0:T(8,128)S(1)}, s32[8,128]{1,0:T(8,128)S(1)}, s32[8,384]{1,0:T(8,128)S(1)}, bf16[1200,12...) custom-call(s32[8,384]{1,0:T(8,128)S(1)} %copy-done, ...), custom_call_target="tpu_custom_call" | custom-call | tf_op jit(solution)/shard_map/first_layer/pallas_call | solution.py:673
  36.4 0.3 collective-permute-start.2
  36.7 0.3 collective-permute-start
  37.0 2.4 %collective-permute-start.1 = (bf16[384,128]{1,0:T(8,128)(2,1)S(1)}, bf16[384,128]{1,0:T(8,128)(2,1)S(1)}, u32[]{:S(2)}, u32[]{:S(2)}) collective-permute-start(bf16[384,128]{1,0:T(8,128)(2,1)S(1)} %get-tuple-element.31), channel_id=1, source_target_pairs={{0,30},{2,4},{4,2},{6,8},{8,6},{10,12},{12,10},{14,16},{16,14},{18... | collective-permute-start | bytes 294920 | tf_op jit(solution)/shard_map/ppermute | solution.py:647
  39.4 3.9 %neighbours.1 = (s32[2,328]{1,0:T(2,128)S(1)}, s32[2,328]{1,0:T(2,128)S(1)}, f32[65,3,8,128]{3,2,1,0:T(8,128)S(1)}, f32[5184,8]{1,0:T(8,128)S(1)}) custom-call(s32[8,384]{1,0:T(8,128)S(1)} %copy-done, s32[8,128]{1,0:T(8,128)S(1)} %get-tuple-element.25.around_ref, f32[32,8,128]{2,1,0:T(8,128)S(1)} %all_to_all.5.recv_ref, s32[8,384]{1,0:T(8,128)S(1)} %copy-done, ...), custom_call_target="tpu_custom_call" | custom-call | tf_op jit(solution)/shard_map/neighbours/pallas_call | solution.py:691
  43.3 0.0 collective-permute-done.rest_0_
  43.3 2.1 %collective-permute-done.1.rest_1_ = bf16[384,128]{1,0:T(8,128)(2,1)S(1)} collective-permute-done((bf16[384,128]{1,0:T(8,128)(2,1)S(1)}, bf16[384,128]{1,0:T(8,128)(2,1)S(1)}, u32[]{:S(2)}, u32[]{:S(2)}) %collective-permute-start.1) | collective-permute-done | bytes 98336 | tf_op jit(solution)/shard_map/ppermute | solution.py:647
  45.4 0.0 collective-permute-done.2.rest_2_
  45.4 13.8 %second_layer.1 = (bf16[1024,128]{1,0:T(8,128)(2,1)}, bf16[1024,128]{1,0:T(8,128)(2,1)S(1)}) custom-call(s32[8,384]{1,0:T(8,128)S(1)} %copy-done, s32[2,328]{1,0:T(2,128)S(1)} %get-tuple-element.28.list_ref, f32[40,3,8,128]{3,2,1,0:T(8,128)S(1)} %get-tuple-element.26.pool_in.pool_ref, f32[1024,8]{1,0:T(8,128)S(1)} %get-tuple-element.27.column_in.column_ref, ...), custom_call_target="tpu_custom_call" | custom-call | tf_op jit(solution)/shard_map/second_layer/pallas_call | solution.py:705
  59.2 0.0 collective-permute-start.3
  59.2 2.4 %collective-permute-start.5 = (bf16[1024,128]{1,0:T(8,128)(2,1)S(1)}, bf16[1024,128]{1,0:T(8,128)(2,1)S(1)}, u32[]{:S(2)}, u32[]{:S(2)}) collective-permute-start(bf16[1024,128]{1,0:T(8,128)(2,1)S(1)} %get-tuple-element.39.g_ref), channel_id=1, source_target_pairs={{0,30},{2,4},{4,2},{6,8},{8,6},{10,12},{12,10},{14,16},{16,14},{18... | collective-permute-start | bytes 786440 | tf_op jit(solution)/shard_map/ppermute | solution.py:647
  61.6 0.0 collective-permute-start.4
  61.6 0.0 collective-permute-done.3.rest_0_
  61.6 6.5 %near_forces.1 = (f32[8,1024]{1,0:T(8,128)S(1)}, bf16[768,128]{1,0:T(8,128)(2,1)S(1)}) custom-call(s32[2,328]{1,0:T(2,128)S(1)} %get-tuple-element.28.list_ref, s32[8,384]{1,0:T(8,128)S(1)} %copy-done, s32[8,384]{1,0:T(8,128)S(1)} %get-tuple-element.36.taken_ref, f32[65,3,8,128]{3,2,1,0:T(8,128)S(1)} %get-tuple-element.37.pool_ref, ...), custom_call_target="tpu_custom_call" | custom-call | flops 4000000000 | bytes 4000000 | tf_op jit(solution)/shard_map/near_forces/pallas_call | solution.py:725
  68.1 3.5 %collective-permute-done.5.second_ref = bf16[1024,128]{1,0:T(8,128)(2,1)S(1)} collective-permute-done((bf16[1024,128]{1,0:T(8,128)(2,1)S(1)}, bf16[1024,128]{1,0:T(8,128)(2,1)S(1)}, u32[]{:S(2)}, u32[]{:S(2)}) %collective-permute-start.5) | collective-permute-done | bytes 262176 | tf_op jit(solution)/shard_map/ppermute | solution.py:647
  71.6 1.1 %collective-permute-done.4.first_ref = bf16[1024,128]{1,0:T(8,128)(2,1)S(1)} collective-permute-done((bf16[1024,128]{1,0:T(8,128)(2,1)S(1)}, bf16[1024,128]{1,0:T(8,128)(2,1)S(1)}, u32[]{:S(2)}, u32[]{:S(2)}) %collective-permute-start.4) | collective-permute-done | bytes 262176 | tf_op jit(solution)/shard_map/ppermute | solution.py:648
  72.8 5.3 %far_forces.1 = f32[3,1024]{1,0:T(4,128)} custom-call(s32[2,328]{1,0:T(2,128)S(1)} %get-tuple-element.35.list_ref, s32[8,384]{1,0:T(8,128)S(1)} %copy-done, s32[8,384]{1,0:T(8,128)S(1)} %get-tuple-element.36.taken_ref, f32[65,3,8,128]{3,2,1,0:T(8,128)S(1)} %get-tuple-element.37.pool_ref, f32[5184,8]{1,0:T(8,128)S(1)} %get-tuple-element.38.column_ref, ...), custom_call_target="tpu_custom_call" | custom-call | tf_op jit(solution)/shard_map/far_forces/pallas_call | solution.py:735
Async XLA Ops:
  18.4 0.7 copy-start
  19.2 1.0 %copy-start.1 = (bf16[1200,128]{1,0:T(8,128)(2,1)S(1)}, bf16[1200,128]{1,0:T(8,128)(2,1)}, u32[]{:S(2)}) copy-start(bf16[1200,128]{1,0:T(8,128)(2,1)} %get-tuple-element.24.weights_ref) | copy-start | bytes 921604
  36.4 9.1 %collective-permute-start.2 = (bf16[768,128]{1,0:T(8,128)(2,1)S(1)}, bf16[768,128]{1,0:T(8,128)(2,1)S(1)}, u32[]{:S(2)}, u32[]{:S(2)}) collective-permute-start(bf16[768,128]{1,0:T(8,128)(2,1)S(1)} %get-tuple-element.32), channel_id=1, source_target_pairs={{0,1},{1,0},{2,3},{3,2},{4,5},{5,4},{6,7},{7,6},{8,9},{9,8},{10,11... | collective-permute-start | bytes 589832 | tf_op jit(solution)/shard_map/ppermute | solution.py:642
  36.7 6.7 %collective-permute-start = (bf16[384,128]{1,0:T(8,128)(2,1)S(1)}, bf16[384,128]{1,0:T(8,128)(2,1)S(1)}, u32[]{:S(2)}, u32[]{:S(2)}) collective-permute-start(bf16[384,128]{1,0:T(8,128)(2,1)S(1)} %get-tuple-element.30), channel_id=1, source_target_pairs={{0,2},{2,0},{4,6},{6,4},{8,10},{10,8},{12,14},{14,12},{16,18},{18,... | collective-permute-start | bytes 294920 | tf_op jit(solution)/shard_map/ppermute | solution.py:648
  37.0 8.4 %collective-permute-start.1 = (bf16[384,128]{1,0:T(8,128)(2,1)S(1)}, bf16[384,128]{1,0:T(8,128)(2,1)S(1)}, u32[]{:S(2)}, u32[]{:S(2)}) collective-permute-start(bf16[384,128]{1,0:T(8,128)(2,1)S(1)} %get-tuple-element.31), channel_id=1, source_target_pairs={{0,30},{2,4},{4,2},{6,8},{8,6},{10,12},{12,10},{14,16},{16,14},{18... | collective-permute-start | bytes 294920 | tf_op jit(solution)/shard_map/ppermute | solution.py:647
  59.2 2.5 %collective-permute-start.3 = (bf16[1024,128]{1,0:T(8,128)(2,1)S(1)}, bf16[1024,128]{1,0:T(8,128)(2,1)S(1)}, u32[]{:S(2)}, u32[]{:S(2)}) collective-permute-start(bf16[1024,128]{1,0:T(8,128)(2,1)S(1)} %get-tuple-element.39.g_ref), channel_id=1, source_target_pairs={{0,1},{1,0},{2,3},{3,2},{4,5},{5,4},{6,7},{7,6},{8,9},{9,8},{10,11... | collective-permute-start | bytes 786440 | tf_op jit(solution)/shard_map/ppermute | solution.py:642
  59.2 12.4 %collective-permute-start.5 = (bf16[1024,128]{1,0:T(8,128)(2,1)S(1)}, bf16[1024,128]{1,0:T(8,128)(2,1)S(1)}, u32[]{:S(2)}, u32[]{:S(2)}) collective-permute-start(bf16[1024,128]{1,0:T(8,128)(2,1)S(1)} %get-tuple-element.39.g_ref), channel_id=1, source_target_pairs={{0,30},{2,4},{4,2},{6,8},{8,6},{10,12},{12,10},{14,16},{16,14},{18... | collective-permute-start | bytes 786440 | tf_op jit(solution)/shard_map/ppermute | solution.py:647
  61.6 11.1 %collective-permute-start.4 = (bf16[1024,128]{1,0:T(8,128)(2,1)S(1)}, bf16[1024,128]{1,0:T(8,128)(2,1)S(1)}, u32[]{:S(2)}, u32[]{:S(2)}) collective-permute-start(bf16[1024,128]{1,0:T(8,128)(2,1)S(1)} %get-tuple-element.39.g_ref), channel_id=1, source_target_pairs={{0,2},{2,0},{4,6},{6,4},{8,10},{10,8},{12,14},{14,12},{16,18},{18,... | collective-permute-start | bytes 786440 | tf_op jit(solution)/shard_map/ppermute | solution.py:648

commit v4 on v3

--- a/solution.py
+++ b/solution.py
@@ -48,7 +48,7 @@
     return lax.broadcasted_iota(jnp.int32, shape, dim)
 
 
-def send_kernel(n_dom, n_slab, pos_in, kind_in, pick_in, ghost_in, near_in, embedding_in, radial_in, update_in, force_in, out_ref, weights_ref, numbers_ref,
+def send_kernel(n_dom, n_slab, pos_in, kind_in, pick_in, ghost_in, near_in, embedding_in, radial_in, update_in, force_in, out_ref, weights_ref,
                 pos_ref, kind_ref, pick_ref, ghost_ref, near_ref, embedding_ref, radial_ref, picked_ref, sems):
     update_spot, force_spot = weight_spots(radial_in.shape, update_in.shape)
     pairs = [(pos_in, pos_ref), (kind_in, kind_ref), (pick_in, pick_ref), (ghost_in, ghost_ref), (near_in, near_ref), (embedding_in, embedding_ref), (radial_in, radial_ref)]
@@ -60,9 +60,11 @@
         copies[-1].start()
     for copy in copies:
         copy.wait()
-    numbers_ref[...] = jnp.zeros_like(numbers_ref)
-    numbers_ref[0:FACES, :] = ghost_ref[...]
-    numbers_ref[FACES : FACES + near_ref.shape[0], 0 : near_ref.shape[1]] = near_ref[...]
+    beside = jnp.zeros((near_ref.shape[0], ghost_ref.shape[1] - near_ref.shape[1]), jnp.int32)
+    numbers = jnp.concatenate([ghost_ref[...], jnp.concatenate([near_ref[...], beside], axis=1)], axis=0)
+    parts = [part[:, m * LANES : (m + 1) * LANES] for part in (numbers >> 5, numbers & 31) for m in range(numbers.shape[1] // LANES)]
+    number_spot = force_spot + force_in.shape[0]
+    weights_ref[number_spot:, :] = jnp.concatenate(parts, axis=0).astype(F32).astype(BF16)
     blank = jnp.zeros((16, embedding_ref.shape[1]), F32)
     for level in range(radial_ref.shape[0]):
         weights_ref[16 * level : 16 * level + 16, :] = jnp.concatenate([radial_ref[level].astype(F32), blank[radial_ref.shape[1] :]], axis=0).astype(BF16)
@@ -128,16 +130,15 @@
 def send_states(n_dom, n_slab, positions, species, send_pick, ghost_pick, near_tiles, embedding, radial, update, force):
     cap = send_pick.shape[1]
     inputs = (positions.T, species.reshape(1, -1), send_pick, ghost_pick, near_tiles.T, embedding, radial, update, force)
-    count = weight_spots(radial.shape, update.shape)[1] + force.shape[0]
+    count = weight_spots(radial.shape, update.shape)[1] + force.shape[0] + 16 * (ghost_pick.shape[1] // LANES)
     return pl.pallas_call(
         functools.partial(send_kernel, n_dom, n_slab),
         out_shape=[
             jax.ShapeDtypeStruct((n_dom * n_slab, 8, LANES), F32),
             jax.ShapeDtypeStruct((count, force.shape[1]), BF16),
-            jax.ShapeDtypeStruct((8, ghost_pick.shape[1]), jnp.int32),
         ],
         in_specs=[pl.BlockSpec(memory_space=pl.ANY)] * len(inputs),
-        out_specs=[VMEM] * 3,
+        out_specs=[VMEM] * 2,
         scratch_shapes=[pltpu.VMEM(one.shape, one.dtype) for one in inputs[:7]]
         + [pltpu.VMEM((n_dom, 8, cap), F32), pltpu.SemaphoreType.DMA((8 + update.shape[0],))],
         compiler_params=params(63),
@@ -382,15 +383,24 @@
     return weights_ref.at[radial : radial + nbasis], weights_ref.at[update : update + depth]
 
 
-def first_kernel(n_dom, n_slab, cap, n_out, spot, emb_spot, tiles, table_ref, recv_ref, weights_ref, numbers_ref, *rest):
+def first_kernel(n_dom, n_slab, cap, n_out, spot, emb_spot, number_spot, tiles, recv_ref, weights_ref, numbers_ref, *rest):
+    *rest, table_ref, sem = rest
+    parts = weights_ref[number_spot:, :].astype(F32).astype(jnp.int32)
+    blocks = parts.shape[0] // 16
+    for m in range(blocks):
+        top, low = parts[8 * m : 8 * m + 8], parts[8 * (m + blocks) : 8 * (m + blocks) + 8]
+        numbers_ref[:, m * LANES : (m + 1) * LANES] = (top << 5) + low
+    copy = pltpu.make_async_copy(numbers_ref, table_ref, sem)
+    copy.start()
     near_ref = Near(table_ref, tiles)
     pick_ref = numbers_ref
     emb_ref = weights_ref.at[emb_spot : emb_spot + 16]
     pool_ref, column_ref, around_ref, taken_ref, kept_ref, out_ref = rest[:6]
     outs = rest[6 : 6 + n_out]
     *scratch, h_ref, kind_ref = rest[6 + n_out :]
-    kept_ref[...] = weights_ref[...]
+    kept_ref[...] = weights_ref[:number_spot, :]
     build_pool(n_dom, n_slab, cap, pick_ref.shape[1], recv_ref, emb_ref, pool_ref, column_ref, around_ref, taken_ref, h_ref, kind_ref)
+    copy.wait()
     run_layer(4, near_ref, pool_ref, column_ref, h_ref, *views(weights_ref, spot), out_ref, *scratch)
     gather_rows(pick_ref, [(face, out_ref, ref, start) for face, (ref, start) in enumerate(spread(outs, pick_ref.shape[1]))], is_even())
 
@@ -665,28 +675,29 @@
     longest = (near * tiles) * 5 + 8
     scratch = layer_scratch(nbasis, near, channels, atom_rows, pool_rows)
 
-    sent, weights, numbers = send_states(n_dom, n_slab, positions, species, send_pick, ghost_pick, near_tiles, embedding, radial_weight, update_weight, force_weight)
+    sent, weights = send_states(n_dom, n_slab, positions, species, send_pick, ghost_pick, near_tiles, embedding, radial_weight, update_weight, force_weight)
     update_spot, force_spot = weight_spots(radial_weight.shape, update_weight.shape)
     spots = [(16 * m, nbasis, at, update_weight.shape[1]) for m, at in enumerate(update_spot)]
     got = lax.all_to_all(sent, ("dom", "slab"), split_axis=0, concat_axis=0, tiled=True)
 
-    pool, column, around, taken, kept, hidden, *faces = pl.pallas_call(
-        functools.partial(first_kernel, n_dom, n_slab, cap, n_out, spots[0], 16 * len(spots), (near, tiles)),
+    numbers, pool, column, around, taken, kept, hidden, *faces = pl.pallas_call(
+        functools.partial(first_kernel, n_dom, n_slab, cap, n_out, spots[0], 16 * len(spots), force_spot + channels, (near, tiles)),
         out_shape=[
+            jax.ShapeDtypeStruct((8, ghost_rows), jnp.int32),
             jax.ShapeDtypeStruct((pool_rows // TILE, 3, 8, LANES), F32),
             jax.ShapeDtypeStruct((atom_rows, 8), F32),
             jax.ShapeDtypeStruct((8, LANES), jnp.int32),
             jax.ShapeDtypeStruct((8, ghost_rows), jnp.int32),
-            jax.ShapeDtypeStruct(weights.shape, BF16),
+            jax.ShapeDtypeStruct((force_spot + channels, channels), BF16),
             jax.ShapeDtypeStruct((atom_rows, channels), BF16),
         ]
         + face_out,
-        in_specs=[SMEM] + [VMEM] * 3,
-        out_specs=[VMEM] * (6 + n_out),
-        scratch_shapes=scratch + [pltpu.VMEM((8, pool_rows), F32)],
+        in_specs=[VMEM] * 2,
+        out_specs=[VMEM] * (7 + n_out),
+        scratch_shapes=scratch + [pltpu.VMEM((8, pool_rows), F32), pltpu.SMEM((8, ghost_rows), jnp.int32), pltpu.SemaphoreType.DMA],
         compiler_params=params(),
         name="first_layer",
-    )(numbers, got, weights, numbers)
+    )(got, weights)
 
     early, late, wide_pool, wide_column = pl.pallas_call(
         functools.partial(neighbour_kernel, n_dom, n_slab, cap, (near, tiles)),

time: 78.3 us -> 76.5 us (0.977)
  Pallas kernels: 48 us -> 47.2 us
    unnamed x4 -> x2, local copies, waits for them, and re-layouts: 1.67 us -> 0.97 us
  transfers between devices with their start and end apart: 6 -> 6, of which waited for: 3 -> 3; matrix products, arithmetic and copies ran while one was open for 0% -> 0% of each run, Pallas kernels for 13% -> 14%
where the time goes in v4:
time: 76.5 us; the launch traced here: 76.6 us
  Pallas kernels  47.2 us (62%)
  blocking collectives  15.5 us (20%)
  waiting for transfers between devices  6.77 us (9%)
  starting transfers between devices  5.46 us (7%)
  local copies, waits for them, and re-layouts  0.97 us (1%)
    pallas_call x1, Pallas kernels, body(): pl.pallas_call(functools.partial(first_kernel, n_dom, n_slab, cap, n_out,...  15.9 us
    all_to_all x1, blocking collectives, body(): lax.all_to_all(sent, ('dom', 'slab'), split_axis=0, concat_axis=0, tiled=...  15.5 us
    pallas_call x1, Pallas kernels, body(): pl.pallas_call(functools.partial(second_kernel, n_out, spots[1], force_sp...  13.7 us
    pallas_call x1, Pallas kernels, body(): pl.pallas_call(functools.partial(near_forces_kernel, n_slab), out_shape=[...  6.49 us
    ppermute x2, waiting for transfers between devices, swapped(): lax.ppermute(second, 'dom', [(i, (i - 1 if i % 2 == 0 else i + 1) % count...  5.6 us
    pallas_call x1, Pallas kernels, body(): pl.pallas_call(far_forces_kernel, out_shape=jax.ShapeDtypeStruct((3, atom...  4.96 us
    ppermute x2, starting transfers between devices, swapped(): lax.ppermute(second, 'dom', [(i, (i - 1 if i % 2 == 0 else i + 1) % count...  4.86 us
    pallas_call x1, Pallas kernels, body(): pl.pallas_call(functools.partial(neighbour_kernel, n_dom, n_slab, cap, (n...  3.89 us
  transfers between devices with their start and end apart: 6, of which 3 were waited for; matrix products, arithmetic and copies ran while one was open for 0% of the time, Pallas kernels for 14%

profile of v4, /device:TPU:0, one launch (start us, length us, event | category | flops | bytes accessed | tf_op | source)
XLA Modules:
  0.0 76.6 jit_solution(6425414126509295461)
XLA Ops:
  0.6 2.3 %send_states.1 = (f32[32,8,128]{2,1,0:T(8,128)}, bf16[1248,128]{1,0:T(8,128)(2,1)}) custom-call(f32[3,1024]{1,0:T(4,128)} %bitcast.3, s32[1,1024]{1,0:T(1,128)} %bitcast.4, s32[16,64]{1,0:T(8,128)} %pick_in.1, s32[4,384]{1,0:T(4,128)} %ghost_in.1, s32[4,16]{1,0:T(4,128)} %bitcast.5, bf16[10,128]{1,0:T(8,128)(2,1)} %embedding_in.1, ...), custom_call_target="tpu_custom_call" | custom-call | tf_op jit(solution)/shard_map/send_states/pallas_call | solution.py:134
  2.9 15.5 %all_to_all.5.recv_ref = f32[32,8,128]{2,1,0:T(8,128)S(1)} all-to-all(f32[32,8,128]{2,1,0:T(8,128)} %get-tuple-element.22), channel_id=1, replica_groups=mesh['dom'=16,'slab'=2] {'dom','slab'}, dimensions={0} | all-to-all | bytes 262144 | tf_op jit(solution)/shard_map/all_to_all | solution.py:681
  18.4 0.0 copy-start
  18.5 1.0 %copy-done = bf16[1248,128]{1,0:T(8,128)(2,1)S(1)} copy-done((bf16[1248,128]{1,0:T(8,128)(2,1)S(1)}, bf16[1248,128]{1,0:T(8,128)(2,1)}, u32[]{:S(2)}) %copy-start) | copy-done | bytes 319512
  19.4 15.9 %first_layer.1 = (s32[8,384]{1,0:T(8,128)S(1)}, f32[40,3,8,128]{3,2,1,0:T(8,128)S(1)}, f32[1024,8]{1,0:T(8,128)S(1)}, s32[8,128]{1,0:T(8,128)S(1)}, s32[8,384]{1...) custom-call(f32[32,8,128]{2,1,0:T(8,128)S(1)} %all_to_all.5.recv_ref, ...), custom_call_target="tpu_custom_call" | custom-call | tf_op jit(solution)/shard_map/first_layer/pallas_call | solution.py:683
  35.3 0.3 collective-permute-start.2
  35.6 0.3 collective-permute-start
  35.9 2.4 %collective-permute-start.1 = (bf16[384,128]{1,0:T(8,128)(2,1)S(1)}, bf16[384,128]{1,0:T(8,128)(2,1)S(1)}, u32[]{:S(2)}, u32[]{:S(2)}) collective-permute-start(bf16[384,128]{1,0:T(8,128)(2,1)S(1)} %get-tuple-element.31), channel_id=1, source_target_pairs={{0,30},{2,4},{4,2},{6,8},{8,6},{10,12},{12,10},{14,16},{16,14},{18... | collective-permute-start | bytes 294920 | tf_op jit(solution)/shard_map/ppermute | solution.py:657
  38.3 3.9 %neighbours.1 = (s32[2,328]{1,0:T(2,128)S(1)}, s32[2,328]{1,0:T(2,128)S(1)}, f32[65,3,8,128]{3,2,1,0:T(8,128)S(1)}, f32[5184,8]{1,0:T(8,128)S(1)}) custom-call(s32[8,384]{1,0:T(8,128)S(1)} %get-tuple-element.24.table_ref.numbers_ref, s32[8,128]{1,0:T(8,128)S(1)} %get-tuple-element.25.around_ref, f32[32,8,128]{2,1,0:T(8,128)S(1)} %all_to_all.5.recv_ref, ...), custom_call_target="tpu_custom_call" | custom-call | tf_op jit(solution)/shard_map/neighbours/pallas_call | solution.py:702
  42.2 0.0 collective-permute-done.rest_0_
  42.3 2.1 %collective-permute-done.1.rest_1_ = bf16[384,128]{1,0:T(8,128)(2,1)S(1)} collective-permute-done((bf16[384,128]{1,0:T(8,128)(2,1)S(1)}, bf16[384,128]{1,0:T(8,128)(2,1)S(1)}, u32[]{:S(2)}, u32[]{:S(2)}) %collective-permute-start.1) | collective-permute-done | bytes 98336 | tf_op jit(solution)/shard_map/ppermute | solution.py:657
  44.4 0.0 collective-permute-done.2.rest_2_
  44.4 13.7 %second_layer.1 = (bf16[1024,128]{1,0:T(8,128)(2,1)}, bf16[1024,128]{1,0:T(8,128)(2,1)S(1)}) custom-call(s32[8,384]{1,0:T(8,128)S(1)} %get-tuple-element.24.table_ref.numbers_ref, s32[2,328]{1,0:T(2,128)S(1)} %get-tuple-element.28.list_ref, f32[40,3,8,128]{3,2,1,0:T(8,128)S(1)} %get-tuple-element.26.pool_in.pool_ref, ...), custom_call_target="tpu_custom_call" | custom-call | tf_op jit(solution)/shard_map/second_layer/pallas_call | solution.py:716
  58.1 0.0 collective-permute-start.3
  58.1 2.4 %collective-permute-start.5 = (bf16[1024,128]{1,0:T(8,128)(2,1)S(1)}, bf16[1024,128]{1,0:T(8,128)(2,1)S(1)}, u32[]{:S(2)}, u32[]{:S(2)}) collective-permute-start(bf16[1024,128]{1,0:T(8,128)(2,1)S(1)} %get-tuple-element.39.g_ref), channel_id=1, source_target_pairs={{0,30},{2,4},{4,2},{6,8},{8,6},{10,12},{12,10},{14,16},{16,14},{18... | collective-permute-start | bytes 786440 | tf_op jit(solution)/shard_map/ppermute | solution.py:657
  60.5 0.0 collective-permute-start.4
  60.5 0.0 collective-permute-done.3.rest_0_
  60.5 6.5 %near_forces.1 = (f32[8,1024]{1,0:T(8,128)S(1)}, bf16[768,128]{1,0:T(8,128)(2,1)S(1)}) custom-call(s32[2,328]{1,0:T(2,128)S(1)} %get-tuple-element.28.list_ref, s32[8,384]{1,0:T(8,128)S(1)} %get-tuple-element.24.table_ref.numbers_ref, s32[8,384]{1,0:T(8,128)S(1)} %get-tuple-element.36.taken_ref, f32[65,3,8,128]{3,2,1,0:T(8,128)S(1)} %get-tuple-element.37.pool_ref, ...), custom_call_target="tpu_custom_call" | custom-call | flops 4000000000 | bytes 4000000 | tf_op jit(solution)/shard_map/near_forces/pallas_call | solution.py:736
  67.0 3.5 %collective-permute-done.5.second_ref = bf16[1024,128]{1,0:T(8,128)(2,1)S(1)} collective-permute-done((bf16[1024,128]{1,0:T(8,128)(2,1)S(1)}, bf16[1024,128]{1,0:T(8,128)(2,1)S(1)}, u32[]{:S(2)}, u32[]{:S(2)}) %collective-permute-start.5) | collective-permute-done | bytes 262176 | tf_op jit(solution)/shard_map/ppermute | solution.py:657
  70.5 1.2 %collective-permute-done.4.first_ref = bf16[1024,128]{1,0:T(8,128)(2,1)S(1)} collective-permute-done((bf16[1024,128]{1,0:T(8,128)(2,1)S(1)}, bf16[1024,128]{1,0:T(8,128)(2,1)S(1)}, u32[]{:S(2)}, u32[]{:S(2)}) %collective-permute-start.4) | collective-permute-done | bytes 262176 | tf_op jit(solution)/shard_map/ppermute | solution.py:658
  71.7 5.0 %far_forces.1 = f32[3,1024]{1,0:T(4,128)} custom-call(s32[2,328]{1,0:T(2,128)S(1)} %get-tuple-element.35.list_ref, s32[8,384]{1,0:T(8,128)S(1)} %get-tuple-element.24.table_ref.numbers_ref, s32[8,384]{1,0:T(8,128)S(1)} %get-tuple-element.36.taken_ref, f32[65,3,8,128]{3,2,1,0:T(8,128)S(1)} %get-tuple-element.37.pool_ref, ...), custom_call_target="tpu_custom_call" | custom-call | tf_op jit(solution)/shard_map/far_forces/pallas_call | solution.py:746
Async XLA Ops:
  18.4 1.0 %copy-start = (bf16[1248,128]{1,0:T(8,128)(2,1)S(1)}, bf16[1248,128]{1,0:T(8,128)(2,1)}, u32[]{:S(2)}) copy-start(bf16[1248,128]{1,0:T(8,128)(2,1)} %get-tuple-element.23.weights_ref) | copy-start | bytes 958468
  35.3 9.0 %collective-permute-start.2 = (bf16[768,128]{1,0:T(8,128)(2,1)S(1)}, bf16[768,128]{1,0:T(8,128)(2,1)S(1)}, u32[]{:S(2)}, u32[]{:S(2)}) collective-permute-start(bf16[768,128]{1,0:T(8,128)(2,1)S(1)} %get-tuple-element.32), channel_id=1, source_target_pairs={{0,1},{1,0},{2,3},{3,2},{4,5},{5,4},{6,7},{7,6},{8,9},{9,8},{10,11... | collective-permute-start | bytes 589832 | tf_op jit(solution)/shard_map/ppermute | solution.py:652
  35.6 6.6 %collective-permute-start = (bf16[384,128]{1,0:T(8,128)(2,1)S(1)}, bf16[384,128]{1,0:T(8,128)(2,1)S(1)}, u32[]{:S(2)}, u32[]{:S(2)}) collective-permute-start(bf16[384,128]{1,0:T(8,128)(2,1)S(1)} %get-tuple-element.30), channel_id=1, source_target_pairs={{0,2},{2,0},{4,6},{6,4},{8,10},{10,8},{12,14},{14,12},{16,18},{18,... | collective-permute-start | bytes 294920 | tf_op jit(solution)/shard_map/ppermute | solution.py:658
  35.9 8.4 %collective-permute-start.1 = (bf16[384,128]{1,0:T(8,128)(2,1)S(1)}, bf16[384,128]{1,0:T(8,128)(2,1)S(1)}, u32[]{:S(2)}, u32[]{:S(2)}) collective-permute-start(bf16[384,128]{1,0:T(8,128)(2,1)S(1)} %get-tuple-element.31), channel_id=1, source_target_pairs={{0,30},{2,4},{4,2},{6,8},{8,6},{10,12},{12,10},{14,16},{16,14},{18... | collective-permute-start | bytes 294920 | tf_op jit(solution)/shard_map/ppermute | solution.py:657
  58.1 2.5 %collective-permute-start.3 = (bf16[1024,128]{1,0:T(8,128)(2,1)S(1)}, bf16[1024,128]{1,0:T(8,128)(2,1)S(1)}, u32[]{:S(2)}, u32[]{:S(2)}) collective-permute-start(bf16[1024,128]{1,0:T(8,128)(2,1)S(1)} %get-tuple-element.39.g_ref), channel_id=1, source_target_pairs={{0,1},{1,0},{2,3},{3,2},{4,5},{5,4},{6,7},{7,6},{8,9},{9,8},{10,11... | collective-permute-start | bytes 786440 | tf_op jit(solution)/shard_map/ppermute | solution.py:652
  58.1 12.4 %collective-permute-start.5 = (bf16[1024,128]{1,0:T(8,128)(2,1)S(1)}, bf16[1024,128]{1,0:T(8,128)(2,1)S(1)}, u32[]{:S(2)}, u32[]{:S(2)}) collective-permute-start(bf16[1024,128]{1,0:T(8,128)(2,1)S(1)} %get-tuple-element.39.g_ref), channel_id=1, source_target_pairs={{0,30},{2,4},{4,2},{6,8},{8,6},{10,12},{12,10},{14,16},{16,14},{18... | collective-permute-start | bytes 786440 | tf_op jit(solution)/shard_map/ppermute | solution.py:657
  60.5 11.1 %collective-permute-start.4 = (bf16[1024,128]{1,0:T(8,128)(2,1)S(1)}, bf16[1024,128]{1,0:T(8,128)(2,1)S(1)}, u32[]{:S(2)}, u32[]{:S(2)}) collective-permute-start(bf16[1024,128]{1,0:T(8,128)(2,1)S(1)} %get-tuple-element.39.g_ref), channel_id=1, source_target_pairs={{0,2},{2,0},{4,6},{6,4},{8,10},{10,8},{12,14},{14,12},{16,18},{18,... | collective-permute-start | bytes 786440 | tf_op jit(solution)/shard_map/ppermute | solution.py:658

commit v5 on v4

--- a/solution.py
+++ b/solution.py
@@ -58,18 +58,8 @@
     for spot, (source, target) in enumerate(pairs):
         copies.append(pltpu.make_async_copy(source, target, sems.at[spot]))
         copies[-1].start()
-    for copy in copies:
+    for copy in copies[:5]:
         copy.wait()
-    beside = jnp.zeros((near_ref.shape[0], ghost_ref.shape[1] - near_ref.shape[1]), jnp.int32)
-    numbers = jnp.concatenate([ghost_ref[...], jnp.concatenate([near_ref[...], beside], axis=1)], axis=0)
-    parts = [part[:, m * LANES : (m + 1) * LANES] for part in (numbers >> 5, numbers & 31) for m in range(numbers.shape[1] // LANES)]
-    number_spot = force_spot + force_in.shape[0]
-    weights_ref[number_spot:, :] = jnp.concatenate(parts, axis=0).astype(F32).astype(BF16)
-    blank = jnp.zeros((16, embedding_ref.shape[1]), F32)
-    for level in range(radial_ref.shape[0]):
-        weights_ref[16 * level : 16 * level + 16, :] = jnp.concatenate([radial_ref[level].astype(F32), blank[radial_ref.shape[1] :]], axis=0).astype(BF16)
-    spot = 16 * radial_ref.shape[0]
-    weights_ref[spot : spot + 16, :] = jnp.concatenate([embedding_ref[...].astype(F32), blank[embedding_ref.shape[0] :]], axis=0).astype(BF16)
     rows = pos_ref.shape[1]
     cap = pick_ref.shape[1]
     blocks = rows // LANES
@@ -119,6 +109,18 @@
     for face, target in enumerate(targets):
         start = 0 if face == 3 else 4
         out_ref[target, start : start + 4, TILE:] = packs[face]
+    for copy in copies[5:]:
+        copy.wait()
+    beside = jnp.zeros((near_ref.shape[0], ghost_ref.shape[1] - near_ref.shape[1]), jnp.int32)
+    numbers = jnp.concatenate([ghost_ref[...], jnp.concatenate([near_ref[...], beside], axis=1)], axis=0)
+    parts = [part[:, m * LANES : (m + 1) * LANES] for part in (numbers >> 5, numbers & 31) for m in range(numbers.shape[1] // LANES)]
+    number_spot = force_spot + force_in.shape[0]
+    weights_ref[number_spot:, :] = jnp.concatenate(parts, axis=0).astype(F32).astype(BF16)
+    blank = jnp.zeros((16, embedding_ref.shape[1]), F32)
+    for level in range(radial_ref.shape[0]):
+        weights_ref[16 * level : 16 * level + 16, :] = jnp.concatenate([radial_ref[level].astype(F32), blank[radial_ref.shape[1] :]], axis=0).astype(BF16)
+    spot = 16 * radial_ref.shape[0]
+    weights_ref[spot : spot + 16, :] = jnp.concatenate([embedding_ref[...].astype(F32), blank[embedding_ref.shape[0] :]], axis=0).astype(BF16)
 
 
 def weight_spots(radial_shape, update_shape):
@@ -413,7 +415,7 @@
     atom_rows, ghost_rows = h_in_ref.shape[0], ghosts[0].shape[0]
     even = is_even().astype(jnp.int32)
     h_ref[0:atom_rows, :] = h_in_ref[...]
-    for block, ref in zip((even, 1 - even), ghosts):
+    for block, ref in zip((1 - even, even), ghosts):
         h_ref[pl.ds(pl.multiple_of(atom_rows + block * ghost_rows, LANES), ghost_rows), :] = ref[...]
     start = atom_rows + 2 * ghost_rows
     for ref in ghosts[2:]:
@@ -721,7 +723,7 @@
         scratch_shapes=scratch,
         compiler_params=params(),
         name="second_layer",
-    )(numbers, early, pool, column, hidden, *faces, kept)
+    )(numbers, early, pool, column, hidden, faces[1], faces[0], *faces[2:], kept)
 
     slabs = [passed_along(mine, "slab", 1)]
     if n_slab != 2:

time: 76.5 us -> 76 us (level); the launches traced: 76.6 us -> 75.1 us
  starting transfers between devices: 5.46 us -> 3.97 us
    ppermute x2, starting transfers between devices: 4.86 us -> 3.2 us  [swapped(): lax.ppermute(second, 'dom', [(i, (i - 1 if i % 2 == 0 else i + 1) % count...]
    ppermute x2, waiting for transfers between devices: 5.6 us -> 6.53 us  [swapped(): lax.ppermute(second, 'dom', [(i, (i - 1 if i % 2 == 0 else i + 1) % count...]
where the time goes in v5:
time: 76 us; the launch traced here: 75.1 us
  Pallas kernels  46.9 us (62%)
  blocking collectives  15.5 us (20%)
  waiting for transfers between devices  7 us (9%)
  starting transfers between devices  3.97 us (5%)
  local copies, waits for them, and re-layouts  0.97 us (1%)
    pallas_call x1, Pallas kernels, body(): pl.pallas_call(functools.partial(first_kernel, n_dom, n_slab, cap, n_out,...  15.9 us
    all_to_all x1, blocking collectives, body(): lax.all_to_all(sent, ('dom', 'slab'), split_axis=0, concat_axis=0, tiled=...  15.5 us
    pallas_call x1, Pallas kernels, body(): pl.pallas_call(functools.partial(second_kernel, n_out, spots[1], force_sp...  13.7 us
    pallas_call x1, Pallas kernels, body(): pl.pallas_call(functools.partial(near_forces_kernel, n_slab), out_shape=[...  6.88 us
    ppermute x2, waiting for transfers between devices, swapped(): lax.ppermute(second, 'dom', [(i, (i - 1 if i % 2 == 0 else i + 1) % count...  6.53 us
    pallas_call x1, Pallas kernels, body(): pl.pallas_call(far_forces_kernel, out_shape=jax.ShapeDtypeStruct((3, atom...  4.56 us
    pallas_call x1, Pallas kernels, body(): pl.pallas_call(functools.partial(neighbour_kernel, n_dom, n_slab, cap, (n...  3.89 us
    ppermute x2, starting transfers between devices, swapped(): lax.ppermute(second, 'dom', [(i, (i - 1 if i % 2 == 0 else i + 1) % count...  3.2 us
  transfers between devices with their start and end apart: 6, of which 3 were waited for; matrix products, arithmetic and copies ran while one was open for 0% of the time, Pallas kernels for 14%

profile of v5, /device:TPU:0, one launch (start us, length us, event | category | flops | bytes accessed | tf_op | source)
XLA Modules:
  0.0 75.1 jit_solution(11388149782823267681)
XLA Ops:
  0.6 2.0 %send_states.1 = (f32[32,8,128]{2,1,0:T(8,128)}, bf16[1248,128]{1,0:T(8,128)(2,1)}) custom-call(f32[3,1024]{1,0:T(4,128)} %bitcast.3, s32[1,1024]{1,0:T(1,128)} %bitcast.4, s32[16,64]{1,0:T(8,128)} %pick_in.1, s32[4,384]{1,0:T(4,128)} %ghost_in.1, s32[4,16]{1,0:T(4,128)} %bitcast.5, bf16[10,128]{1,0:T(8,128)(2,1)} %embedding_in.1, ...), custom_call_target="tpu_custom_call" | custom-call | tf_op jit(solution)/shard_map/send_states/pallas_call | solution.py:136
  2.6 15.5 %all_to_all.5.recv_ref = f32[32,8,128]{2,1,0:T(8,128)S(1)} all-to-all(f32[32,8,128]{2,1,0:T(8,128)} %get-tuple-element.22), channel_id=1, replica_groups=mesh['dom'=16,'slab'=2] {'dom','slab'}, dimensions={0} | all-to-all | bytes 262144 | tf_op jit(solution)/shard_map/all_to_all | solution.py:683
  18.2 0.0 copy-start
  18.2 1.0 %copy-done = bf16[1248,128]{1,0:T(8,128)(2,1)S(1)} copy-done((bf16[1248,128]{1,0:T(8,128)(2,1)S(1)}, bf16[1248,128]{1,0:T(8,128)(2,1)}, u32[]{:S(2)}) %copy-start) | copy-done | bytes 319512
  19.2 15.9 %first_layer.1 = (s32[8,384]{1,0:T(8,128)S(1)}, f32[40,3,8,128]{3,2,1,0:T(8,128)S(1)}, f32[1024,8]{1,0:T(8,128)S(1)}, s32[8,128]{1,0:T(8,128)S(1)}, s32[8,384]{1...) custom-call(f32[32,8,128]{2,1,0:T(8,128)S(1)} %all_to_all.5.recv_ref, ...), custom_call_target="tpu_custom_call" | custom-call | tf_op jit(solution)/shard_map/first_layer/pallas_call | solution.py:685
  35.1 0.3 collective-permute-start.2
  35.3 1.5 %collective-permute-start = (bf16[384,128]{1,0:T(8,128)(2,1)S(1)}, bf16[384,128]{1,0:T(8,128)(2,1)S(1)}, u32[]{:S(2)}, u32[]{:S(2)}) collective-permute-start(bf16[384,128]{1,0:T(8,128)(2,1)S(1)} %get-tuple-element.30), channel_id=1, source_target_pairs={{0,30},{2,4},{4,2},{6,8},{8,6},{10,12},{12,10},{14,16},{16,14},{18... | collective-permute-start | bytes 294920 | tf_op jit(solution)/shard_map/ppermute | solution.py:659
  36.8 0.5 collective-permute-start.1
  37.3 3.9 %neighbours.1 = (s32[2,328]{1,0:T(2,128)S(1)}, s32[2,328]{1,0:T(2,128)S(1)}, f32[65,3,8,128]{3,2,1,0:T(8,128)S(1)}, f32[5184,8]{1,0:T(8,128)S(1)}) custom-call(s32[8,384]{1,0:T(8,128)S(1)} %get-tuple-element.24.table_ref.numbers_ref, s32[8,128]{1,0:T(8,128)S(1)} %get-tuple-element.25.around_ref, f32[32,8,128]{2,1,0:T(8,128)S(1)} %all_to_all.5.recv_ref, ...), custom_call_target="tpu_custom_call" | custom-call | tf_op jit(solution)/shard_map/neighbours/pallas_call | solution.py:704
  41.2 2.7 %collective-permute-done.rest_0_ = bf16[384,128]{1,0:T(8,128)(2,1)S(1)} collective-permute-done((bf16[384,128]{1,0:T(8,128)(2,1)S(1)}, bf16[384,128]{1,0:T(8,128)(2,1)S(1)}, u32[]{:S(2)}, u32[]{:S(2)}) %collective-permute-start) | collective-permute-done | bytes 98336 | tf_op jit(solution)/shard_map/ppermute | solution.py:659
  43.9 0.0 collective-permute-done.1.rest_1_
  43.9 0.0 collective-permute-done.2.rest_2_
  44.0 13.7 %second_layer.1 = (bf16[1024,128]{1,0:T(8,128)(2,1)}, bf16[1024,128]{1,0:T(8,128)(2,1)S(1)}) custom-call(s32[8,384]{1,0:T(8,128)S(1)} %get-tuple-element.24.table_ref.numbers_ref, s32[2,328]{1,0:T(2,128)S(1)} %get-tuple-element.28.list_ref, f32[40,3,8,128]{3,2,1,0:T(8,128)S(1)} %get-tuple-element.26.pool_in.pool_ref, ...), custom_call_target="tpu_custom_call" | custom-call | tf_op jit(solution)/shard_map/second_layer/pallas_call | solution.py:718
  57.6 0.0 collective-permute-start.3
  57.7 1.7 %collective-permute-start.5 = (bf16[1024,128]{1,0:T(8,128)(2,1)S(1)}, bf16[1024,128]{1,0:T(8,128)(2,1)S(1)}, u32[]{:S(2)}, u32[]{:S(2)}) collective-permute-start(bf16[1024,128]{1,0:T(8,128)(2,1)S(1)} %get-tuple-element.39.g_ref), channel_id=1, source_target_pairs={{0,30},{2,4},{4,2},{6,8},{8,6},{10,12},{12,10},{14,16},{16,14},{18... | collective-permute-start | bytes 786440 | tf_op jit(solution)/shard_map/ppermute | solution.py:659
  59.4 0.0 collective-permute-start.4
  59.4 0.0 collective-permute-done.3.rest_0_
  59.4 6.9 %near_forces.1 = (f32[8,1024]{1,0:T(8,128)S(1)}, bf16[768,128]{1,0:T(8,128)(2,1)S(1)}) custom-call(s32[2,328]{1,0:T(2,128)S(1)} %get-tuple-element.28.list_ref, s32[8,384]{1,0:T(8,128)S(1)} %get-tuple-element.24.table_ref.numbers_ref, s32[8,384]{1,0:T(8,128)S(1)} %get-tuple-element.36.taken_ref, f32[65,3,8,128]{3,2,1,0:T(8,128)S(1)} %get-tuple-element.37.pool_ref, ...), custom_call_target="tpu_custom_call" | custom-call | flops 4000000000 | bytes 4000000 | tf_op jit(solution)/shard_map/near_forces/pallas_call | solution.py:738
  66.3 3.8 %collective-permute-done.5.second_ref = bf16[1024,128]{1,0:T(8,128)(2,1)S(1)} collective-permute-done((bf16[1024,128]{1,0:T(8,128)(2,1)S(1)}, bf16[1024,128]{1,0:T(8,128)(2,1)S(1)}, u32[]{:S(2)}, u32[]{:S(2)}) %collective-permute-start.5) | collective-permute-done | bytes 262176 | tf_op jit(solution)/shard_map/ppermute | solution.py:659
  70.1 0.5 collective-permute-done.4.first_ref
  70.5 4.6 %far_forces.1 = f32[3,1024]{1,0:T(4,128)} custom-call(s32[2,328]{1,0:T(2,128)S(1)} %get-tuple-element.35.list_ref, s32[8,384]{1,0:T(8,128)S(1)} %get-tuple-element.24.table_ref.numbers_ref, s32[8,384]{1,0:T(8,128)S(1)} %get-tuple-element.36.taken_ref, f32[65,3,8,128]{3,2,1,0:T(8,128)S(1)} %get-tuple-element.37.pool_ref, ...), custom_call_target="tpu_custom_call" | custom-call | tf_op jit(solution)/shard_map/far_forces/pallas_call | solution.py:748
Async XLA Ops:
  18.2 1.0 %copy-start = (bf16[1248,128]{1,0:T(8,128)(2,1)S(1)}, bf16[1248,128]{1,0:T(8,128)(2,1)}, u32[]{:S(2)}) copy-start(bf16[1248,128]{1,0:T(8,128)(2,1)} %get-tuple-element.23.weights_ref) | copy-start | bytes 958468
  35.1 8.9 %collective-permute-start.2 = (bf16[768,128]{1,0:T(8,128)(2,1)S(1)}, bf16[768,128]{1,0:T(8,128)(2,1)S(1)}, u32[]{:S(2)}, u32[]{:S(2)}) collective-permute-start(bf16[768,128]{1,0:T(8,128)(2,1)S(1)} %get-tuple-element.32), channel_id=1, source_target_pairs={{0,1},{1,0},{2,3},{3,2},{4,5},{5,4},{6,7},{7,6},{8,9},{9,8},{10,11... | collective-permute-start | bytes 589832 | tf_op jit(solution)/shard_map/ppermute | solution.py:654
  35.3 8.6 %collective-permute-start = (bf16[384,128]{1,0:T(8,128)(2,1)S(1)}, bf16[384,128]{1,0:T(8,128)(2,1)S(1)}, u32[]{:S(2)}, u32[]{:S(2)}) collective-permute-start(bf16[384,128]{1,0:T(8,128)(2,1)S(1)} %get-tuple-element.30), channel_id=1, source_target_pairs={{0,30},{2,4},{4,2},{6,8},{8,6},{10,12},{12,10},{14,16},{16,14},{18... | collective-permute-start | bytes 294920 | tf_op jit(solution)/shard_map/ppermute | solution.py:659
  36.8 7.2 %collective-permute-start.1 = (bf16[384,128]{1,0:T(8,128)(2,1)S(1)}, bf16[384,128]{1,0:T(8,128)(2,1)S(1)}, u32[]{:S(2)}, u32[]{:S(2)}) collective-permute-start(bf16[384,128]{1,0:T(8,128)(2,1)S(1)} %get-tuple-element.31), channel_id=1, source_target_pairs={{0,2},{2,0},{4,6},{6,4},{8,10},{10,8},{12,14},{14,12},{16,18},{18,... | collective-permute-start | bytes 294920 | tf_op jit(solution)/shard_map/ppermute | solution.py:660
  57.6 1.8 %collective-permute-start.3 = (bf16[1024,128]{1,0:T(8,128)(2,1)S(1)}, bf16[1024,128]{1,0:T(8,128)(2,1)S(1)}, u32[]{:S(2)}, u32[]{:S(2)}) collective-permute-start(bf16[1024,128]{1,0:T(8,128)(2,1)S(1)} %get-tuple-element.39.g_ref), channel_id=1, source_target_pairs={{0,1},{1,0},{2,3},{3,2},{4,5},{5,4},{6,7},{7,6},{8,9},{9,8},{10,11... | collective-permute-start | bytes 786440 | tf_op jit(solution)/shard_map/ppermute | solution.py:654
  57.7 12.4 %collective-permute-start.5 = (bf16[1024,128]{1,0:T(8,128)(2,1)S(1)}, bf16[1024,128]{1,0:T(8,128)(2,1)S(1)}, u32[]{:S(2)}, u32[]{:S(2)}) collective-permute-start(bf16[1024,128]{1,0:T(8,128)(2,1)S(1)} %get-tuple-element.39.g_ref), channel_id=1, source_target_pairs={{0,30},{2,4},{4,2},{6,8},{8,6},{10,12},{12,10},{14,16},{16,14},{18... | collective-permute-start | bytes 786440 | tf_op jit(solution)/shard_map/ppermute | solution.py:659
  59.4 11.1 %collective-permute-start.4 = (bf16[1024,128]{1,0:T(8,128)(2,1)S(1)}, bf16[1024,128]{1,0:T(8,128)(2,1)S(1)}, u32[]{:S(2)}, u32[]{:S(2)}) collective-permute-start(bf16[1024,128]{1,0:T(8,128)(2,1)S(1)} %get-tuple-element.39.g_ref), channel_id=1, source_target_pairs={{0,2},{2,0},{4,6},{6,4},{8,10},{10,8},{12,14},{14,12},{16,18},{18,... | collective-permute-start | bytes 786440 | tf_op jit(solution)/shard_map/ppermute | solution.py:660
